TPU v7x, 32 devices: a whole 2x2x4 slice. The times are simulated.
32 devices in a mesh: cont: 4 (over y, x), net: 8 (over z, core).
Axes of the slice: x: 2, y: 2, z: 4, core: 2. Of those that a mesh axis runs over, the one named last changes fastest.
Arguments:
- angles: float32 [256, 4096], P('cont', 'net'), may hold values from -6 to 6
- lam_from: float32 [256, 5120], P('cont', 'net'), may hold values from -4 to 4
- lam_to: float32 [256, 5120], P('cont', 'net'), may hold values from -4 to 4
- gen_dual: float32 [256, 4096], P('cont', 'net'), may hold values from -6 to 6
- base_prev: float32 [4096], P('net'), may hold values from 0 to 0.5
- outage: int32 [256, 5120], P('cont', 'net'), may hold values 0 or 1
- from_bus: int32 [5120], P('net'), may hold values from 0 to 511
- to_ref: int32 [5120], P('net'), may hold values from 0 to 639, as said below
- halo_rows: int32 [1024], P('net'), may hold values from 0 to 512, as said below
- stiffness: float32 [5120], P('net'), may hold values from 0.5 to 8
- bus_load: float32 [4096], P('net'), may hold values from -3 to 3
- gen_cost: float32 [4096], P('net'), may hold values from 0.25 to 4
- gen_limit: float32 [4096], P('net'), may hold values from 0.05 to 0.6
Outputs:
- angle_field: float32 [256, 4096], P('cont', 'net')
- generation: float32 [256, 4096], P('cont', 'net')
- base_setpoint: float32 [4096], P('net')
Inputs may be any that keep to these rules, and one draw needn't show every extreme that they name: `halo_rows`: in each partition's 128 entries the live rows come first and are distinct buses of that partition, the rest equal 512; the first partition has no live entry; some partition has all 128 entries live, the others at least half. `to_ref`: A value below 512 is a bus of the branch's own partition; 512 + s names live slot s of the next partition's list; branches of the last partition are all local.
All inputs are finite; a program needn't handle non-finite values. No bound on the sum of `outage` on one device may be relied on, other than what follows from the above.
Results may differ from a plain program's by a relative error of at most 0.0001.
Values sent between devices are 32-bit elements; how exact they have to be, the bound alone decides.
No kernel may reach another device: no remote copies, remote signals or barrier semaphores. Data moves between devices by JAX's collectives and lax.ppermute only.
A program may use at most 64 MiB of HBM per device.

v0:
```python
import jax
import jax.numpy as jnp
from jax import lax
from jax.sharding import PartitionSpec as P

ROUNDS = 4


penalty = 1.0
balance = 2.0


def from_behind(value, axis, by):
    peers = lax.axis_size(axis)
    pairs = [(i, i + by) for i in range(peers) if 0 <= i + by < peers]
    return lax.ppermute(value, axis, pairs)


def one_hot_rows(index, count):
    return (index[:, None] == jnp.arange(count, dtype=jnp.int32)[None, :]).astype(jnp.float32)


def lookup(values, table):
    return lax.dot_general(
        values,
        table,
        (((1,), (1,)), ((), ())),
        precision=lax.Precision.HIGHEST,
        preferred_element_type=jnp.float32,
    )


def spread(values, table):
    return jnp.dot(
        values, table, precision=lax.Precision.HIGHEST, preferred_element_type=jnp.float32
    )


def branch_step(theta_from, theta_to, lam_f, lam_t, copy_f, copy_t, weights, later):
    if later:
        lam_f = lam_f + penalty * (copy_f - theta_from)
        lam_t = lam_t + penalty * (copy_t - theta_to)
    target_from = theta_from - lam_f / penalty
    target_to = theta_to - lam_t / penalty
    angle_gap = penalty * (target_from - target_to) / (penalty + 2.0 * weights)
    centre = 0.5 * (target_from + target_to)
    copy_f = centre + 0.5 * angle_gap
    copy_t = centre - 0.5 * angle_gap
    return (lam_f, lam_t, copy_f, copy_t, weights * angle_gap)


def local(
    angles,
    lam_from,
    lam_to,
    gen_dual,
    base_prev,
    outage,
    from_bus,
    to_ref,
    halo_rows,
    stiffness,
    bus_load,
    gen_cost,
    gen_limit,
):
    local_count = angles.shape[1]
    cont_local = angles.shape[0]
    slot_count = halo_rows.shape[0]
    branch_count = from_bus.shape[0]
    contingencies = cont_local * lax.axis_size("cont")
    weighted = stiffness[None, :] * (1.0 - outage.astype(jnp.float32))
    extended = local_count + slot_count
    branch_table = jnp.concatenate(
        [one_hot_rows(from_bus, extended), one_hot_rows(to_ref, extended)], axis=0
    )
    count_ext = jnp.sum(branch_table, axis=0)
    own_table = one_hot_rows(halo_rows, local_count)
    theta = angles
    base_set = base_prev
    copy_from = jnp.zeros_like(lam_from)
    copy_to = jnp.zeros_like(lam_to)
    generation = jnp.zeros_like(gen_dual)
    for round_index in range(ROUNDS):
        picked = lookup(theta, own_table)
        theta_ext = jnp.concatenate([theta, from_behind(picked, "net", -1)], axis=1)
        ends = lookup(theta_ext, branch_table)
        theta_from = ends[:, :branch_count]
        theta_to = ends[:, branch_count:]
        lam_from, lam_to, copy_from, copy_to, branch_flow = branch_step(
            theta_from, theta_to, lam_from, lam_to, copy_from, copy_to, weighted, round_index > 0
        )
        copy_terms = jnp.concatenate(
            [copy_from + lam_from / penalty, copy_to + lam_to / penalty], axis=1
        )
        flow_terms = jnp.concatenate([branch_flow, -branch_flow], axis=1)
        sums_ext = spread(jnp.concatenate([copy_terms, flow_terms], axis=0), branch_table)
        copy_ext = sums_ext[:cont_local]
        flow_ext = sums_ext[cont_local:]
        copy_in, flow_in, count_in = from_behind(
            (copy_ext[:, local_count:], flow_ext[:, local_count:], count_ext[local_count:]),
            "net",
            1,
        )
        stacked = spread(jnp.concatenate([copy_in, flow_in, count_in[None, :]], axis=0), own_table)
        copy_back = stacked[:cont_local]
        flow_back = stacked[cont_local : 2 * cont_local]
        count_back = stacked[2 * cont_local]
        copy_sum = copy_ext[:, :local_count] + copy_back
        net_out = flow_ext[:, :local_count] + flow_back
        degree = count_ext[:local_count] + count_back
        theta = copy_sum / (degree + 1.0)[None, :]
        generation = (
            penalty * base_set[None, :] - gen_dual + balance * (bus_load[None, :] + net_out)
        ) / (gen_cost + penalty + balance)[None, :]
        gen_dual = gen_dual + penalty * (generation - base_set[None, :])
        partial_value = jnp.sum(generation + gen_dual / penalty, axis=0)
        total = lax.psum(partial_value, "cont")
        base_set = jnp.clip(total / contingencies, 0.0, gen_limit)
    return (theta, generation, base_set)


def solution(mesh):
    placed = (
        P("cont", "net"),
        P("cont", "net"),
        P("cont", "net"),
        P("cont", "net"),
        P("net"),
        P("cont", "net"),
        P("net"),
        P("net"),
        P("net"),
        P("net"),
        P("net"),
        P("net"),
        P("net"),
    )
    return jax.shard_map(
        local,
        mesh=mesh,
        in_specs=placed,
        out_specs=(P("cont", "net"), P("cont", "net"), P("net")),
        check_vma=False,
    )
```

profile of v0, /device:TPU:0, one launch (start us, length us, event | category | flops | bytes accessed | tf_op | source)
XLA Modules:
  0.0 120.1 jit_solution(16465933510774965927)
XLA Ops:
  1.8 2.4 %collective-permute-start.3 = (f32[128]{0:T(128)S(1)}, f32[128]{0:T(128)S(1)}, u32[]{:S(2)}, u32[]{:S(2)}) collective-permute-start(f32[128]{0:T(128)S(1)} %slice.149), channel_id=1, source_target_pairs={{0,1},{1,2},{2,3},{3,4},{4,5},{5,6},{6,7},{8,9},{9,10},{10,11},{11... | collective-permute-start | bytes 1544 | tf_op jit(solution)/shard_map/ppermute | solution.py:16
  5.4 1.4 %collective-permute-start = (f32[64,128]{1,0:T(8,128)S(1)}, f32[64,128]{1,0:T(8,128)S(1)}, u32[]{:S(2)}, u32[]{:S(2)}) collective-permute-start(f32[64,128]{1,0:T(8,128)S(1)} %convolution_bitcast_fusion), channel_id=1, source_target_pairs={{1,0},{2,1},{3,2},{4,3},{5,4},{6,5},{7,6},{9,8},{10,9},{11,10},{12... | collective-permute-start | bytes 98312 | tf_op jit(solution)/shard_map/ppermute | solution.py:16
  7.8 3.0 %collective-permute-done = f32[64,128]{1,0:T(8,128)S(1)} collective-permute-done((f32[64,128]{1,0:T(8,128)S(1)}, f32[64,128]{1,0:T(8,128)S(1)}, u32[]{:S(2)}, u32[]{:S(2)}) %collective-permute-start) | collective-permute-done | bytes 32800 | tf_op jit(solution)/shard_map/ppermute | solution.py:16
  10.8 3.3 %fusion.43 = f32[64,1280]{1,0:T(8,128)S(1)} fusion(f32[64,128]{1,0:T(8,128)S(1)} %collective-permute-done, f32[64,512]{1,0:T(8,128)S(1)} %copy-done.34, f32[640,640]{1,0:T(8,128)S(1)} %get-tuple-element.50, f32[640,640]{1,0:T(8,128)S(1)} %get-tuple-element.49), kind=kOutput, calls=%fused_computation.50 | convolution fusion | flops 630005760 | bytes 3768320 | tf_op jit(solution)/shard_map/dot_general | solution.py:24
  15.1 2.2 %fusion.2 = f32[128,640]{1,0:T(8,128)S(1)} fusion(f32[64,640]{1,0:T(8,128)S(1)} %get-tuple-element.27, f32[64,640]{1,0:T(8,128)S(1)} %get-tuple-element.28, f32[64,640]{1,0:T(8,128)S(1)} %get-tuple-element.46, f32[64,640]{1,0:T(8,128)S(1)} %get-tuple-element.25, f32[640,640]{1,0:T(8,128)S(1)} %get-tuple-element.50, f32[640,640]{1,0:T(8,128)S(1)} %get-tuple-element.49), kind=kOutput, calls=%fused_computation.6 | convolution fusion | flops 1259601920 | bytes 4259840 | tf_op jit(solution)/shard_map/dot_general | solution.py:34
  17.2 4.5 %collective-permute-start.1 = (f32[64,128]{1,0:T(8,128)S(1)}, f32[64,128]{1,0:T(8,128)S(1)}, u32[]{:S(2)}, u32[]{:S(2)}) collective-permute-start(f32[64,128]{1,0:T(8,128)S(1)} %get-tuple-element.41), channel_id=1, source_target_pairs={{0,1},{1,2},{2,3},{3,4},{4,5},{5,6},{6,7},{8,9},{9,10},{10,11},{11... | collective-permute-start | bytes 98312 | tf_op jit(solution)/shard_map/ppermute | solution.py:16
  21.8 1.9 %collective-permute-start.2 = (f32[64,128]{1,0:T(8,128)S(1)}, f32[64,128]{1,0:T(8,128)S(1)}, u32[]{:S(2)}, u32[]{:S(2)}) collective-permute-start(f32[64,128]{1,0:T(8,128)S(1)} %get-tuple-element.42), channel_id=1, source_target_pairs={{0,1},{1,2},{2,3},{3,4},{4,5},{5,6},{6,7},{8,9},{9,10},{10,11},{11... | collective-permute-start | bytes 98312 | tf_op jit(solution)/shard_map/ppermute | solution.py:16
  26.6 1.3 %collective-permute-start.4 = (f32[64,128]{1,0:T(8,128)S(1)}, f32[64,128]{1,0:T(8,128)S(1)}, u32[]{:S(2)}, u32[]{:S(2)}) collective-permute-start(f32[64,128]{1,0:T(8,128)S(1)} %fusion.41), channel_id=1, source_target_pairs={{1,0},{2,1},{3,2},{4,3},{5,4},{6,5},{7,6},{9,8},{10,9},{11,10},{12... | collective-permute-start | bytes 98312 | tf_op jit(solution)/shard_map/ppermute | solution.py:16
  27.9 9.9 %psum.28 = f32[512]{0:T(512)S(1)} all-reduce(f32[512]{0:T(512)S(1)} %get-tuple-element.33), channel_id=1, replica_groups=mesh['cont'=4,'net'=8] {'cont'}, use_global_device_ids=true, to_apply=%region_3.4 | all-reduce | flops 512 | bytes 4096 | tf_op jit(solution)/shard_map/psum | solution.py:118
  37.9 4.3 %fusion.47 = f32[64,1280]{1,0:T(8,128)S(1)} fusion(f32[64,128]{1,0:T(8,128)S(1)} %collective-permute-done.4, f32[64,512]{1,0:T(8,128)} %copy-done.32, f32[640,640]{1,0:T(8,128)S(1)} %get-tuple-element.50, f32[640,640]{1,0:T(8,128)S(1)} %get-tuple-element.49), kind=kOutput, calls=%fused_computation.54 | convolution fusion | flops 630005760 | bytes 3768320 | tf_op jit(solution)/shard_map/dot_general | solution.py:24
  43.2 2.1 %fusion.10 = f32[128,640]{1,0:T(8,128)S(1)} fusion(f32[64,640]{1,0:T(8,128)S(1)} %get-tuple-element.23, f32[64,640]{1,0:T(8,128)S(1)} %get-tuple-element.24, f32[64,640]{1,0:T(8,128)S(1)} %get-tuple-element.45, f32[64,640]{1,0:T(8,128)S(1)} %get-tuple-element.19, f32[640,640]{1,0:T(8,128)S(1)} %get-tuple-element.50, f32[640,640]{1,0:T(8,128)S(1)} %get-tuple-element.49), kind=kOutput, calls=%fused_computation.14 | convolution fusion | flops 1259601920 | bytes 4259840 | tf_op jit(solution)/shard_map/dot_general | solution.py:34
  45.3 2.3 %collective-permute-start.5 = (f32[64,128]{1,0:T(8,128)S(1)}, f32[64,128]{1,0:T(8,128)S(1)}, u32[]{:S(2)}, u32[]{:S(2)}) collective-permute-start(f32[64,128]{1,0:T(8,128)S(1)} %get-tuple-element.39), channel_id=1, source_target_pairs={{0,1},{1,2},{2,3},{3,4},{4,5},{5,6},{6,7},{8,9},{9,10},{10,11},{11... | collective-permute-start | bytes 98312 | tf_op jit(solution)/shard_map/ppermute | solution.py:16
  47.7 6.4 %collective-permute-start.6 = (f32[64,128]{1,0:T(8,128)S(1)}, f32[64,128]{1,0:T(8,128)S(1)}, u32[]{:S(2)}, u32[]{:S(2)}) collective-permute-start(f32[64,128]{1,0:T(8,128)S(1)} %get-tuple-element.40), channel_id=1, source_target_pairs={{0,1},{1,2},{2,3},{3,4},{4,5},{5,6},{6,7},{8,9},{9,10},{10,11},{11... | collective-permute-start | bytes 98312 | tf_op jit(solution)/shard_map/ppermute | solution.py:16
  55.2 1.7 %add_reduce_fusion.2 = (f32[512]{0:T(512)S(1)}, f32[64,512]{1,0:T(8,128)}, f32[64,512]{1,0:T(8,128)S(1)}) fusion(f32[512]{0:T(512)S(1)} %broadcast_add_fusion, f32[129,512]{1,0:T(8,128)S(1)} %fusion.40, f32[128,640]{1,0:T(8,128)S(1)} %fusion.10, f32[512]{0:T(512)S(1)} %copy-done.38, f32[64,512]{1,0:T(8,128)S(1)} %copy-done.36, f32[512]{0:T(512)S(1)} %copy-done.41, ...), kind=kLoop, calls=%fused_computation.131 | loop fusion | flops 654848 | bytes 1191936 | tf_op jit(solution)/shard_map/reduce_sum | solution.py:117
  59.2 8.0 %psum.29 = f32[512]{0:T(512)S(1)} all-reduce(f32[512]{0:T(512)S(1)} %get-tuple-element.5), channel_id=1, replica_groups=mesh['cont'=4,'net'=8] {'cont'}, use_global_device_ids=true, to_apply=%region_5.6 | all-reduce | flops 512 | bytes 4096 | tf_op jit(solution)/shard_map/psum | solution.py:118
  67.2 4.3 %fusion.51 = f32[64,1280]{1,0:T(8,128)S(1)} fusion(f32[64,128]{1,0:T(8,128)S(1)} %collective-permute-done.7, f32[64,512]{1,0:T(8,128)} %copy-done.31, f32[640,640]{1,0:T(8,128)S(1)} %get-tuple-element.50, f32[640,640]{1,0:T(8,128)S(1)} %get-tuple-element.49), kind=kOutput, calls=%fused_computation.58 | convolution fusion | flops 630005760 | bytes 3768320 | tf_op jit(solution)/shard_map/dot_general | solution.py:24
  72.5 2.2 %fusion.18 = f32[128,640]{1,0:T(8,128)S(1)} fusion(f32[64,640]{1,0:T(8,128)S(1)} %get-tuple-element.17, f32[64,640]{1,0:T(8,128)S(1)} %get-tuple-element.18, f32[64,640]{1,0:T(8,128)S(1)} %get-tuple-element.44, f32[64,640]{1,0:T(8,128)S(1)} %get-tuple-element.13, f32[640,640]{1,0:T(8,128)S(1)} %get-tuple-element.50, f32[640,640]{1,0:T(8,128)S(1)} %get-tuple-element.49), kind=kOutput, calls=%fused_computation.22 | convolution fusion | flops 1259601920 | bytes 4259840 | tf_op jit(solution)/shard_map/dot_general | solution.py:34
  76.0 5.6 %collective-permute-start.9 = (f32[64,128]{1,0:T(8,128)S(1)}, f32[64,128]{1,0:T(8,128)S(1)}, u32[]{:S(2)}, u32[]{:S(2)}) collective-permute-start(f32[64,128]{1,0:T(8,128)S(1)} %get-tuple-element.38), channel_id=1, source_target_pairs={{0,1},{1,2},{2,3},{3,4},{4,5},{5,6},{6,7},{8,9},{9,10},{10,11},{11... | collective-permute-start | bytes 98312 | tf_op jit(solution)/shard_map/ppermute | solution.py:16
  85.8 9.0 %psum.30 = f32[512]{0:T(512)S(1)} all-reduce(f32[512]{0:T(512)S(1)} %get-tuple-element.30), channel_id=1, replica_groups=mesh['cont'=4,'net'=8] {'cont'}, use_global_device_ids=true, to_apply=%region_7.8 | all-reduce | flops 512 | bytes 4096 | tf_op jit(solution)/shard_map/psum | solution.py:118
  94.9 4.3 %fusion.55 = f32[64,1280]{1,0:T(8,128)S(1)} fusion(f32[64,128]{1,0:T(8,128)S(1)} %collective-permute-done.10, f32[64,512]{1,0:T(8,128)} %copy-done.33, f32[640,640]{1,0:T(8,128)S(1)} %get-tuple-element.50, f32[640,640]{1,0:T(8,128)S(1)} %get-tuple-element.49), kind=kOutput, calls=%fused_computation.62 | convolution fusion | flops 630005760 | bytes 3768320 | tf_op jit(solution)/shard_map/dot_general | solution.py:24
  99.4 2.2 %fusion.26 = f32[128,640]{1,0:T(8,128)S(1)} fusion(f32[64,640]{1,0:T(8,128)S(1)} %get-tuple-element.11, f32[64,640]{1,0:T(8,128)S(1)} %get-tuple-element.12, f32[64,640]{1,0:T(8,128)S(1)} %get-tuple-element.43, f32[64,640]{1,0:T(8,128)S(1)} %get-tuple-element.7, f32[640,640]{1,0:T(8,128)S(1)} %get-tuple-element.50, f32[640,640]{1,0:T(8,128)S(1)} %get-tuple-element.49), kind=kOutput, calls=%fused_computation.30 | convolution fusion | flops 1259601920 | bytes 4259840 | tf_op jit(solution)/shard_map/dot_general | solution.py:34
  102.9 5.6 %collective-permute-start.12 = (f32[64,128]{1,0:T(8,128)S(1)}, f32[64,128]{1,0:T(8,128)S(1)}, u32[]{:S(2)}, u32[]{:S(2)}) collective-permute-start(f32[64,128]{1,0:T(8,128)S(1)} %get-tuple-element.36), channel_id=1, source_target_pairs={{0,1},{1,2},{2,3},{3,4},{4,5},{5,6},{6,7},{8,9},{9,10},{10,11},{11... | collective-permute-start | bytes 98312 | tf_op jit(solution)/shard_map/ppermute | solution.py:16
  109.8 1.8 %add_reduce_fusion = (f32[512]{0:T(512)S(1)}, f32[64,512]{1,0:T(8,128)}, f32[64,512]{1,0:T(8,128)}) fusion(f32[512]{0:T(512)S(1)} %maximum_minimum_fusion.1, f32[64,512]{1,0:T(8,128)S(1)} %copy-done.30, f32[512]{0:T(512)S(1)} %maximum_minimum_fusion.2, f32[512]{0:T(512)S(1)} %broadcast_add_fusion, f32[129,512]{1,0:T(8,128)} %copy-done.9, ...), kind=kLoop, calls=%fused_computation.128 | loop fusion | flops 654848 | bytes 1191936 | tf_op jit(solution)/shard_map/reduce_sum | solution.py:117
  111.6 7.9 %psum.31 = f32[512]{0:T(512)S(1)} all-reduce(f32[512]{0:T(512)S(1)} %get-tuple-element.3), channel_id=1, replica_groups=mesh['cont'=4,'net'=8] {'cont'}, use_global_device_ids=true, to_apply=%region_9.10 | all-reduce | flops 512 | bytes 4096 | tf_op jit(solution)/shard_map/psum | solution.py:118
  (141 shorter events, 20.9 us)
Async XLA Ops:
  1.8 22.0 %collective-permute-start.3 = (f32[128]{0:T(128)S(1)}, f32[128]{0:T(128)S(1)}, u32[]{:S(2)}, u32[]{:S(2)}) collective-permute-start(f32[128]{0:T(128)S(1)} %slice.149), channel_id=1, source_target_pairs={{0,1},{1,2},{2,3},{3,4},{4,5},{5,6},{6,7},{8,9},{9,10},{10,11},{11... | collective-permute-start | bytes 1544 | tf_op jit(solution)/shard_map/ppermute | solution.py:16
  5.4 5.4 %collective-permute-start = (f32[64,128]{1,0:T(8,128)S(1)}, f32[64,128]{1,0:T(8,128)S(1)}, u32[]{:S(2)}, u32[]{:S(2)}) collective-permute-start(f32[64,128]{1,0:T(8,128)S(1)} %convolution_bitcast_fusion), channel_id=1, source_target_pairs={{1,0},{2,1},{3,2},{4,3},{5,4},{6,5},{7,6},{9,8},{10,9},{11,10},{12... | collective-permute-start | bytes 98312 | tf_op jit(solution)/shard_map/ppermute | solution.py:16
  15.0 8.7 %copy-start.42 = (f32[512]{0:T(512)S(1)}, f32[512]{0:T(512)}, u32[]{:S(2)}) copy-start(f32[512]{0:T(512)} %param.24) | copy-start | bytes 6148
  15.0 9.5 %copy-start.39 = (s32[128]{0:T(128)S(1)}, s32[128]{0:T(128)}, u32[]{:S(2)}) copy-start(s32[128]{0:T(128)} %param.21) | copy-start | bytes 1540
  15.0 9.9 %copy-start.35 = (f32[64,512]{1,0:T(8,128)S(1)}, f32[64,512]{1,0:T(8,128)}, u32[]{:S(2)}) copy-start(f32[64,512]{1,0:T(8,128)} %param.16) | copy-start | bytes 393220
  15.0 9.9 %copy-start.38 = (f32[512]{0:T(512)S(1)}, f32[512]{0:T(512)}, u32[]{:S(2)}) copy-start(f32[512]{0:T(512)} %param.23) | copy-start | bytes 6148
  15.0 9.9 %copy-start.41 = (f32[512]{0:T(512)S(1)}, f32[512]{0:T(512)}, u32[]{:S(2)}) copy-start(f32[512]{0:T(512)} %param.17) | copy-start | bytes 6148
  17.2 7.7 %copy-start.8 = (f32[128,640]{1,0:T(8,128)}, f32[128,640]{1,0:T(8,128)S(1)}, u32[]{:S(2)}) copy-start(f32[128,640]{1,0:T(8,128)S(1)} %fusion.2) | copy-start | bytes 983044
  17.2 6.5 %collective-permute-start.1 = (f32[64,128]{1,0:T(8,128)S(1)}, f32[64,128]{1,0:T(8,128)S(1)}, u32[]{:S(2)}, u32[]{:S(2)}) collective-permute-start(f32[64,128]{1,0:T(8,128)S(1)} %get-tuple-element.41), channel_id=1, source_target_pairs={{0,1},{1,2},{2,3},{3,4},{4,5},{5,6},{6,7},{8,9},{9,10},{10,11},{11... | collective-permute-start | bytes 98312 | tf_op jit(solution)/shard_map/ppermute | solution.py:16
  21.8 2.8 %collective-permute-start.2 = (f32[64,128]{1,0:T(8,128)S(1)}, f32[64,128]{1,0:T(8,128)S(1)}, u32[]{:S(2)}, u32[]{:S(2)}) collective-permute-start(f32[64,128]{1,0:T(8,128)S(1)} %get-tuple-element.42), channel_id=1, source_target_pairs={{0,1},{1,2},{2,3},{3,4},{4,5},{5,6},{6,7},{8,9},{9,10},{10,11},{11... | collective-permute-start | bytes 98312 | tf_op jit(solution)/shard_map/ppermute | solution.py:16
  26.6 11.2 %collective-permute-start.4 = (f32[64,128]{1,0:T(8,128)S(1)}, f32[64,128]{1,0:T(8,128)S(1)}, u32[]{:S(2)}, u32[]{:S(2)}) collective-permute-start(f32[64,128]{1,0:T(8,128)S(1)} %fusion.41), channel_id=1, source_target_pairs={{1,0},{2,1},{3,2},{4,3},{5,4},{6,5},{7,6},{9,8},{10,9},{11,10},{12... | collective-permute-start | bytes 98312 | tf_op jit(solution)/shard_map/ppermute | solution.py:16
  43.2 11.0 %copy-start.40 = (f32[512]{0:T(512)S(1)}, f32[512]{0:T(512)}, u32[]{:S(2)}) copy-start(f32[512]{0:T(512)} %param.25) | copy-start | bytes 6148
  43.2 12.0 %copy-start.36 = (f32[64,512]{1,0:T(8,128)S(1)}, f32[64,512]{1,0:T(8,128)}, u32[]{:S(2)}) copy-start(f32[64,512]{1,0:T(8,128)} %param.16) | copy-start | bytes 393220
  45.3 8.8 %collective-permute-start.5 = (f32[64,128]{1,0:T(8,128)S(1)}, f32[64,128]{1,0:T(8,128)S(1)}, u32[]{:S(2)}, u32[]{:S(2)}) collective-permute-start(f32[64,128]{1,0:T(8,128)S(1)} %get-tuple-element.39), channel_id=1, source_target_pairs={{0,1},{1,2},{2,3},{3,4},{4,5},{5,6},{6,7},{8,9},{9,10},{10,11},{11... | collective-permute-start | bytes 98312 | tf_op jit(solution)/shard_map/ppermute | solution.py:16
  47.7 7.1 %collective-permute-start.6 = (f32[64,128]{1,0:T(8,128)S(1)}, f32[64,128]{1,0:T(8,128)S(1)}, u32[]{:S(2)}, u32[]{:S(2)}) collective-permute-start(f32[64,128]{1,0:T(8,128)S(1)} %get-tuple-element.40), channel_id=1, source_target_pairs={{0,1},{1,2},{2,3},{3,4},{4,5},{5,6},{6,7},{8,9},{9,10},{10,11},{11... | collective-permute-start | bytes 98312 | tf_op jit(solution)/shard_map/ppermute | solution.py:16
  57.9 9.3 %collective-permute-start.7 = (f32[64,128]{1,0:T(8,128)S(1)}, f32[64,128]{1,0:T(8,128)S(1)}, u32[]{:S(2)}, u32[]{:S(2)}) collective-permute-start(f32[64,128]{1,0:T(8,128)S(1)} %fusion.39), channel_id=1, source_target_pairs={{1,0},{2,1},{3,2},{4,3},{5,4},{6,5},{7,6},{9,8},{10,9},{11,10},{12... | collective-permute-start | bytes 98312 | tf_op jit(solution)/shard_map/ppermute | solution.py:16
  72.5 10.4 %copy-start.29 = (f32[64,512]{1,0:T(8,128)S(1)}, f32[64,512]{1,0:T(8,128)}, u32[]{:S(2)}) copy-start(f32[64,512]{1,0:T(8,128)} %get-tuple-element.6) | copy-start | bytes 393220
  74.6 8.2 %copy-start.7 = (f32[128,640]{1,0:T(8,128)}, f32[128,640]{1,0:T(8,128)S(1)}, u32[]{:S(2)}) copy-start(f32[128,640]{1,0:T(8,128)S(1)} %fusion.18) | copy-start | bytes 983044
  74.7 7.0 %collective-permute-start.8 = (f32[64,128]{1,0:T(8,128)S(1)}, f32[64,128]{1,0:T(8,128)S(1)}, u32[]{:S(2)}, u32[]{:S(2)}) collective-permute-start(f32[64,128]{1,0:T(8,128)S(1)} %get-tuple-element.37), channel_id=1, source_target_pairs={{0,1},{1,2},{2,3},{3,4},{4,5},{5,6},{6,7},{8,9},{9,10},{10,11},{11... | collective-permute-start | bytes 98312 | tf_op jit(solution)/shard_map/ppermute | solution.py:16
  76.0 6.5 %collective-permute-start.9 = (f32[64,128]{1,0:T(8,128)S(1)}, f32[64,128]{1,0:T(8,128)S(1)}, u32[]{:S(2)}, u32[]{:S(2)}) collective-permute-start(f32[64,128]{1,0:T(8,128)S(1)} %get-tuple-element.38), channel_id=1, source_target_pairs={{0,1},{1,2},{2,3},{3,4},{4,5},{5,6},{6,7},{8,9},{9,10},{10,11},{11... | collective-permute-start | bytes 98312 | tf_op jit(solution)/shard_map/ppermute | solution.py:16
  84.5 10.3 %collective-permute-start.10 = (f32[64,128]{1,0:T(8,128)S(1)}, f32[64,128]{1,0:T(8,128)S(1)}, u32[]{:S(2)}, u32[]{:S(2)}) collective-permute-start(f32[64,128]{1,0:T(8,128)S(1)} %fusion.37), channel_id=1, source_target_pairs={{1,0},{2,1},{3,2},{4,3},{5,4},{6,5},{7,6},{9,8},{10,9},{11,10},{12... | collective-permute-start | bytes 98312 | tf_op jit(solution)/shard_map/ppermute | solution.py:16
  99.4 10.4 %copy-start.30 = (f32[64,512]{1,0:T(8,128)S(1)}, f32[64,512]{1,0:T(8,128)}, u32[]{:S(2)}) copy-start(f32[64,512]{1,0:T(8,128)} %get-tuple-element.6) | copy-start | bytes 393220
  101.6 7.0 %collective-permute-start.11 = (f32[64,128]{1,0:T(8,128)S(1)}, f32[64,128]{1,0:T(8,128)S(1)}, u32[]{:S(2)}, u32[]{:S(2)}) collective-permute-start(f32[64,128]{1,0:T(8,128)S(1)} %get-tuple-element.35), channel_id=1, source_target_pairs={{0,1},{1,2},{2,3},{3,4},{4,5},{5,6},{6,7},{8,9},{9,10},{10,11},{11... | collective-permute-start | bytes 98312 | tf_op jit(solution)/shard_map/ppermute | solution.py:16
  102.9 6.5 %collective-permute-start.12 = (f32[64,128]{1,0:T(8,128)S(1)}, f32[64,128]{1,0:T(8,128)S(1)}, u32[]{:S(2)}, u32[]{:S(2)}) collective-permute-start(f32[64,128]{1,0:T(8,128)S(1)} %get-tuple-element.36), channel_id=1, source_target_pairs={{0,1},{1,2},{2,3},{3,4},{4,5},{5,6},{6,7},{8,9},{9,10},{10,11},{11... | collective-permute-start | bytes 98312 | tf_op jit(solution)/shard_map/ppermute | solution.py:16
  (32 other events, 81.1 us)
where the time goes:
time: 121 us; the launch traced here: 120 us
  starting transfers between devices  36.8 us (30%)
  blocking collectives  34.8 us (29%)
  matrix products  28.4 us (23%)
  other arithmetic  7.32 us (6%)
  waiting for transfers between devices  6.08 us (5%)
  local copies, waits for them, and re-layouts  5.23 us (4%)
  between operations  1.52 us (1%)
    ppermute x13, starting transfers between devices, from_behind(): return lax.ppermute(value, axis, pairs)  36.8 us
    psum x4, blocking collectives, local(): total = lax.psum(partial_value, 'cont')  34.8 us
    dot_general x8, matrix products, lookup(): lax.dot_general(values, table, (((1,), (1,)), ((), ())), precision=lax.Pr...  18.3 us
    dot_general x8, matrix products, spread(): jnp.dot(values, table, precision=lax.Precision.HIGHEST, preferred_element...  10 us
    ppermute x13, waiting for transfers between devices, from_behind(): return lax.ppermute(value, axis, pairs)  6.08 us
    unnamed x86, local copies, waits for them, and re-layouts  5.18 us
    reduce_sum x4, other arithmetic, local(): partial_value = jnp.sum(generation + gen_dual / penalty, axis=0)  3.7 us
  transfers between devices with their start and end apart: 13, of which 5 were waited for; matrix products, arithmetic and copies ran while one was open for 7% of the time, Pallas kernels for 0%

commit v1 on v0

v1 whole, which is shorter than its diff:
```python
import jax
import jax.numpy as jnp
from jax import lax
from jax.experimental import pallas as pl
from jax.experimental.pallas import tpu as pltpu
from jax.sharding import PartitionSpec as P

ROUNDS = 4
PENALTY = 1.0
BALANCE = 2.0
F32 = jnp.float32
BF16 = jnp.bfloat16


def halves(value):
    high = value.astype(BF16)
    low = (value - high.astype(F32)).astype(BF16)
    return jnp.concatenate([high, low], axis=0)


def times(value, table):
    rows = value.shape[0]
    both = jnp.dot(halves(value), table, preferred_element_type=F32)
    return both[:rows] + both[rows:]


def times_t(value, table):
    rows = value.shape[0]
    both = lax.dot_general(
        halves(value), table, (((1,), (1,)), ((), ())), preferred_element_type=F32
    )
    return both[:rows] + both[rows:]


def column_ids(halo_row, buses):
    slots = halo_row.shape[1]
    own = jnp.where(halo_row < buses, halo_row, -1)
    away = buses + lax.broadcasted_iota(jnp.int32, (1, slots), 1)
    even = lax.axis_index("net") % 2 == 0
    first = jnp.where(even, away, own)
    second = jnp.where(even, own, away)
    return jnp.concatenate([first, second], axis=1)


def pick_kernel(theta_ref, halo_ref, pick1_ref, pick2_ref, own_ref):
    buses = theta_ref.shape[1]
    ids = column_ids(halo_ref[...], buses)
    rows = lax.broadcasted_iota(jnp.int32, (buses, ids.shape[1]), 0)
    table = jnp.where(rows == ids, 1.0, 0.0).astype(BF16)
    own_ref[...] = table
    pick = times(theta_ref[...], table)
    slots = halo_ref.shape[1]
    pick1_ref[...] = pick[:, :slots]
    pick2_ref[...] = pick[:, slots:]


def prep_kernel(
    theta_ref,
    lam_f_ref,
    lam_t_ref,
    outage_ref,
    from_ref,
    to_ref,
    halo_ref,
    stiff_ref,
    dual_ref,
    edge_ref,
    inner_ref,
    gain_ref,
    x_ref,
    p_ref,
    c_ref,
    count_edge_ref,
    count_inner_ref,
    sum_ref,
):
    buses = theta_ref.shape[1]
    branches = from_ref.shape[1]
    ids = column_ids(halo_ref[...], buses)
    edges = ids.shape[1]
    lanes = lax.broadcasted_iota(jnp.int32, (edges, buses), 1)
    ids_col = jnp.broadcast_to(ids, (edges, edges)).T[:, :1]
    inner = 1.0 - jnp.max(jnp.where(lanes == ids_col, 1.0, 0.0), axis=0, keepdims=True)
    bus_ids = lax.broadcasted_iota(jnp.int32, (1, buses), 1)
    inner_ids = jnp.where(inner > 0.0, bus_ids, -1)
    all_ids = jnp.concatenate([ids, inner_ids], axis=1)
    counts = jnp.zeros((8, all_ids.shape[1]), F32)
    step = 128
    for start in range(0, branches, step):
        part = slice(start, start + step)
        f_col = jnp.broadcast_to(from_ref[:, part], (step, step)).T[:, :1]
        t_col = jnp.broadcast_to(to_ref[:, part], (step, step)).T[:, :1]
        is_f = jnp.where(f_col == all_ids, 1.0, 0.0)
        is_t = jnp.where(t_col == all_ids, 1.0, 0.0)
        signed = (is_f - is_t).astype(BF16)
        edge_ref[part, :] = signed[:, :edges]
        inner_ref[part, :] = signed[:, edges:]
        ends = (is_f + is_t).reshape(step // 8, 8, all_ids.shape[1])
        counts = counts + jnp.sum(ends, axis=0)
    count = jnp.broadcast_to(jnp.sum(counts, axis=0, keepdims=True), counts.shape)
    count_edge_ref[...] = count[:, :edges]
    count_inner_ref[...] = count[:, edges:]
    weight = stiff_ref[...] * (1.0 - outage_ref[...].astype(F32))
    gain_ref[...] = PENALTY * weight / (PENALTY + 2.0 * weight)
    x = theta_ref[...] * inner
    x_ref[...] = x
    p = times_t(x, inner_ref[...])
    p_ref[...] = p
    c_ref[...] = p - (lam_f_ref[...] - lam_t_ref[...]) / PENALTY
    sum_ref[...] = jnp.broadcast_to(jnp.sum(dual_ref[...], axis=0, keepdims=True), sum_ref.shape)


def first_kernel(
    pick1_ref,
    pick2_ref,
    got1_ref,
    got2_ref,
    halo_ref,
    edge_ref,
    p_ref,
    c_ref,
    gain_ref,
    count_ref,
    send1_ref,
    send2_ref,
    z_ref,
    delta_ref,
    flow_ref,
):
    slots = halo_ref.shape[1]
    conts = p_ref.shape[0]
    even = lax.axis_index("net") % 2 == 0
    z1 = jnp.where(even, got1_ref[...], pick1_ref[...])
    z2 = jnp.where(even, pick2_ref[...], got2_ref[...])
    z = jnp.concatenate([z1, z2], axis=1)
    z_ref[...] = z
    moved = times_t(z, edge_ref[...])
    delta_ref[...] = p_ref[...] + moved
    flow = gain_ref[...] * (c_ref[...] + moved)
    flow_ref[...] = flow
    sums = times(flow, edge_ref[...])
    send1_ref[:conts, :] = sums[:, :slots]
    send2_ref[:conts, :] = sums[:, slots:]
    send1_ref[conts:, :] = count_ref[:, :slots]
    send2_ref[conts:, :] = count_ref[:, slots:]


def next_kernel(
    send1_ref,
    send2_ref,
    got1_ref,
    got2_ref,
    z_ref,
    degree_ref,
    edge_ref,
    p_ref,
    c_ref,
    gain_ref,
    out1_ref,
    out2_ref,
    z_out_ref,
    delta_ref,
    flow_ref,
    both_ref,
):
    conts = p_ref.shape[0]
    slots = out1_ref.shape[1]
    both = jnp.concatenate(
        [
            send1_ref[:conts, :] + got1_ref[:conts, :],
            send2_ref[:conts, :] + got2_ref[:conts, :],
        ],
        axis=1,
    )
    both_ref[...] = both
    degree = degree_ref[:1, :]
    z = (degree * z_ref[...] - both) / (degree + 1.0)
    z_out_ref[...] = z
    moved = times_t(z, edge_ref[...])
    delta_ref[...] = p_ref[...] + moved
    flow = gain_ref[...] * (c_ref[...] + 2.0 * moved)
    flow_ref[...] = flow
    sums = times(flow, edge_ref[...])
    out1_ref[...] = sums[:, :slots]
    out2_ref[...] = sums[:, slots:]


def second_kernel(
    send1_ref,
    send2_ref,
    got1_ref,
    got2_ref,
    z_ref,
    edge_ref,
    p_ref,
    c_ref,
    gain_ref,
    out1_ref,
    out2_ref,
    z_out_ref,
    delta_ref,
    flow_ref,
    both_ref,
    degree_ref,
):
    conts = p_ref.shape[0]
    degree_ref[...] = jnp.concatenate(
        [
            send1_ref[conts:, :] + got1_ref[conts:, :],
            send2_ref[conts:, :] + got2_ref[conts:, :],
        ],
        axis=1,
    )
    next_kernel(
        send1_ref,
        send2_ref,
        got1_ref,
        got2_ref,
        z_ref,
        degree_ref,
        edge_ref,
        p_ref,
        c_ref,
        gain_ref,
        out1_ref,
        out2_ref,
        z_out_ref,
        delta_ref,
        flow_ref,
        both_ref,
    )


def inner_step(flow_ref, x_ref, count_ref, inner_ref):
    net = times(flow_ref[...], inner_ref[...])
    count = count_ref[:1, :]
    return net, (count * x_ref[...] - net) / (count + 1.0)


def beside_kernel(
    flow_ref, delta_ref, x_ref, count_ref, inner_ref, net_ref, x_out_ref, p_ref, c_ref
):
    net, x = inner_step(flow_ref, x_ref, count_ref, inner_ref)
    net_ref[...] = net
    x_out_ref[...] = x
    p = times_t(x, inner_ref[...])
    p_ref[...] = p
    c_ref[...] = 2.0 * (p + flow_ref[...]) - delta_ref[...]


def beside_last_kernel(
    flow_ref,
    x_ref,
    count_ref,
    inner_ref,
    own_ref,
    dual_ref,
    cost_ref,
    dsum_ref,
    both0_ref,
    both1_ref,
    both2_ref,
    net0_ref,
    net1_ref,
    net2_ref,
    net_ref,
    x_out_ref,
    dual_out_ref,
    sums_ref,
):
    net, x = inner_step(flow_ref, x_ref, count_ref, inner_ref)
    net_ref[...] = net
    x_out_ref[...] = x
    conts = net.shape[0]
    edge = jnp.concatenate([both0_ref[...], both1_ref[...], both2_ref[...]], axis=0)
    spread = times_t(edge, own_ref[...])
    part = 1.0 / (cost_ref[...] + PENALTY + BALANCE)
    dual = dual_ref[...]
    sums_ref[0:1, :] = dsum_ref[:1, :]
    for index, ref in enumerate((net0_ref, net1_ref, net2_ref)):
        whole = ref[...] + spread[index * conts : (index + 1) * conts]
        sums_ref[index + 1 : index + 2, :] = jnp.sum(whole, axis=0, keepdims=True)
        dual = dual + part * (BALANCE * whole - dual)
    sums_ref[4:, :] = jnp.zeros((4, sums_ref.shape[1]), F32)
    dual_out_ref[...] = dual


def last_kernel(
    send1_ref,
    send2_ref,
    got1_ref,
    got2_ref,
    z_ref,
    degree_ref,
    own_ref,
    x_ref,
    net_ref,
    sums_in_ref,
    theta_ref,
    net_out_ref,
    sums_ref,
):
    conts = net_ref.shape[0]
    both = jnp.concatenate(
        [send1_ref[...] + got1_ref[...], send2_ref[...] + got2_ref[...]], axis=1
    )
    degree = degree_ref[:1, :]
    z = (degree * z_ref[...] - both) / (degree + 1.0)
    spread = times_t(jnp.concatenate([both, z], axis=0), own_ref[...])
    net = net_ref[...] + spread[:conts]
    net_out_ref[...] = net
    theta_ref[...] = x_ref[...] + spread[conts:]
    sums_ref[...] = sums_in_ref[...]
    sums_ref[4:5, :] = jnp.sum(net, axis=0, keepdims=True)


def end_kernel(
    contingencies,
    *refs,
):
    *sum_refs, base_ref, load_ref, cost_ref, limit_ref, dual_ref, net_ref, gen_ref, base_out_ref = refs
    total = sum_refs[0][...]
    for ref in sum_refs[1:]:
        total = total + ref[...]
    mean = total / contingencies
    base = base_ref[...]
    load = load_ref[...]
    limit = limit_ref[...]
    part = 1.0 / (cost_ref[...] + PENALTY + BALANCE)
    dual_mean = mean[0:1, :]
    shared = jnp.zeros_like(base)
    for index in range(ROUNDS):
        net_mean = mean[index + 1 : index + 2, :]
        if index == ROUNDS - 1:
            gen_ref[...] = part * (
                PENALTY * base - (dual_ref[...] + shared) + BALANCE * (load + net_ref[...])
            )
        gen_mean = part * (PENALTY * base - dual_mean + BALANCE * (load + net_mean))
        dual_mean = dual_mean + PENALTY * (gen_mean - base)
        shared = shared + PENALTY * (part * (PENALTY * base - shared + BALANCE * load) - base)
        base = jnp.clip(gen_mean + dual_mean / PENALTY, 0.0, limit)
    base_out_ref[...] = base


def call(kernel, outs, *args, flops=2 * 128 * 640 * 512):
    shapes = [jax.ShapeDtypeStruct(shape, dtype) for shape, dtype in outs]
    moved = sum(a.size * a.dtype.itemsize for a in args)
    return pl.pallas_call(
        kernel,
        out_shape=shapes,
        in_specs=[pl.BlockSpec(memory_space=pltpu.VMEM)] * len(args),
        out_specs=[pl.BlockSpec(memory_space=pltpu.VMEM)] * len(outs),
        compiler_params=pltpu.CompilerParams(vmem_limit_bytes=32 * 1024 * 1024),
        cost_estimate=pl.CostEstimate(flops=flops, bytes_accessed=moved, transcendentals=0),
    )(*args)


def swaps(conts, nets):
    def pairs(shift):
        found = []
        for c in range(conts):
            for p in range(nets):
                q = p + 1 if p % 2 == shift else p - 1
                if 0 <= q < nets:
                    found.append((c * nets + p, c * nets + q))
                elif (c ^ 1) < conts:
                    found.append((c * nets + p, (c ^ 1) * nets + p))
                else:
                    found.append((c * nets + p, c * nets + p))
        return found

    return pairs(0), pairs(1)


def local(
    angles,
    lam_from,
    lam_to,
    gen_dual,
    base_prev,
    outage,
    from_bus,
    to_ref,
    halo_rows,
    stiffness,
    bus_load,
    gen_cost,
    gen_limit,
):
    conts, buses = angles.shape
    branches = from_bus.shape[0]
    slots = halo_rows.shape[0]
    edges = 2 * slots
    cont_size = lax.axis_size("cont")
    net_size = lax.axis_size("net")
    swap1, swap2 = swaps(cont_size, net_size)
    axes = ("cont", "net")

    def trade(first, second):
        return lax.ppermute(first, axes, swap1), lax.ppermute(second, axes, swap2)

    from_row = from_bus.reshape(1, branches)
    to_row = to_ref.reshape(1, branches)
    halo_row = halo_rows.reshape(1, slots)
    stiff_row = stiffness.reshape(1, branches)
    base_row = base_prev.reshape(1, buses)
    load_row = bus_load.reshape(1, buses)
    cost_row = gen_cost.reshape(1, buses)
    limit_row = gen_limit.reshape(1, buses)

    bus = ((conts, buses), F32)
    branch = ((conts, branches), F32)
    half = ((conts, slots), F32)
    edge = ((conts, edges), F32)
    tall = ((conts + 8, slots), F32)

    pick1, pick2, own = call(
        pick_kernel, [half, half, ((buses, edges), BF16)], angles, halo_row
    )
    got1, got2 = trade(pick1, pick2)
    edge_table, inner_table, gain, x, p, c, count_edge, count_inner, dual_sum = call(
        prep_kernel,
        [
            ((branches, edges), BF16),
            ((branches, buses), BF16),
            branch,
            bus,
            branch,
            branch,
            ((8, edges), F32),
            ((8, buses), F32),
            ((8, buses), F32),
        ],
        angles,
        lam_from,
        lam_to,
        outage,
        from_row,
        to_row,
        halo_row,
        stiff_row,
        gen_dual,
    )
    send1, send2, z, delta, flow = call(
        first_kernel,
        [tall, tall, edge, branch, branch],
        pick1,
        pick2,
        got1,
        got2,
        halo_row,
        edge_table,
        p,
        c,
        gain,
        count_edge,
    )
    nets = []
    boths = []
    for index in range(1, ROUNDS):
        got1, got2 = trade(send1, send2)
        net, x, p, c = call(
            beside_kernel,
            [bus, bus, branch, branch],
            flow,
            delta,
            x,
            count_inner,
            inner_table,
        )
        nets.append(net)
        if index == 1:
            send1, send2, z, delta, flow, both, degree = call(
                second_kernel,
                [half, half, edge, branch, branch, edge, ((8, edges), F32)],
                send1,
                send2,
                got1,
                got2,
                z,
                edge_table,
                p,
                c,
                gain,
            )
        else:
            send1, send2, z, delta, flow, both = call(
                next_kernel,
                [half, half, edge, branch, branch, edge],
                send1,
                send2,
                got1,
                got2,
                z,
                degree,
                edge_table,
                p,
                c,
                gain,
            )
        boths.append(both)
    got1, got2 = trade(send1, send2)
    net, x, dual, sums = call(
        beside_last_kernel,
        [bus, bus, bus, ((8, buses), F32)],
        flow,
        x,
        count_inner,
        inner_table,
        own,
        gen_dual,
        cost_row,
        dual_sum,
        *boths,
        *nets,
    )
    theta, net, sums = call(
        last_kernel,
        [bus, bus, ((8, buses), F32)],
        send1,
        send2,
        got1,
        got2,
        z,
        degree,
        own,
        x,
        net,
        sums,
    )
    parts = [sums]
    for shift in range(1, cont_size):
        parts.append(
            lax.ppermute(sums, "cont", [(i, (i + shift) % cont_size) for i in range(cont_size)])
        )

    def finish(*refs):
        end_kernel(float(conts * cont_size), *refs)

    generation, base = call(
        finish,
        [bus, ((1, buses), F32)],
        *parts,
        base_row,
        load_row,
        cost_row,
        limit_row,
        dual,
        net,
    )
    return theta, generation, base.reshape(buses)


def solution(mesh):
    placed = (
        P("cont", "net"),
        P("cont", "net"),
        P("cont", "net"),
        P("cont", "net"),
        P("net"),
        P("cont", "net"),
        P("net"),
        P("net"),
        P("net"),
        P("net"),
        P("net"),
        P("net"),
        P("net"),
    )
    return jax.shard_map(
        local,
        mesh=mesh,
        in_specs=placed,
        out_specs=(P("cont", "net"), P("cont", "net"), P("net")),
        check_vma=False,
    )
```

time: 121 us -> 38 us (0.31)
  blocking collectives: 34.8 us -> 0 us
  matrix products: 28.4 us -> 0 us
  starting transfers between devices: 36.8 us -> 13.3 us
  other arithmetic: 7.32 us -> 0 us
  Pallas kernels: 0 us -> 7.27 us
  waiting for transfers between devices: 6.08 us -> 11 us
    psum x4 -> x0, blocking collectives: 34.8 us -> none  [local(): total = lax.psum(partial_value, 'cont')]
    dot_general x16 -> x0, matrix products: 28.4 us -> none  [the longest x8 18.3 us: lookup(): lax.dot_general(values, table, (((1,), (1,)), ((), ())), precision=lax.Pr...]
    ppermute x13, starting transfers between devices: 36.8 us -> 13.3 us  [the longest x10 9.75 us: trade(): return (lax.ppermute(first, axes, swap1), lax.ppermute(second, axes, swap2))]
    pallas_call x0 -> x12, Pallas kernels: none -> 7.27 us  [call(): pl.pallas_call(kernel, out_shape=shapes, in_specs=[pl.BlockSpec(memory_sp...]
    ppermute x13, waiting for transfers between devices: 6.08 us -> 11 us  [the longest x10 6.91 us: trade(): return (lax.ppermute(first, axes, swap1), lax.ppermute(second, axes, swap2))]
    reduce_sum x6 -> x0, other arithmetic: 4.8 us -> none  [the longest x4 3.7 us: local(): partial_value = jnp.sum(generation + gen_dual / penalty, axis=0)]
    unnamed x86 -> x26, local copies, waits for them, and re-layouts: 5.18 us -> 5.44 us
  transfers between devices with their start and end apart: 13 -> 13, of which waited for: 5 -> 7; matrix products, arithmetic and copies ran while one was open for 7% -> 0% of each run, Pallas kernels for 0% -> 8%
where the time goes in v1:
time: 38 us; the launch traced here: 37.8 us
  starting transfers between devices  13.3 us (35%)
  waiting for transfers between devices  11 us (29%)
  Pallas kernels  7.27 us (19%)
  local copies, waits for them, and re-layouts  5.45 us (14%)
  between operations  0.8 us (2%)
    ppermute x10, starting transfers between devices, trade(): return (lax.ppermute(first, axes, swap1), lax.ppermute(second, axes, swap2))  9.75 us
    pallas_call x12, Pallas kernels, call(): pl.pallas_call(kernel, out_shape=shapes, in_specs=[pl.BlockSpec(memory_sp...  7.27 us
    ppermute x10, waiting for transfers between devices, trade(): return (lax.ppermute(first, axes, swap1), lax.ppermute(second, axes, swap2))  6.91 us
    unnamed x26, local copies, waits for them, and re-layouts  5.44 us
    ppermute x3, waiting for transfers between devices, local(): lax.ppermute(sums, 'cont', [(i, (i + shift) % cont_size) for i in range(c...  4.04 us
    ppermute x3, starting transfers between devices, local(): lax.ppermute(sums, 'cont', [(i, (i + shift) % cont_size) for i in range(c...  3.55 us
  transfers between devices with their start and end apart: 13, of which 7 were waited for; matrix products, arithmetic and copies ran while one was open for 0% of the time, Pallas kernels for 8%

profile of v1, /device:TPU:0, one launch (start us, length us, event | category | flops | bytes accessed | tf_op | source)
XLA Modules:
  0.0 37.8 jit_solution(13599709938747901760)
XLA Ops:
  0.6 0.6 %copy-done.6 = s32[128]{0:T(128)S(1)} copy-done((s32[128]{0:T(128)S(1)}, s32[128]{0:T(128)}, u32[]{:S(2)}) %copy-start.6) | copy-done | bytes 536
  1.3 0.9 %copy-done.4 = f32[64,512]{1,0:T(8,128)S(1)} copy-done((f32[64,512]{1,0:T(8,128)S(1)}, f32[64,512]{1,0:T(8,128)}, u32[]{:S(2)}) %copy-start.4) | copy-done | bytes 131096
  3.0 2.6 %collective-permute-start.1 = (f32[64,128]{1,0:T(8,128)S(1)}, f32[64,128]{1,0:T(8,128)S(1)}, u32[]{:S(2)}, u32[]{:S(2)}) collective-permute-start(f32[64,128]{1,0:T(8,128)S(1)} %get-tuple-element.60.pick2_ref), channel_id=1, source_target_pairs={{0,8},{1,2},{2,1},{3,4},{4,3},{5,6},{6,5},{7,15},{8,0},{9,10},{10,... | collective-permute-start | bytes 98312 | tf_op jit(solution)/shard_map/ppermute | solution.py:400
  5.5 0.7 %copy-done.12 = f32[640]{0:T(1024)S(1)} copy-done((f32[640]{0:T(1024)S(1)}, f32[640]{0:T(1024)}, u32[]{:S(2)}) %copy-start.12) | copy-done | bytes 2584
  6.2 0.9 %copy-done.2 = f32[64,640]{1,0:T(8,128)S(1)} copy-done((f32[64,640]{1,0:T(8,128)S(1)}, f32[64,640]{1,0:T(8,128)}, u32[]{:S(2)}) %copy-start.2) | copy-done | bytes 163864
  7.1 0.9 %copy-done.3 = s32[64,640]{1,0:T(8,128)S(1)} copy-done((s32[64,640]{1,0:T(8,128)S(1)}, s32[64,640]{1,0:T(8,128)}, u32[]{:S(2)}) %copy-start.3) | copy-done | bytes 163864
  8.1 1.1 %shard_map.149 = (bf16[640,256]{1,0:T(8,128)(2,1)S(1)}, bf16[640,512]{1,0:T(8,128)(2,1)S(1)}, f32[64,640]{1,0:T(8,128)S(1)}, f32[64,512]{1,0:T(8,128)S(1)}, f32[...) custom-call(f32[64,512]{1,0:T(8,128)S(1)} %copy-done.4, ...), custom_call_target="tpu_custom_call" | custom-call | flops 83886080 | bytes 761856 | tf_op jit(solution)/shard_map/pallas_call | solution.py:348
  9.9 1.5 %collective-permute-start.3 = (f32[72,128]{1,0:T(8,128)S(1)}, f32[72,128]{1,0:T(8,128)S(1)}, u32[]{:S(2)}, u32[]{:S(2)}) collective-permute-start(f32[72,128]{1,0:T(8,128)S(1)} %get-tuple-element.67.send2_ref), channel_id=1, source_target_pairs={{0,8},{1,2},{2,1},{3,4},{4,3},{5,6},{6,5},{7,15},{8,0},{9,10},{10,... | collective-permute-start | bytes 110600 | tf_op jit(solution)/shard_map/ppermute | solution.py:400
  11.9 1.9 %collective-permute-done.3.got2_ref = f32[72,128]{1,0:T(8,128)S(1)} collective-permute-done((f32[72,128]{1,0:T(8,128)S(1)}, f32[72,128]{1,0:T(8,128)S(1)}, u32[]{:S(2)}, u32[]{:S(2)}) %collective-permute-start.3) | collective-permute-done | bytes 36896 | tf_op jit(solution)/shard_map/ppermute | solution.py:400
  14.4 1.5 %collective-permute-start.5 = (f32[64,128]{1,0:T(8,128)S(1)}, f32[64,128]{1,0:T(8,128)S(1)}, u32[]{:S(2)}, u32[]{:S(2)}) collective-permute-start(f32[64,128]{1,0:T(8,128)S(1)} %get-tuple-element.77.send2_ref), channel_id=1, source_target_pairs={{0,8},{1,2},{2,1},{3,4},{4,3},{5,6},{6,5},{7,15},{8,0},{9,10},{10,... | collective-permute-start | bytes 98312 | tf_op jit(solution)/shard_map/ppermute | solution.py:400
  16.5 1.9 %collective-permute-done.5.got2_ref = f32[64,128]{1,0:T(8,128)S(1)} collective-permute-done((f32[64,128]{1,0:T(8,128)S(1)}, f32[64,128]{1,0:T(8,128)S(1)}, u32[]{:S(2)}, u32[]{:S(2)}) %collective-permute-start.5) | collective-permute-done | bytes 32800 | tf_op jit(solution)/shard_map/ppermute | solution.py:400
  18.9 1.5 %collective-permute-start.7 = (f32[64,128]{1,0:T(8,128)S(1)}, f32[64,128]{1,0:T(8,128)S(1)}, u32[]{:S(2)}, u32[]{:S(2)}) collective-permute-start(f32[64,128]{1,0:T(8,128)S(1)} %get-tuple-element.86.send2_ref), channel_id=1, source_target_pairs={{0,8},{1,2},{2,1},{3,4},{4,3},{5,6},{6,5},{7,15},{8,0},{9,10},{10,... | collective-permute-start | bytes 98312 | tf_op jit(solution)/shard_map/ppermute | solution.py:400
  21.0 1.9 %collective-permute-done.7.got2_ref = f32[64,128]{1,0:T(8,128)S(1)} collective-permute-done((f32[64,128]{1,0:T(8,128)S(1)}, f32[64,128]{1,0:T(8,128)S(1)}, u32[]{:S(2)}, u32[]{:S(2)}) %collective-permute-start.7) | collective-permute-done | bytes 32800 | tf_op jit(solution)/shard_map/ppermute | solution.py:400
  22.9 0.9 %shard_map.156 = (f32[64,128]{1,0:T(8,128)S(1)}, f32[64,128]{1,0:T(8,128)S(1)}, f32[64,256]{1,0:T(8,128)S(1)}, f32[64,640]{1,0:T(8,128)}, f32[64,640]{1,0:T(8,128)S(1)}, /*index=5*/f32[64,256]{1,0:T(8,128)S(1)}) custom-call(f32[64,128]{1,0:T(8,128)S(1)} %get-tuple-element.85.send1_ref, f32[64,128]{1,0:T(8,128)S(1)} %get-tuple-element.86.send2_ref, ...), custom_call_target="tpu_custom_call" | custom-call | flops 83886080 | bytes 1024000 | tf_op jit(solution)/shard_map/pallas_call | solution.py:348
  23.9 1.5 %collective-permute-start.9 = (f32[64,128]{1,0:T(8,128)S(1)}, f32[64,128]{1,0:T(8,128)S(1)}, u32[]{:S(2)}, u32[]{:S(2)}) collective-permute-start(f32[64,128]{1,0:T(8,128)S(1)} %get-tuple-element.94.send2_ref), channel_id=1, source_target_pairs={{0,8},{1,2},{2,1},{3,4},{4,3},{5,6},{6,5},{7,15},{8,0},{9,10},{10,... | collective-permute-start | bytes 98312 | tf_op jit(solution)/shard_map/ppermute | solution.py:400
  25.4 0.7 %copy-done.5 = f32[512]{0:T(512)S(1)} copy-done((f32[512]{0:T(512)S(1)}, f32[512]{0:T(512)}, u32[]{:S(2)}) %copy-start.5) | copy-done | bytes 2072
  26.6 1.3 %collective-permute-done.9.got2_ref = f32[64,128]{1,0:T(8,128)S(1)} collective-permute-done((f32[64,128]{1,0:T(8,128)S(1)}, f32[64,128]{1,0:T(8,128)S(1)}, u32[]{:S(2)}, u32[]{:S(2)}) %collective-permute-start.9) | collective-permute-done | bytes 32800 | tf_op jit(solution)/shard_map/ppermute | solution.py:400
  27.8 0.9 %shard_map.158 = (f32[64,512]{1,0:T(8,128)}, f32[64,512]{1,0:T(8,128)S(1)}, f32[8,512]{1,0:T(8,128)S(1)}) custom-call(f32[64,128]{1,0:T(8,128)S(1)} %get-tuple-element.93.send1_ref, f32[64,128]{1,0:T(8,128)S(1)} %get-tuple-element.94.send2_ref, f32[64,128]{1,0:T(8,128)S(1)} %collective-permute-done.8.got1_ref, ...), custom_call_target="tpu_custom_call" | custom-call | flops 83886080 | bytes 745472 | tf_op jit(solution)/shard_map/pallas_call | solution.py:348
  28.8 2.4 %collective-permute-start.12 = (f32[8,512]{1,0:T(8,128)S(1)}, f32[8,512]{1,0:T(8,128)S(1)}, u32[]{:S(2)}, u32[]{:S(2)}) collective-permute-start(f32[8,512]{1,0:T(8,128)S(1)} %get-tuple-element.110.refs_0_), channel_id=1, source_target_pairs={{0,24},{8,0},{16,8},{24,16},{1,25},{9,1},{17,9},{25,17},{2,26},{10... | collective-permute-start | bytes 49160 | tf_op jit(solution)/shard_map/ppermute | solution.py:534
  31.7 0.6 %collective-permute-start.10 = (f32[8,512]{1,0:T(8,128)S(1)}, f32[8,512]{1,0:T(8,128)S(1)}, u32[]{:S(2)}, u32[]{:S(2)}) collective-permute-start(f32[8,512]{1,0:T(8,128)S(1)} %get-tuple-element.110.refs_0_), channel_id=1, source_target_pairs={{0,8},{8,16},{16,24},{24,0},{1,9},{9,17},{17,25},{25,1},{2,10},{10... | collective-permute-start | bytes 49160 | tf_op jit(solution)/shard_map/ppermute | solution.py:534
  32.6 2.5 %collective-permute-done.11.refs_2_ = f32[8,512]{1,0:T(8,128)S(1)} collective-permute-done((f32[8,512]{1,0:T(8,128)S(1)}, f32[8,512]{1,0:T(8,128)S(1)}, u32[]{:S(2)}, u32[]{:S(2)}) %collective-permute-start.11) | collective-permute-done | bytes 16416 | tf_op jit(solution)/shard_map/ppermute | solution.py:534
  35.1 1.2 %collective-permute-done.10.refs_1_ = f32[8,512]{1,0:T(8,128)S(1)} collective-permute-done((f32[8,512]{1,0:T(8,128)S(1)}, f32[8,512]{1,0:T(8,128)S(1)}, u32[]{:S(2)}, u32[]{:S(2)}) %collective-permute-start.10) | collective-permute-done | bytes 16416 | tf_op jit(solution)/shard_map/ppermute | solution.py:534
  36.4 0.7 %copy-done.8 = f32[512]{0:T(512)S(1)} copy-done((f32[512]{0:T(512)S(1)}, f32[512]{0:T(512)}, u32[]{:S(2)}) %copy-start.8) | copy-done | bytes 2072
  37.0 0.7 %shard_map.159 = (f32[64,512]{1,0:T(8,128)}, f32[1,512]{1,0:T(1,128)}) custom-call(f32[8,512]{1,0:T(8,128)S(1)} %get-tuple-element.110.refs_0_, f32[8,512]{1,0:T(8,128)S(1)} %collective-permute-done.10.refs_1_, f32[8,512]{1,0:T(8,128)S(1)} %collective-permute-done.11.refs_2_, f32[8,512]{1,0:T(8,128)S(1)} %collective-permute-done.12.refs_3_, ...), custom_call_target="tpu_custom_call" | custom-call | flops 83886080 | bytes 335872 | tf_op jit(solution)/shard_map/pallas_call | solution.py:348
  (43 shorter events, 5.7 us)
Async XLA Ops:
  1.3 0.9 %copy-start.4 = (f32[64,512]{1,0:T(8,128)S(1)}, f32[64,512]{1,0:T(8,128)}, u32[]{:S(2)}) copy-start(f32[64,512]{1,0:T(8,128)} %theta_ref.3) | copy-start | bytes 393220
  2.2 3.3 %copy-start.10 = (s32[640]{0:T(1024)S(1)}, s32[640]{0:T(1024)}, u32[]{:S(2)}) copy-start(s32[640]{0:T(1024)} %param.19) | copy-start | bytes 7684
  2.2 4.0 %copy-start = (f32[64,512]{1,0:T(8,128)S(1)}, f32[64,512]{1,0:T(8,128)}, u32[]{:S(2)}) copy-start(f32[64,512]{1,0:T(8,128)} %dual_ref.3) | copy-start | bytes 393220
  2.2 4.0 %copy-start.1 = (f32[64,640]{1,0:T(8,128)S(1)}, f32[64,640]{1,0:T(8,128)}, u32[]{:S(2)}) copy-start(f32[64,640]{1,0:T(8,128)} %lam_f_ref.1) | copy-start | bytes 491524
  2.4 3.1 %copy-start.11 = (s32[640]{0:T(1024)S(1)}, s32[640]{0:T(1024)}, u32[]{:S(2)}) copy-start(s32[640]{0:T(1024)} %param.20) | copy-start | bytes 7684
  2.4 6.7 %collective-permute-start = (f32[64,128]{1,0:T(8,128)S(1)}, f32[64,128]{1,0:T(8,128)S(1)}, u32[]{:S(2)}, u32[]{:S(2)}) collective-permute-start(f32[64,128]{1,0:T(8,128)S(1)} %get-tuple-element.59.pick1_ref), channel_id=1, source_target_pairs={{0,1},{1,0},{2,3},{3,2},{4,5},{5,4},{6,7},{7,6},{8,9},{9,8},{10,11... | collective-permute-start | bytes 98312 | tf_op jit(solution)/shard_map/ppermute | solution.py:400
  3.0 6.2 %collective-permute-start.1 = (f32[64,128]{1,0:T(8,128)S(1)}, f32[64,128]{1,0:T(8,128)S(1)}, u32[]{:S(2)}, u32[]{:S(2)}) collective-permute-start(f32[64,128]{1,0:T(8,128)S(1)} %get-tuple-element.60.pick2_ref), channel_id=1, source_target_pairs={{0,8},{1,2},{2,1},{3,4},{4,3},{5,6},{6,5},{7,15},{8,0},{9,10},{10,... | collective-permute-start | bytes 98312 | tf_op jit(solution)/shard_map/ppermute | solution.py:400
  5.5 0.7 %copy-start.12 = (f32[640]{0:T(1024)S(1)}, f32[640]{0:T(1024)}, u32[]{:S(2)}) copy-start(f32[640]{0:T(1024)} %param.22) | copy-start | bytes 7684
  6.2 0.9 %copy-start.2 = (f32[64,640]{1,0:T(8,128)S(1)}, f32[64,640]{1,0:T(8,128)}, u32[]{:S(2)}) copy-start(f32[64,640]{1,0:T(8,128)} %lam_t_ref.1) | copy-start | bytes 491524
  7.1 0.9 %copy-start.3 = (s32[64,640]{1,0:T(8,128)S(1)}, s32[64,640]{1,0:T(8,128)}, u32[]{:S(2)}) copy-start(s32[64,640]{1,0:T(8,128)} %outage_ref.1) | copy-start | bytes 491524
  9.6 2.3 %collective-permute-start.2 = (f32[72,128]{1,0:T(8,128)S(1)}, f32[72,128]{1,0:T(8,128)S(1)}, u32[]{:S(2)}, u32[]{:S(2)}) collective-permute-start(f32[72,128]{1,0:T(8,128)S(1)} %get-tuple-element.66.send1_ref), channel_id=1, source_target_pairs={{0,1},{1,0},{2,3},{3,2},{4,5},{5,4},{6,7},{7,6},{8,9},{9,8},{10,11... | collective-permute-start | bytes 110600 | tf_op jit(solution)/shard_map/ppermute | solution.py:400
  9.9 4.0 %collective-permute-start.3 = (f32[72,128]{1,0:T(8,128)S(1)}, f32[72,128]{1,0:T(8,128)S(1)}, u32[]{:S(2)}, u32[]{:S(2)}) collective-permute-start(f32[72,128]{1,0:T(8,128)S(1)} %get-tuple-element.67.send2_ref), channel_id=1, source_target_pairs={{0,8},{1,2},{2,1},{3,4},{4,3},{5,6},{6,5},{7,15},{8,0},{9,10},{10,... | collective-permute-start | bytes 110600 | tf_op jit(solution)/shard_map/ppermute | solution.py:400
  14.3 2.2 %collective-permute-start.4 = (f32[64,128]{1,0:T(8,128)S(1)}, f32[64,128]{1,0:T(8,128)S(1)}, u32[]{:S(2)}, u32[]{:S(2)}) collective-permute-start(f32[64,128]{1,0:T(8,128)S(1)} %get-tuple-element.76.send1_ref), channel_id=1, source_target_pairs={{0,1},{1,0},{2,3},{3,2},{4,5},{5,4},{6,7},{7,6},{8,9},{9,8},{10,11... | collective-permute-start | bytes 98312 | tf_op jit(solution)/shard_map/ppermute | solution.py:400
  14.4 4.0 %collective-permute-start.5 = (f32[64,128]{1,0:T(8,128)S(1)}, f32[64,128]{1,0:T(8,128)S(1)}, u32[]{:S(2)}, u32[]{:S(2)}) collective-permute-start(f32[64,128]{1,0:T(8,128)S(1)} %get-tuple-element.77.send2_ref), channel_id=1, source_target_pairs={{0,8},{1,2},{2,1},{3,4},{4,3},{5,6},{6,5},{7,15},{8,0},{9,10},{10,... | collective-permute-start | bytes 98312 | tf_op jit(solution)/shard_map/ppermute | solution.py:400
  18.8 2.2 %collective-permute-start.6 = (f32[64,128]{1,0:T(8,128)S(1)}, f32[64,128]{1,0:T(8,128)S(1)}, u32[]{:S(2)}, u32[]{:S(2)}) collective-permute-start(f32[64,128]{1,0:T(8,128)S(1)} %get-tuple-element.85.send1_ref), channel_id=1, source_target_pairs={{0,1},{1,0},{2,3},{3,2},{4,5},{5,4},{6,7},{7,6},{8,9},{9,8},{10,11... | collective-permute-start | bytes 98312 | tf_op jit(solution)/shard_map/ppermute | solution.py:400
  18.9 3.9 %collective-permute-start.7 = (f32[64,128]{1,0:T(8,128)S(1)}, f32[64,128]{1,0:T(8,128)S(1)}, u32[]{:S(2)}, u32[]{:S(2)}) collective-permute-start(f32[64,128]{1,0:T(8,128)S(1)} %get-tuple-element.86.send2_ref), channel_id=1, source_target_pairs={{0,8},{1,2},{2,1},{3,4},{4,3},{5,6},{6,5},{7,15},{8,0},{9,10},{10,... | collective-permute-start | bytes 98312 | tf_op jit(solution)/shard_map/ppermute | solution.py:400
  23.8 2.8 %collective-permute-start.8 = (f32[64,128]{1,0:T(8,128)S(1)}, f32[64,128]{1,0:T(8,128)S(1)}, u32[]{:S(2)}, u32[]{:S(2)}) collective-permute-start(f32[64,128]{1,0:T(8,128)S(1)} %get-tuple-element.93.send1_ref), channel_id=1, source_target_pairs={{0,1},{1,0},{2,3},{3,2},{4,5},{5,4},{6,7},{7,6},{8,9},{9,8},{10,11... | collective-permute-start | bytes 98312 | tf_op jit(solution)/shard_map/ppermute | solution.py:400
  23.9 3.9 %collective-permute-start.9 = (f32[64,128]{1,0:T(8,128)S(1)}, f32[64,128]{1,0:T(8,128)S(1)}, u32[]{:S(2)}, u32[]{:S(2)}) collective-permute-start(f32[64,128]{1,0:T(8,128)S(1)} %get-tuple-element.94.send2_ref), channel_id=1, source_target_pairs={{0,8},{1,2},{2,1},{3,4},{4,3},{5,6},{6,5},{7,15},{8,0},{9,10},{10,... | collective-permute-start | bytes 98312 | tf_op jit(solution)/shard_map/ppermute | solution.py:400
  27.8 8.5 %copy-start.9 = (f32[512]{0:T(512)S(1)}, f32[512]{0:T(512)}, u32[]{:S(2)}) copy-start(f32[512]{0:T(512)} %param.25) | copy-start | bytes 6148
  28.8 3.9 %collective-permute-start.12 = (f32[8,512]{1,0:T(8,128)S(1)}, f32[8,512]{1,0:T(8,128)S(1)}, u32[]{:S(2)}, u32[]{:S(2)}) collective-permute-start(f32[8,512]{1,0:T(8,128)S(1)} %get-tuple-element.110.refs_0_), channel_id=1, source_target_pairs={{0,24},{8,0},{16,8},{24,16},{1,25},{9,1},{17,9},{25,17},{2,26},{10... | collective-permute-start | bytes 49160 | tf_op jit(solution)/shard_map/ppermute | solution.py:534
  31.2 3.9 %collective-permute-start.11 = (f32[8,512]{1,0:T(8,128)S(1)}, f32[8,512]{1,0:T(8,128)S(1)}, u32[]{:S(2)}, u32[]{:S(2)}) collective-permute-start(f32[8,512]{1,0:T(8,128)S(1)} %get-tuple-element.110.refs_0_), channel_id=1, source_target_pairs={{0,16},{8,24},{16,0},{24,8},{1,17},{9,25},{17,1},{25,9},{2,18},{10... | collective-permute-start | bytes 49160 | tf_op jit(solution)/shard_map/ppermute | solution.py:534
  31.7 4.6 %collective-permute-start.10 = (f32[8,512]{1,0:T(8,128)S(1)}, f32[8,512]{1,0:T(8,128)S(1)}, u32[]{:S(2)}, u32[]{:S(2)}) collective-permute-start(f32[8,512]{1,0:T(8,128)S(1)} %get-tuple-element.110.refs_0_), channel_id=1, source_target_pairs={{0,8},{8,16},{16,24},{24,0},{1,9},{9,17},{17,25},{25,1},{2,10},{10... | collective-permute-start | bytes 49160 | tf_op jit(solution)/shard_map/ppermute | solution.py:534
  36.4 0.7 %copy-start.8 = (f32[512]{0:T(512)S(1)}, f32[512]{0:T(512)}, u32[]{:S(2)}) copy-start(f32[512]{0:T(512)} %param.23) | copy-start | bytes 6148
  36.4 0.7 %copy-start.7 = (f32[512]{0:T(512)S(1)}, f32[512]{0:T(512)}, u32[]{:S(2)}) copy-start(f32[512]{0:T(512)} %param.17) | copy-start | bytes 6148
  (2 other events, 1.3 us)

commit v2 on v1

--- a/solution.py
+++ b/solution.py
@@ -42,16 +42,29 @@
     return jnp.concatenate([first, second], axis=1)
 
 
-def pick_kernel(theta_ref, halo_ref, pick1_ref, pick2_ref, own_ref):
+def load_kernel(count, *refs):
+    sources, targets = refs[:count], refs[count : 2 * count]
+    pick1_ref, pick2_ref, own_ref, semaphores = refs[2 * count :]
+    copies = [
+        pltpu.make_async_copy(source, target, semaphores.at[index])
+        for index, (source, target) in enumerate(zip(sources, targets))
+    ]
+    for copy in copies:
+        copy.start()
+    halo_ref, theta_ref = targets[:2]
     buses = theta_ref.shape[1]
+    slots = halo_ref.shape[1]
+    copies[0].wait()
     ids = column_ids(halo_ref[...], buses)
     rows = lax.broadcasted_iota(jnp.int32, (buses, ids.shape[1]), 0)
     table = jnp.where(rows == ids, 1.0, 0.0).astype(BF16)
     own_ref[...] = table
+    copies[1].wait()
     pick = times(theta_ref[...], table)
-    slots = halo_ref.shape[1]
     pick1_ref[...] = pick[:, :slots]
     pick2_ref[...] = pick[:, slots:]
+    for copy in copies[2:]:
+        copy.wait()
 
 
 def prep_kernel(
@@ -64,6 +77,10 @@
     halo_ref,
     stiff_ref,
     dual_ref,
+    base_ref,
+    load_ref,
+    cost_ref,
+    limit_ref,
     edge_ref,
     inner_ref,
     gain_ref,
@@ -73,6 +90,7 @@
     count_edge_ref,
     count_inner_ref,
     sum_ref,
+    rows_ref,
 ):
     buses = theta_ref.shape[1]
     branches = from_ref.shape[1]
@@ -108,6 +126,8 @@
     p_ref[...] = p
     c_ref[...] = p - (lam_f_ref[...] - lam_t_ref[...]) / PENALTY
     sum_ref[...] = jnp.broadcast_to(jnp.sum(dual_ref[...], axis=0, keepdims=True), sum_ref.shape)
+    for index, ref in enumerate((base_ref, load_ref, cost_ref, limit_ref)):
+        rows_ref[2 * index : 2 * index + 2, :] = jnp.broadcast_to(ref[...], (2, buses))
 
 
 def first_kernel(
@@ -159,9 +179,9 @@
     out1_ref,
     out2_ref,
     z_out_ref,
-    delta_ref,
     flow_ref,
     both_ref,
+    delta_ref=None,
 ):
     conts = p_ref.shape[0]
     slots = out1_ref.shape[1]
@@ -177,7 +197,8 @@
     z = (degree * z_ref[...] - both) / (degree + 1.0)
     z_out_ref[...] = z
     moved = times_t(z, edge_ref[...])
-    delta_ref[...] = p_ref[...] + moved
+    if delta_ref is not None:
+        delta_ref[...] = p_ref[...] + moved
     flow = gain_ref[...] * (c_ref[...] + 2.0 * moved)
     flow_ref[...] = flow
     sums = times(flow, edge_ref[...])
@@ -198,9 +219,9 @@
     out1_ref,
     out2_ref,
     z_out_ref,
-    delta_ref,
     flow_ref,
     both_ref,
+    delta_ref,
     degree_ref,
 ):
     conts = p_ref.shape[0]
@@ -225,9 +246,9 @@
         out1_ref,
         out2_ref,
         z_out_ref,
-        delta_ref,
         flow_ref,
         both_ref,
+        delta_ref,
     )
 
 
@@ -255,7 +276,7 @@
     inner_ref,
     own_ref,
     dual_ref,
-    cost_ref,
+    rows_ref,
     dsum_ref,
     both0_ref,
     both1_ref,
@@ -274,82 +295,82 @@
     conts = net.shape[0]
     edge = jnp.concatenate([both0_ref[...], both1_ref[...], both2_ref[...]], axis=0)
     spread = times_t(edge, own_ref[...])
-    part = 1.0 / (cost_ref[...] + PENALTY + BALANCE)
+    part = 1.0 / (rows_ref[4:5, :] + PENALTY + BALANCE)
     dual = dual_ref[...]
     sums_ref[0:1, :] = dsum_ref[:1, :]
     for index, ref in enumerate((net0_ref, net1_ref, net2_ref)):
         whole = ref[...] + spread[index * conts : (index + 1) * conts]
         sums_ref[index + 1 : index + 2, :] = jnp.sum(whole, axis=0, keepdims=True)
         dual = dual + part * (BALANCE * whole - dual)
-    sums_ref[4:, :] = jnp.zeros((4, sums_ref.shape[1]), F32)
+    tail = sums_ref.shape[0] - 4
+    sums_ref[4:, :] = jnp.broadcast_to(jnp.sum(net, axis=0, keepdims=True), (tail, net.shape[1]))
     dual_out_ref[...] = dual
 
 
-def last_kernel(
-    send1_ref,
-    send2_ref,
-    got1_ref,
-    got2_ref,
+def total_kernel(send1_ref, send2_ref, got1_ref, got2_ref, own_ref, sums_in_ref, both_ref, sums_ref):
+    both = jnp.concatenate(
+        [send1_ref[...] + got1_ref[...], send2_ref[...] + got2_ref[...]], axis=1
+    )
+    both_ref[...] = both
+    row = jnp.broadcast_to(jnp.sum(both, axis=0, keepdims=True), (8, both.shape[1]))
+    sums_ref[...] = sums_in_ref[...]
+    sums_ref[4:5, :] = sums_in_ref[4:5, :] + times_t(row, own_ref[...])[:1]
+
+
+def field_kernel(
+    both_ref,
     z_ref,
     degree_ref,
     own_ref,
     x_ref,
     net_ref,
-    sums_in_ref,
+    dual_ref,
+    rows_ref,
     theta_ref,
-    net_out_ref,
-    sums_ref,
+    gen_ref,
 ):
     conts = net_ref.shape[0]
-    both = jnp.concatenate(
-        [send1_ref[...] + got1_ref[...], send2_ref[...] + got2_ref[...]], axis=1
-    )
+    both = both_ref[...]
     degree = degree_ref[:1, :]
     z = (degree * z_ref[...] - both) / (degree + 1.0)
     spread = times_t(jnp.concatenate([both, z], axis=0), own_ref[...])
-    net = net_ref[...] + spread[:conts]
-    net_out_ref[...] = net
     theta_ref[...] = x_ref[...] + spread[conts:]
-    sums_ref[...] = sums_in_ref[...]
-    sums_ref[4:5, :] = jnp.sum(net, axis=0, keepdims=True)
-
-
-def end_kernel(
-    contingencies,
-    *refs,
-):
-    *sum_refs, base_ref, load_ref, cost_ref, limit_ref, dual_ref, net_ref, gen_ref, base_out_ref = refs
+    part = 1.0 / (rows_ref[4:5, :] + PENALTY + BALANCE)
+    gen_ref[...] = part * (BALANCE * (net_ref[...] + spread[:conts]) - dual_ref[...])
+
+
+def end_kernel(contingencies, *refs):
+    *sum_refs, rows_ref, part_gen_ref, gen_ref, base_out_ref = refs
     total = sum_refs[0][...]
     for ref in sum_refs[1:]:
         total = total + ref[...]
     mean = total / contingencies
-    base = base_ref[...]
-    load = load_ref[...]
-    limit = limit_ref[...]
-    part = 1.0 / (cost_ref[...] + PENALTY + BALANCE)
+    base, load = rows_ref[0:1, :], rows_ref[2:3, :]
+    limit = rows_ref[6:7, :]
+    part = 1.0 / (rows_ref[4:5, :] + PENALTY + BALANCE)
     dual_mean = mean[0:1, :]
     shared = jnp.zeros_like(base)
     for index in range(ROUNDS):
         net_mean = mean[index + 1 : index + 2, :]
+        gen_shared = part * (PENALTY * base - shared + BALANCE * load)
         if index == ROUNDS - 1:
-            gen_ref[...] = part * (
-                PENALTY * base - (dual_ref[...] + shared) + BALANCE * (load + net_ref[...])
-            )
+            gen_ref[...] = part_gen_ref[...] + gen_shared
         gen_mean = part * (PENALTY * base - dual_mean + BALANCE * (load + net_mean))
         dual_mean = dual_mean + PENALTY * (gen_mean - base)
-        shared = shared + PENALTY * (part * (PENALTY * base - shared + BALANCE * load) - base)
+        shared = shared + PENALTY * (gen_shared - base)
         base = jnp.clip(gen_mean + dual_mean / PENALTY, 0.0, limit)
     base_out_ref[...] = base
 
 
-def call(kernel, outs, *args, flops=2 * 128 * 640 * 512):
+def call(kernel, outs, *args, scratch=(), space=pltpu.VMEM, flops=2 * 128 * 640 * 512):
     shapes = [jax.ShapeDtypeStruct(shape, dtype) for shape, dtype in outs]
     moved = sum(a.size * a.dtype.itemsize for a in args)
     return pl.pallas_call(
         kernel,
         out_shape=shapes,
-        in_specs=[pl.BlockSpec(memory_space=pltpu.VMEM)] * len(args),
+        in_specs=[pl.BlockSpec(memory_space=space)] * len(args),
         out_specs=[pl.BlockSpec(memory_space=pltpu.VMEM)] * len(outs),
+        scratch_shapes=list(scratch),
         compiler_params=pltpu.CompilerParams(vmem_limit_bytes=32 * 1024 * 1024),
         cost_estimate=pl.CostEstimate(flops=flops, bytes_accessed=moved, transcendentals=0),
     )(*args)
@@ -397,12 +418,10 @@
     axes = ("cont", "net")
 
     def trade(first, second):
-        return lax.ppermute(first, axes, swap1), lax.ppermute(second, axes, swap2)
-
-    from_row = from_bus.reshape(1, branches)
-    to_row = to_ref.reshape(1, branches)
+        far = lax.ppermute(second, axes, swap2)
+        return lax.ppermute(first, axes, swap1), far
+
     halo_row = halo_rows.reshape(1, slots)
-    stiff_row = stiffness.reshape(1, branches)
     base_row = base_prev.reshape(1, buses)
     load_row = bus_load.reshape(1, buses)
     cost_row = gen_cost.reshape(1, buses)
@@ -414,11 +433,23 @@
     edge = ((conts, edges), F32)
     tall = ((conts + 8, slots), F32)
 
-    pick1, pick2, own = call(
-        pick_kernel, [half, half, ((buses, edges), BF16)], angles, halo_row
-    )
+    fetched = [halo_row, angles, lam_from, lam_to, outage, gen_dual]
+    fetched += [base_row, load_row, cost_row, limit_row, from_bus, to_ref, stiffness]
+
+    def load(*refs):
+        load_kernel(len(fetched), *refs)
+
+    *here, pick1, pick2, own = call(
+        load,
+        [(a.shape, a.dtype) for a in fetched] + [half, half, ((buses, edges), BF16)],
+        *[pltpu.with_memory_space_constraint(a, pltpu.HBM) for a in fetched],
+        space=pltpu.HBM,
+        scratch=[pltpu.SemaphoreType.DMA((len(fetched),))],
+    )
+    halo_row, angles, lam_from, lam_to, outage, gen_dual = here[:6]
+    from_row, to_row, stiff_row = (a.reshape(1, branches) for a in here[10:])
     got1, got2 = trade(pick1, pick2)
-    edge_table, inner_table, gain, x, p, c, count_edge, count_inner, dual_sum = call(
+    edge_table, inner_table, gain, x, p, c, count_edge, count_inner, dual_sum, rows = call(
         prep_kernel,
         [
             ((branches, edges), BF16),
@@ -428,6 +459,7 @@
             branch,
             branch,
             ((8, edges), F32),
+            ((8, buses), F32),
             ((8, buses), F32),
             ((8, buses), F32),
         ],
@@ -440,6 +472,7 @@
         halo_row,
         stiff_row,
         gen_dual,
+        *here[6:10],
     )
     send1, send2, z, delta, flow = call(
         first_kernel,
@@ -469,10 +502,11 @@
             inner_table,
         )
         nets.append(net)
+        outs = [half, half, edge, branch, edge]
         if index == 1:
-            send1, send2, z, delta, flow, both, degree = call(
+            send1, send2, z, flow, both, delta, degree = call(
                 second_kernel,
-                [half, half, edge, branch, branch, edge, ((8, edges), F32)],
+                outs + [branch, ((8, edges), F32)],
                 send1,
                 send2,
                 got1,
@@ -484,9 +518,11 @@
                 gain,
             )
         else:
-            send1, send2, z, delta, flow, both = call(
+            if index < ROUNDS - 1:
+                outs = outs + [branch]
+            send1, send2, z, flow, both, *deltas = call(
                 next_kernel,
-                [half, half, edge, branch, branch, edge],
+                outs,
                 send1,
                 send2,
                 got1,
@@ -498,6 +534,7 @@
                 c,
                 gain,
             )
+            delta = deltas[0] if deltas else None
         boths.append(both)
     got1, got2 = trade(send1, send2)
     net, x, dual, sums = call(
@@ -509,24 +546,13 @@
         inner_table,
         own,
         gen_dual,
-        cost_row,
+        rows,
         dual_sum,
         *boths,
         *nets,
     )
-    theta, net, sums = call(
-        last_kernel,
-        [bus, bus, ((8, buses), F32)],
-        send1,
-        send2,
-        got1,
-        got2,
-        z,
-        degree,
-        own,
-        x,
-        net,
-        sums,
+    both, sums = call(
+        total_kernel, [edge, ((8, buses), F32)], send1, send2, got1, got2, own, sums
     )
     parts = [sums]
     for shift in range(1, cont_size):
@@ -534,20 +560,14 @@
             lax.ppermute(sums, "cont", [(i, (i + shift) % cont_size) for i in range(cont_size)])
         )
 
+    theta, part_gen = call(
+        field_kernel, [bus, bus], both, z, degree, own, x, net, dual, rows
+    )
+
     def finish(*refs):
         end_kernel(float(conts * cont_size), *refs)
 
-    generation, base = call(
-        finish,
-        [bus, ((1, buses), F32)],
-        *parts,
-        base_row,
-        load_row,
-        cost_row,
-        limit_row,
-        dual,
-        net,
-    )
+    generation, base = call(finish, [bus, ((1, buses), F32)], *parts, rows, part_gen)
     return theta, generation, base.reshape(buses)
 
 

time: 38 us -> 33.5 us (0.88)
  local copies, waits for them, and re-layouts: 5.45 us -> 0.01 us
  starting transfers between devices: 13.3 us -> 16.9 us
  waiting for transfers between devices: 11 us -> 7.61 us
  Pallas kernels: 7.27 us -> 8.07 us
    unnamed x26 -> x0, local copies, waits for them, and re-layouts: 5.44 us -> none
    ppermute x3, waiting for transfers between devices: 4.04 us -> 1.38 us  [local(): lax.ppermute(sums, 'cont', [(i, (i + shift) % cont_size) for i in range(c...]
    ppermute x10, starting transfers between devices: 9.75 us -> 11.9 us  [the longest x5 10.6 us: trade(): far = lax.ppermute(second, axes, swap2)]
    ppermute x3, starting transfers between devices: 3.55 us -> 5 us  [local(): lax.ppermute(sums, 'cont', [(i, (i + shift) % cont_size) for i in range(c...]
    pallas_call x12 -> x13, Pallas kernels: 7.27 us -> 8.07 us  [call(): pl.pallas_call(kernel, out_shape=shapes, in_specs=[pl.BlockSpec(memory_sp...]
    ppermute x10, waiting for transfers between devices: 6.91 us -> 6.23 us  [the longest x5 6.21 us: trade(): far = lax.ppermute(second, axes, swap2)]
  transfers between devices with their start and end apart: 13 -> 13, of which waited for: 7 -> 6; matrix products, arithmetic and copies ran while one was open for 0% -> 0% of each run, Pallas kernels for 8% -> 12%
where the time goes in v2:
time: 33.5 us; the launch traced here: 33.3 us
  starting transfers between devices  16.9 us (50%)
  Pallas kernels  8.07 us (24%)
  waiting for transfers between devices  7.61 us (23%)
  between operations  0.76 us (2%)
    ppermute x5, starting transfers between devices, trade(): far = lax.ppermute(second, axes, swap2)  10.6 us
    pallas_call x13, Pallas kernels, call(): pl.pallas_call(kernel, out_shape=shapes, in_specs=[pl.BlockSpec(memory_sp...  8.07 us
    ppermute x5, waiting for transfers between devices, trade(): far = lax.ppermute(second, axes, swap2)  6.21 us
    ppermute x3, starting transfers between devices, local(): lax.ppermute(sums, 'cont', [(i, (i + shift) % cont_size) for i in range(c...  5 us
    ppermute x3, waiting for transfers between devices, local(): lax.ppermute(sums, 'cont', [(i, (i + shift) % cont_size) for i in range(c...  1.38 us
    ppermute x5, starting transfers between devices, trade(): return (lax.ppermute(first, axes, swap1), far)  1.24 us
  transfers between devices with their start and end apart: 13, of which 6 were waited for; matrix products, arithmetic and copies ran while one was open for 0% of the time, Pallas kernels for 12%

profile of v2, /device:TPU:0, one launch (start us, length us, event | category | flops | bytes accessed | tf_op | source)
XLA Modules:
  0.0 33.3 jit_solution(14171210808548037066)
XLA Ops:
  0.6 1.4 %shard_map.148 = (s32[1,128]{1,0:T(1,128)S(1)}, f32[64,512]{1,0:T(8,128)S(1)}, f32[64,640]{1,0:T(8,128)S(1)}, f32[64,640]{1,0:T(8,128)S(1)}, s32[64,640]{1,0:T(8...) custom-call(s32[1,128]{1,0:T(1,128)} %bitcast.10, ...), custom_call_target="tpu_custom_call" | custom-call | flops 83886080 | bytes 770048 | tf_op jit(solution)/shard_map/pallas_call | solution.py:368
  2.0 0.5 %collective-permute-start = (f32[64,128]{1,0:T(8,128)S(1)}, f32[64,128]{1,0:T(8,128)S(1)}, u32[]{:S(2)}, u32[]{:S(2)}) collective-permute-start(f32[64,128]{1,0:T(8,128)S(1)} %get-tuple-element.74.pick1_ref), channel_id=1, source_target_pairs={{0,1},{1,0},{2,3},{3,2},{4,5},{5,4},{6,7},{7,6},{8,9},{9,8},{10,11... | collective-permute-start | bytes 98312 | tf_op jit(solution)/shard_map/ppermute | solution.py:422
  2.5 2.6 %collective-permute-start.1 = (f32[64,128]{1,0:T(8,128)S(1)}, f32[64,128]{1,0:T(8,128)S(1)}, u32[]{:S(2)}, u32[]{:S(2)}) collective-permute-start(f32[64,128]{1,0:T(8,128)S(1)} %get-tuple-element.75.pick2_ref), channel_id=1, source_target_pairs={{0,8},{1,2},{2,1},{3,4},{4,3},{5,6},{6,5},{7,15},{8,0},{9,10},{10,... | collective-permute-start | bytes 98312 | tf_op jit(solution)/shard_map/ppermute | solution.py:421
  5.1 1.1 %shard_map.149 = (bf16[640,256]{1,0:T(8,128)(2,1)S(1)}, bf16[640,512]{1,0:T(8,128)(2,1)S(1)}, f32[64,640]{1,0:T(8,128)S(1)}, f32[64,512]{1,0:T(8,128)S(1)}, f32[...) custom-call(f32[64,512]{1,0:T(8,128)S(1)} %get-tuple-element.77.thet, ...), custom_call_target="tpu_custom_call" | custom-call | flops 83886080 | bytes 770048 | tf_op jit(solution)/shard_map/pallas_call | solution.py:368
  6.2 0.8 %collective-permute-done.1.got2_ref = f32[64,128]{1,0:T(8,128)S(1)} collective-permute-done((f32[64,128]{1,0:T(8,128)S(1)}, f32[64,128]{1,0:T(8,128)S(1)}, u32[]{:S(2)}, u32[]{:S(2)}) %collective-permute-start.1) | collective-permute-done | bytes 32800 | tf_op jit(solution)/shard_map/ppermute | solution.py:421
  7.6 2.0 %collective-permute-start.3 = (f32[72,128]{1,0:T(8,128)S(1)}, f32[72,128]{1,0:T(8,128)S(1)}, u32[]{:S(2)}, u32[]{:S(2)}) collective-permute-start(f32[72,128]{1,0:T(8,128)S(1)} %get-tuple-element.95.send2_ref), channel_id=1, source_target_pairs={{0,8},{1,2},{2,1},{3,4},{4,3},{5,6},{6,5},{7,15},{8,0},{9,10},{10,... | collective-permute-start | bytes 110600 | tf_op jit(solution)/shard_map/ppermute | solution.py:421
  9.6 0.5 %shard_map.151 = (f32[64,512]{1,0:T(8,128)S(1)}, f32[64,512]{1,0:T(8,128)S(1)}, f32[64,640]{1,0:T(8,128)S(1)}, f32[64,640]{1,0:T(8,128)S(1)}) custom-call(f32[64,640]{1,0:T(8,128)S(1)} %get-tuple-element.97.flow_ref, f32[64,640]{1,0:T(8,128)S(1)} %get-tuple-element.98.delta_ref, f32[64,512]{1,0:T(8,128)S(1)} %get-tuple-element.99.x_ref, ...), custom_call_target="tpu_custom_call" | custom-call | flops 83886080 | bytes 1130496 | tf_op jit(solution)/shard_map/pallas_call | solution.py:368
  10.2 1.4 %collective-permute-done.3.got2_ref = f32[72,128]{1,0:T(8,128)S(1)} collective-permute-done((f32[72,128]{1,0:T(8,128)S(1)}, f32[72,128]{1,0:T(8,128)S(1)}, u32[]{:S(2)}, u32[]{:S(2)}) %collective-permute-start.3) | collective-permute-done | bytes 36896 | tf_op jit(solution)/shard_map/ppermute | solution.py:421
  11.5 0.4 %shard_map.152 = (f32[64,128]{1,0:T(8,128)S(1)}, f32[64,128]{1,0:T(8,128)S(1)}, f32[64,256]{1,0:T(8,128)S(1)}, f32[64,640]{1,0:T(8,128)S(1)}, f32[64,256]{1,0:T(...) custom-call(f32[72,128]{1,0:T(8,128)S(1)} %get-tuple-element.94.send1_ref, ...), custom_call_target="tpu_custom_call" | custom-call | flops 83886080 | bytes 1032192 | tf_op jit(solution)/shard_map/pallas_call | solution.py:368
  12.2 2.0 %collective-permute-start.5 = (f32[64,128]{1,0:T(8,128)S(1)}, f32[64,128]{1,0:T(8,128)S(1)}, u32[]{:S(2)}, u32[]{:S(2)}) collective-permute-start(f32[64,128]{1,0:T(8,128)S(1)} %get-tuple-element.105.send2_ref), channel_id=1, source_target_pairs={{0,8},{1,2},{2,1},{3,4},{4,3},{5,6},{6,5},{7,15},{8,0},{9,10},{10,... | collective-permute-start | bytes 98312 | tf_op jit(solution)/shard_map/ppermute | solution.py:421
  14.2 0.5 %shard_map.153 = (f32[64,512]{1,0:T(8,128)S(1)}, f32[64,512]{1,0:T(8,128)S(1)}, f32[64,640]{1,0:T(8,128)S(1)}, f32[64,640]{1,0:T(8,128)S(1)}) custom-call(f32[64,640]{1,0:T(8,128)S(1)} %get-tuple-element.108.flow_ref, f32[64,640]{1,0:T(8,128)S(1)} %get-tuple-element.109.delta_ref, f32[64,512]{1,0:T(8,128)S(1)} %get-tuple-element.110.x_ref, ...), custom_call_target="tpu_custom_call" | custom-call | flops 83886080 | bytes 1130496 | tf_op jit(solution)/shard_map/pallas_call | solution.py:368
  14.7 1.3 %collective-permute-done.5.got2_ref = f32[64,128]{1,0:T(8,128)S(1)} collective-permute-done((f32[64,128]{1,0:T(8,128)S(1)}, f32[64,128]{1,0:T(8,128)S(1)}, u32[]{:S(2)}, u32[]{:S(2)}) %collective-permute-start.5) | collective-permute-done | bytes 32800 | tf_op jit(solution)/shard_map/ppermute | solution.py:421
  16.7 2.0 %collective-permute-start.7 = (f32[64,128]{1,0:T(8,128)S(1)}, f32[64,128]{1,0:T(8,128)S(1)}, u32[]{:S(2)}, u32[]{:S(2)}) collective-permute-start(f32[64,128]{1,0:T(8,128)S(1)} %get-tuple-element.114.send2_ref), channel_id=1, source_target_pairs={{0,8},{1,2},{2,1},{3,4},{4,3},{5,6},{6,5},{7,15},{8,0},{9,10},{10,... | collective-permute-start | bytes 98312 | tf_op jit(solution)/shard_map/ppermute | solution.py:421
  18.7 0.5 %shard_map.155 = (f32[64,512]{1,0:T(8,128)S(1)}, f32[64,512]{1,0:T(8,128)S(1)}, f32[64,640]{1,0:T(8,128)S(1)}, f32[64,640]{1,0:T(8,128)S(1)}) custom-call(f32[64,640]{1,0:T(8,128)S(1)} %get-tuple-element.116.flow_ref, f32[64,640]{1,0:T(8,128)S(1)} %get-tuple-element.117.delta_ref, f32[64,512]{1,0:T(8,128)S(1)} %get-tuple-element.118.x_ref, ...), custom_call_target="tpu_custom_call" | custom-call | flops 83886080 | bytes 1130496 | tf_op jit(solution)/shard_map/pallas_call | solution.py:368
  19.3 1.3 %collective-permute-done.7.got2_ref = f32[64,128]{1,0:T(8,128)S(1)} collective-permute-done((f32[64,128]{1,0:T(8,128)S(1)}, f32[64,128]{1,0:T(8,128)S(1)}, u32[]{:S(2)}, u32[]{:S(2)}) %collective-permute-start.7) | collective-permute-done | bytes 32800 | tf_op jit(solution)/shard_map/ppermute | solution.py:421
  21.2 2.0 %collective-permute-start.9 = (f32[64,128]{1,0:T(8,128)S(1)}, f32[64,128]{1,0:T(8,128)S(1)}, u32[]{:S(2)}, u32[]{:S(2)}) collective-permute-start(f32[64,128]{1,0:T(8,128)S(1)} %get-tuple-element.122.send2_ref), channel_id=1, source_target_pairs={{0,8},{1,2},{2,1},{3,4},{4,3},{5,6},{6,5},{7,15},{8,0},{9,10},{10,... | collective-permute-start | bytes 98312 | tf_op jit(solution)/shard_map/ppermute | solution.py:421
  23.2 0.5 %shard_map.157 = (f32[64,512]{1,0:T(8,128)S(1)}, f32[64,512]{1,0:T(8,128)S(1)}, f32[64,512]{1,0:T(8,128)S(1)}, f32[8,512]{1,0:T(8,128)S(1)}) custom-call(f32[64,640]{1,0:T(8,128)S(1)} %get-tuple-element.124.flow_ref, f32[64,512]{1,0:T(8,128)S(1)} %get-tuple-element.125.x_ref, f32[8,512]{1,0:T(8,128)S(1)} %get-tuple-element.100.count_ref, ...), custom_call_target="tpu_custom_call" | custom-call | flops 83886080 | bytes 1982464 | tf_op jit(solution)/shard_map/pallas_call | solution.py:368
  23.7 1.4 %collective-permute-done.9.got2_ref = f32[64,128]{1,0:T(8,128)S(1)} collective-permute-done((f32[64,128]{1,0:T(8,128)S(1)}, f32[64,128]{1,0:T(8,128)S(1)}, u32[]{:S(2)}, u32[]{:S(2)}) %collective-permute-start.9) | collective-permute-done | bytes 32800 | tf_op jit(solution)/shard_map/ppermute | solution.py:421
  25.3 2.0 %collective-permute-start.10 = (f32[8,512]{1,0:T(8,128)S(1)}, f32[8,512]{1,0:T(8,128)S(1)}, u32[]{:S(2)}, u32[]{:S(2)}) collective-permute-start(f32[8,512]{1,0:T(8,128)S(1)} %get-tuple-element.141.refs_0_), channel_id=1, source_target_pairs={{0,8},{8,16},{16,24},{24,0},{1,9},{9,17},{17,25},{25,1},{2,10},{10... | collective-permute-start | bytes 49160 | tf_op jit(solution)/shard_map/ppermute | solution.py:560
  27.3 1.5 %collective-permute-start.11 = (f32[8,512]{1,0:T(8,128)S(1)}, f32[8,512]{1,0:T(8,128)S(1)}, u32[]{:S(2)}, u32[]{:S(2)}) collective-permute-start(f32[8,512]{1,0:T(8,128)S(1)} %get-tuple-element.141.refs_0_), channel_id=1, source_target_pairs={{0,16},{8,24},{16,0},{24,8},{1,17},{9,25},{17,1},{25,9},{2,18},{10... | collective-permute-start | bytes 49160 | tf_op jit(solution)/shard_map/ppermute | solution.py:560
  28.9 1.4 %collective-permute-start.12 = (f32[8,512]{1,0:T(8,128)S(1)}, f32[8,512]{1,0:T(8,128)S(1)}, u32[]{:S(2)}, u32[]{:S(2)}) collective-permute-start(f32[8,512]{1,0:T(8,128)S(1)} %get-tuple-element.141.refs_0_), channel_id=1, source_target_pairs={{0,24},{8,0},{16,8},{24,16},{1,25},{9,1},{17,9},{25,17},{2,26},{10... | collective-permute-start | bytes 49160 | tf_op jit(solution)/shard_map/ppermute | solution.py:560
  30.3 0.9 %shard_map.159 = (f32[64,512]{1,0:T(8,128)}, f32[64,512]{1,0:T(8,128)S(1)}) custom-call(f32[64,256]{1,0:T(8,128)S(1)} %get-tuple-element.135.both_ref, f32[64,256]{1,0:T(8,128)S(1)} %get-tuple-element.136.z_ref, f32[8,256]{1,0:T(8,128)S(1)} %get-tuple-element.107.degree_ref, bf16[512,256]{1,0:T(8,128)(2,1)S(1)} %get-tuple-element.123.own_ref, ...), custom_call_target="tpu_custom_call" | custom-call | flops 83886080 | bytes 811008 | tf_op jit(solution)/shard_map/pallas_call | solution.py:368
  31.2 1.4 %collective-permute-done.12.refs_3_ = f32[8,512]{1,0:T(8,128)S(1)} collective-permute-done((f32[8,512]{1,0:T(8,128)S(1)}, f32[8,512]{1,0:T(8,128)S(1)}, u32[]{:S(2)}, u32[]{:S(2)}) %collective-permute-start.12) | collective-permute-done | bytes 16416 | tf_op jit(solution)/shard_map/ppermute | solution.py:560
  32.6 0.7 %shard_map.160 = (f32[64,512]{1,0:T(8,128)}, f32[1,512]{1,0:T(1,128)}) custom-call(f32[8,512]{1,0:T(8,128)S(1)} %get-tuple-element.141.refs_0_, f32[8,512]{1,0:T(8,128)S(1)} %collective-permute-done.10.refs_1_, f32[8,512]{1,0:T(8,128)S(1)} %collective-permute-done.11.refs_2_, f32[8,512]{1,0:T(8,128)S(1)} %collective-permute-done.12.refs_3_, ...), custom_call_target="tpu_custom_call" | custom-call | flops 83886080 | bytes 212992 | tf_op jit(solution)/shard_map/pallas_call | solution.py:368
  (18 shorter events, 2.2 us)
Async XLA Ops:
  2.0 4.2 %collective-permute-start = (f32[64,128]{1,0:T(8,128)S(1)}, f32[64,128]{1,0:T(8,128)S(1)}, u32[]{:S(2)}, u32[]{:S(2)}) collective-permute-start(f32[64,128]{1,0:T(8,128)S(1)} %get-tuple-element.74.pick1_ref), channel_id=1, source_target_pairs={{0,1},{1,0},{2,3},{3,2},{4,5},{5,4},{6,7},{7,6},{8,9},{9,8},{10,11... | collective-permute-start | bytes 98312 | tf_op jit(solution)/shard_map/ppermute | solution.py:422
  2.5 4.5 %collective-permute-start.1 = (f32[64,128]{1,0:T(8,128)S(1)}, f32[64,128]{1,0:T(8,128)S(1)}, u32[]{:S(2)}, u32[]{:S(2)}) collective-permute-start(f32[64,128]{1,0:T(8,128)S(1)} %get-tuple-element.75.pick2_ref), channel_id=1, source_target_pairs={{0,8},{1,2},{2,1},{3,4},{4,3},{5,6},{6,5},{7,15},{8,0},{9,10},{10,... | collective-permute-start | bytes 98312 | tf_op jit(solution)/shard_map/ppermute | solution.py:421
  7.4 2.8 %collective-permute-start.2 = (f32[72,128]{1,0:T(8,128)S(1)}, f32[72,128]{1,0:T(8,128)S(1)}, u32[]{:S(2)}, u32[]{:S(2)}) collective-permute-start(f32[72,128]{1,0:T(8,128)S(1)} %get-tuple-element.94.send1_ref), channel_id=1, source_target_pairs={{0,1},{1,0},{2,3},{3,2},{4,5},{5,4},{6,7},{7,6},{8,9},{9,8},{10,11... | collective-permute-start | bytes 110600 | tf_op jit(solution)/shard_map/ppermute | solution.py:422
  7.6 4.0 %collective-permute-start.3 = (f32[72,128]{1,0:T(8,128)S(1)}, f32[72,128]{1,0:T(8,128)S(1)}, u32[]{:S(2)}, u32[]{:S(2)}) collective-permute-start(f32[72,128]{1,0:T(8,128)S(1)} %get-tuple-element.95.send2_ref), channel_id=1, source_target_pairs={{0,8},{1,2},{2,1},{3,4},{4,3},{5,6},{6,5},{7,15},{8,0},{9,10},{10,... | collective-permute-start | bytes 110600 | tf_op jit(solution)/shard_map/ppermute | solution.py:421
  12.0 2.8 %collective-permute-start.4 = (f32[64,128]{1,0:T(8,128)S(1)}, f32[64,128]{1,0:T(8,128)S(1)}, u32[]{:S(2)}, u32[]{:S(2)}) collective-permute-start(f32[64,128]{1,0:T(8,128)S(1)} %get-tuple-element.104.send1_ref), channel_id=1, source_target_pairs={{0,1},{1,0},{2,3},{3,2},{4,5},{5,4},{6,7},{7,6},{8,9},{9,8},{10,11... | collective-permute-start | bytes 98312 | tf_op jit(solution)/shard_map/ppermute | solution.py:422
  12.2 3.9 %collective-permute-start.5 = (f32[64,128]{1,0:T(8,128)S(1)}, f32[64,128]{1,0:T(8,128)S(1)}, u32[]{:S(2)}, u32[]{:S(2)}) collective-permute-start(f32[64,128]{1,0:T(8,128)S(1)} %get-tuple-element.105.send2_ref), channel_id=1, source_target_pairs={{0,8},{1,2},{2,1},{3,4},{4,3},{5,6},{6,5},{7,15},{8,0},{9,10},{10,... | collective-permute-start | bytes 98312 | tf_op jit(solution)/shard_map/ppermute | solution.py:421
  16.5 2.8 %collective-permute-start.6 = (f32[64,128]{1,0:T(8,128)S(1)}, f32[64,128]{1,0:T(8,128)S(1)}, u32[]{:S(2)}, u32[]{:S(2)}) collective-permute-start(f32[64,128]{1,0:T(8,128)S(1)} %get-tuple-element.113.send1_ref), channel_id=1, source_target_pairs={{0,1},{1,0},{2,3},{3,2},{4,5},{5,4},{6,7},{7,6},{8,9},{9,8},{10,11... | collective-permute-start | bytes 98312 | tf_op jit(solution)/shard_map/ppermute | solution.py:422
  16.7 3.9 %collective-permute-start.7 = (f32[64,128]{1,0:T(8,128)S(1)}, f32[64,128]{1,0:T(8,128)S(1)}, u32[]{:S(2)}, u32[]{:S(2)}) collective-permute-start(f32[64,128]{1,0:T(8,128)S(1)} %get-tuple-element.114.send2_ref), channel_id=1, source_target_pairs={{0,8},{1,2},{2,1},{3,4},{4,3},{5,6},{6,5},{7,15},{8,0},{9,10},{10,... | collective-permute-start | bytes 98312 | tf_op jit(solution)/shard_map/ppermute | solution.py:421
  21.0 2.7 %collective-permute-start.8 = (f32[64,128]{1,0:T(8,128)S(1)}, f32[64,128]{1,0:T(8,128)S(1)}, u32[]{:S(2)}, u32[]{:S(2)}) collective-permute-start(f32[64,128]{1,0:T(8,128)S(1)} %get-tuple-element.121.send1_ref), channel_id=1, source_target_pairs={{0,1},{1,0},{2,3},{3,2},{4,5},{5,4},{6,7},{7,6},{8,9},{9,8},{10,11... | collective-permute-start | bytes 98312 | tf_op jit(solution)/shard_map/ppermute | solution.py:422
  21.2 3.9 %collective-permute-start.9 = (f32[64,128]{1,0:T(8,128)S(1)}, f32[64,128]{1,0:T(8,128)S(1)}, u32[]{:S(2)}, u32[]{:S(2)}) collective-permute-start(f32[64,128]{1,0:T(8,128)S(1)} %get-tuple-element.122.send2_ref), channel_id=1, source_target_pairs={{0,8},{1,2},{2,1},{3,4},{4,3},{5,6},{6,5},{7,15},{8,0},{9,10},{10,... | collective-permute-start | bytes 98312 | tf_op jit(solution)/shard_map/ppermute | solution.py:421
  25.3 5.9 %collective-permute-start.10 = (f32[8,512]{1,0:T(8,128)S(1)}, f32[8,512]{1,0:T(8,128)S(1)}, u32[]{:S(2)}, u32[]{:S(2)}) collective-permute-start(f32[8,512]{1,0:T(8,128)S(1)} %get-tuple-element.141.refs_0_), channel_id=1, source_target_pairs={{0,8},{8,16},{16,24},{24,0},{1,9},{9,17},{17,25},{25,1},{2,10},{10... | collective-permute-start | bytes 49160 | tf_op jit(solution)/shard_map/ppermute | solution.py:560
  27.3 3.9 %collective-permute-start.11 = (f32[8,512]{1,0:T(8,128)S(1)}, f32[8,512]{1,0:T(8,128)S(1)}, u32[]{:S(2)}, u32[]{:S(2)}) collective-permute-start(f32[8,512]{1,0:T(8,128)S(1)} %get-tuple-element.141.refs_0_), channel_id=1, source_target_pairs={{0,16},{8,24},{16,0},{24,8},{1,17},{9,25},{17,1},{25,9},{2,18},{10... | collective-permute-start | bytes 49160 | tf_op jit(solution)/shard_map/ppermute | solution.py:560
  28.9 3.7 %collective-permute-start.12 = (f32[8,512]{1,0:T(8,128)S(1)}, f32[8,512]{1,0:T(8,128)S(1)}, u32[]{:S(2)}, u32[]{:S(2)}) collective-permute-start(f32[8,512]{1,0:T(8,128)S(1)} %get-tuple-element.141.refs_0_), channel_id=1, source_target_pairs={{0,24},{8,0},{16,8},{24,16},{1,25},{9,1},{17,9},{25,17},{2,26},{10... | collective-permute-start | bytes 49160 | tf_op jit(solution)/shard_map/ppermute | solution.py:560

commit v3 on v2

v3 whole, which is shorter than its diff:
```python
import jax
import jax.numpy as jnp
from jax import lax
from jax.experimental import pallas as pl
from jax.experimental.pallas import tpu as pltpu
from jax.sharding import PartitionSpec as P

ROUNDS = 4
PENALTY = 1.0
BALANCE = 2.0
F32 = jnp.float32
BF16 = jnp.bfloat16


def halves(value):
    high = value.astype(BF16)
    low = (value - high.astype(F32)).astype(BF16)
    return jnp.concatenate([high, low], axis=0)


def times(value, table):
    rows = value.shape[0]
    both = jnp.dot(halves(value), table, preferred_element_type=F32)
    return both[:rows] + both[rows:]


def times_t(value, table):
    rows = value.shape[0]
    both = lax.dot_general(
        halves(value), table, (((1,), (1,)), ((), ())), preferred_element_type=F32
    )
    return both[:rows] + both[rows:]


def column_ids(halo_row, buses):
    slots = halo_row.shape[1]
    own = jnp.where(halo_row < buses, halo_row, -1)
    away = buses + lax.broadcasted_iota(jnp.int32, (1, slots), 1)
    even = lax.axis_index("net") % 2 == 0
    first = jnp.where(even, away, own)
    second = jnp.where(even, own, away)
    return jnp.concatenate([first, second], axis=1)


def fetch(sources, targets, semaphores):
    copies = [
        pltpu.make_async_copy(source, target, semaphores.at[index])
        for index, (source, target) in enumerate(zip(sources, targets))
    ]
    for copy in copies:
        copy.start()
    return copies


def load_kernel(count, *refs):
    sources, targets = refs[:count], refs[count : 2 * count]
    pick_ref, own_ref, semaphores = refs[2 * count :]
    copies = fetch(sources, targets, semaphores)
    halo_ref, theta_ref = targets[:2]
    buses = theta_ref.shape[1]
    slots = halo_ref.shape[1]
    copies[0].wait()
    ids = column_ids(halo_ref[...], buses)
    rows = lax.broadcasted_iota(jnp.int32, (buses, ids.shape[1]), 0)
    table = jnp.where(rows == ids, 1.0, 0.0).astype(BF16)
    own_ref[...] = table
    copies[1].wait()
    pick_ref[...] = times(theta_ref[...], table[:, slots:])
    for copy in copies[2:]:
        copy.wait()


def prep_kernel(
    lam_f_hbm,
    lam_t_hbm,
    outage_hbm,
    dual_hbm,
    base_hbm,
    load_hbm,
    cost_hbm,
    limit_hbm,
    theta_ref,
    from_ref,
    to_ref,
    halo_ref,
    stiff_ref,
    own_ref,
    dual_ref,
    pick_ref,
    edge_ref,
    inner_ref,
    gain_ref,
    x_ref,
    p_ref,
    c_ref,
    count_edge_ref,
    count_inner_ref,
    sum_ref,
    rows_ref,
    lam_f_ref,
    lam_t_ref,
    outage_ref,
    base_ref,
    load_ref,
    cost_ref,
    limit_ref,
    semaphores,
):
    sources = (
        lam_f_hbm, lam_t_hbm, outage_hbm, dual_hbm, base_hbm, load_hbm, cost_hbm, limit_hbm
    )
    targets = (
        lam_f_ref, lam_t_ref, outage_ref, dual_ref, base_ref, load_ref, cost_ref, limit_ref
    )
    copies = fetch(sources, targets, semaphores)
    buses = theta_ref.shape[1]
    branches = from_ref.shape[1]
    slots = halo_ref.shape[1]
    ids = column_ids(halo_ref[...], buses)
    edges = ids.shape[1]
    pick_ref[...] = times(theta_ref[...], own_ref[:, :slots])
    lanes = lax.broadcasted_iota(jnp.int32, (edges, buses), 1)
    ids_col = jnp.broadcast_to(ids, (edges, edges)).T[:, :1]
    inner = 1.0 - jnp.max(jnp.where(lanes == ids_col, 1.0, 0.0), axis=0, keepdims=True)
    bus_ids = lax.broadcasted_iota(jnp.int32, (1, buses), 1)
    inner_ids = jnp.where(inner > 0.0, bus_ids, -1)
    all_ids = jnp.concatenate([ids, inner_ids], axis=1)
    counts = jnp.zeros((8, all_ids.shape[1]), F32)
    step = 128
    for start in range(0, branches, step):
        part = slice(start, start + step)
        f_col = jnp.broadcast_to(from_ref[:, part], (step, step)).T[:, :1]
        t_col = jnp.broadcast_to(to_ref[:, part], (step, step)).T[:, :1]
        is_f = jnp.where(f_col == all_ids, 1.0, 0.0)
        is_t = jnp.where(t_col == all_ids, 1.0, 0.0)
        signed = (is_f - is_t).astype(BF16)
        edge_ref[part, :] = signed[:, :edges]
        inner_ref[part, :] = signed[:, edges:]
        ends = (is_f + is_t).reshape(step // 8, 8, all_ids.shape[1])
        counts = counts + jnp.sum(ends, axis=0)
    count = jnp.broadcast_to(jnp.sum(counts, axis=0, keepdims=True), counts.shape)
    count_edge_ref[...] = count[:, :edges]
    count_inner_ref[...] = count[:, edges:]
    x = theta_ref[...] * inner
    x_ref[...] = x
    p = times_t(x, inner_ref[...])
    p_ref[...] = p
    for copy in copies:
        copy.wait()
    weight = stiff_ref[...] * (1.0 - outage_ref[...].astype(F32))
    gain_ref[...] = PENALTY * weight / (PENALTY + 2.0 * weight)
    c_ref[...] = p - (lam_f_ref[...] - lam_t_ref[...]) / PENALTY
    sum_ref[...] = jnp.broadcast_to(jnp.sum(dual_ref[...], axis=0, keepdims=True), sum_ref.shape)
    for index, ref in enumerate((base_ref, load_ref, cost_ref, limit_ref)):
        rows_ref[2 * index : 2 * index + 2, :] = jnp.broadcast_to(ref[...], (2, buses))


def near_first_kernel(pick_ref, got_ref, edge_ref, p_ref, c_ref, z_ref, p_out_ref, c_out_ref):
    slots = pick_ref.shape[1]
    even = lax.axis_index("net") % 2 == 0
    z = jnp.where(even, got_ref[...], pick_ref[...])
    z_ref[...] = z
    moved = times_t(z, edge_ref[:, :slots])
    p_out_ref[...] = p_ref[...] + moved
    c_out_ref[...] = c_ref[...] + moved


def far_first_kernel(
    pick_ref,
    got_ref,
    edge_ref,
    p_ref,
    c_ref,
    gain_ref,
    count_ref,
    send_ref,
    z_ref,
    delta_ref,
    flow_ref,
):
    slots = pick_ref.shape[1]
    conts = p_ref.shape[0]
    table = edge_ref[:, slots:]
    even = lax.axis_index("net") % 2 == 0
    z = jnp.where(even, pick_ref[...], got_ref[...])
    z_ref[...] = z
    moved = times_t(z, table)
    delta_ref[...] = p_ref[...] + moved
    flow = gain_ref[...] * (c_ref[...] + moved)
    flow_ref[...] = flow
    send_ref[:conts, :] = times(flow, table)
    send_ref[conts:, :] = count_ref[:, slots:]


def traded(send_ref, got_ref, z_ref, both_ref, z_out_ref, degree):
    conts = z_ref.shape[0]
    both = send_ref[:conts, :] + got_ref[:conts, :]
    both_ref[...] = both
    z = (degree * z_ref[...] - both) / (degree + 1.0)
    z_out_ref[...] = z
    return z


def near(send_ref, got_ref, z_ref, degree, edge_ref, p_ref, c_ref, outs):
    both_ref, z_out_ref, p_out_ref, c_out_ref = outs
    slots = z_ref.shape[1]
    z = traded(send_ref, got_ref, z_ref, both_ref, z_out_ref, degree)
    moved = times_t(z, edge_ref[:, :slots])
    p_out_ref[...] = p_ref[...] + moved
    c_out_ref[...] = c_ref[...] + 2.0 * moved


def near_second_kernel(send_ref, got_ref, z_ref, edge_ref, p_ref, c_ref, *outs):
    conts = z_ref.shape[0]
    *outs, degree_ref = outs
    degree = send_ref[conts:, :] + got_ref[conts:, :]
    degree_ref[...] = degree
    near(send_ref, got_ref, z_ref, degree[:1, :], edge_ref, p_ref, c_ref, outs)


def near_kernel(send_ref, got_ref, z_ref, degree_ref, edge_ref, p_ref, c_ref, *outs):
    near(send_ref, got_ref, z_ref, degree_ref[:1, :], edge_ref, p_ref, c_ref, outs)


def far(send_ref, got_ref, z_ref, degree, edge_ref, p_ref, c_ref, gain_ref, outs):
    both_ref, z_out_ref, flow_ref, out_ref, *deltas = outs
    slots = z_ref.shape[1]
    table = edge_ref[:, slots:]
    z = traded(send_ref, got_ref, z_ref, both_ref, z_out_ref, degree)
    moved = times_t(z, table)
    for delta_ref in deltas:
        delta_ref[...] = p_ref[...] + moved
    flow = gain_ref[...] * (c_ref[...] + 2.0 * moved)
    flow_ref[...] = flow
    out_ref[...] = times(flow, table)


def far_second_kernel(send_ref, got_ref, z_ref, edge_ref, p_ref, c_ref, gain_ref, *outs):
    conts = z_ref.shape[0]
    *outs, degree_ref = outs
    degree = send_ref[conts:, :] + got_ref[conts:, :]
    degree_ref[...] = degree
    far(send_ref, got_ref, z_ref, degree[:1, :], edge_ref, p_ref, c_ref, gain_ref, outs)


def far_kernel(send_ref, got_ref, z_ref, degree_ref, edge_ref, p_ref, c_ref, gain_ref, *outs):
    far(send_ref, got_ref, z_ref, degree_ref[:1, :], edge_ref, p_ref, c_ref, gain_ref, outs)


def inner_step(flow_ref, x_ref, count_ref, inner_ref, edge_ref, send_ref):
    flow = flow_ref[...]
    conts = flow.shape[0]
    slots = send_ref.shape[1]
    send_ref[:conts, :] = times(flow, edge_ref[:, :slots])
    net = times(flow, inner_ref[...])
    count = count_ref[:1, :]
    return net, (count * x_ref[...] - net) / (count + 1.0)


def beside_kernel(
    flow_ref,
    delta_ref,
    x_ref,
    count_ref,
    inner_ref,
    edge_ref,
    *refs,
):
    *counts, net_ref, x_out_ref, p_ref, c_ref, send_ref = refs
    conts, slots = flow_ref.shape[0], send_ref.shape[1]
    for ref in counts:
        send_ref[conts:, :] = ref[:, :slots]
    net, x = inner_step(flow_ref, x_ref, count_ref, inner_ref, edge_ref, send_ref)
    net_ref[...] = net
    x_out_ref[...] = x
    p = times_t(x, inner_ref[...])
    p_ref[...] = p
    c_ref[...] = 2.0 * (p + flow_ref[...]) - delta_ref[...]


def send_last_kernel(flow_ref, edge_ref, send_ref):
    send_ref[...] = times(flow_ref[...], edge_ref[:, : send_ref.shape[1]])


def beside_last_kernel(
    flow_ref,
    x_ref,
    count_ref,
    inner_ref,
    own_ref,
    dual_ref,
    rows_ref,
    dsum_ref,
    *refs,
):
    *refs, net_ref, x_out_ref, dual_out_ref, sums_ref = refs
    rounds = len(refs) // 3
    net = times(flow_ref[...], inner_ref[...])
    count = count_ref[:1, :]
    net_ref[...] = net
    x_out_ref[...] = (count * x_ref[...] - net) / (count + 1.0)
    conts = net.shape[0]
    edge = jnp.concatenate(
        [
            jnp.concatenate([refs[index][...], refs[rounds + index][...]], axis=1)
            for index in range(rounds)
        ],
        axis=0,
    )
    spread = times_t(edge, own_ref[...])
    part = 1.0 / (rows_ref[4:5, :] + PENALTY + BALANCE)
    dual = dual_ref[...]
    sums_ref[0:1, :] = dsum_ref[:1, :]
    for index, ref in enumerate(refs[2 * rounds :]):
        whole = ref[...] + spread[index * conts : (index + 1) * conts]
        sums_ref[index + 1 : index + 2, :] = jnp.sum(whole, axis=0, keepdims=True)
        dual = dual + part * (BALANCE * whole - dual)
    tail = sums_ref.shape[0] - rounds - 1
    sums_ref[rounds + 1 :, :] = jnp.broadcast_to(
        jnp.sum(net, axis=0, keepdims=True), (tail, net.shape[1])
    )
    dual_out_ref[...] = dual


def total_kernel(
    send1_ref, send2_ref, got1_ref, got2_ref, own_ref, sums_in_ref, both_ref, sums_ref
):
    both = jnp.concatenate(
        [send1_ref[...] + got1_ref[...], send2_ref[...] + got2_ref[...]], axis=1
    )
    both_ref[...] = both
    row = jnp.broadcast_to(jnp.sum(both, axis=0, keepdims=True), (8, both.shape[1]))
    sums_ref[...] = sums_in_ref[...]
    last = slice(ROUNDS, ROUNDS + 1)
    sums_ref[last, :] = sums_in_ref[last, :] + times_t(row, own_ref[...])[:1]


def field_kernel(
    both_ref,
    z1_ref,
    z2_ref,
    degree1_ref,
    degree2_ref,
    own_ref,
    x_ref,
    net_ref,
    dual_ref,
    rows_ref,
    theta_ref,
    gen_ref,
):
    conts = net_ref.shape[0]
    both = both_ref[...]
    old = jnp.concatenate([z1_ref[...], z2_ref[...]], axis=1)
    degree = jnp.concatenate([degree1_ref[:1, :], degree2_ref[:1, :]], axis=1)
    z = (degree * old - both) / (degree + 1.0)
    spread = times_t(jnp.concatenate([both, z], axis=0), own_ref[...])
    theta_ref[...] = x_ref[...] + spread[conts:]
    part = 1.0 / (rows_ref[4:5, :] + PENALTY + BALANCE)
    gen_ref[...] = part * (BALANCE * (net_ref[...] + spread[:conts]) - dual_ref[...])


def end_kernel(contingencies, *refs):
    *sum_refs, rows_ref, part_gen_ref, gen_ref, base_out_ref = refs
    total = sum_refs[0][...]
    for ref in sum_refs[1:]:
        total = total + ref[...]
    mean = total / contingencies
    base, load = rows_ref[0:1, :], rows_ref[2:3, :]
    limit = rows_ref[6:7, :]
    part = 1.0 / (rows_ref[4:5, :] + PENALTY + BALANCE)
    dual_mean = mean[0:1, :]
    shared = jnp.zeros_like(base)
    for index in range(ROUNDS):
        net_mean = mean[index + 1 : index + 2, :]
        gen_shared = part * (PENALTY * base - shared + BALANCE * load)
        if index == ROUNDS - 1:
            gen_ref[...] = part_gen_ref[...] + gen_shared
        gen_mean = part * (PENALTY * base - dual_mean + BALANCE * (load + net_mean))
        dual_mean = dual_mean + PENALTY * (gen_mean - base)
        shared = shared + PENALTY * (gen_shared - base)
        base = jnp.clip(gen_mean + dual_mean / PENALTY, 0.0, limit)
    base_out_ref[...] = base


def call(kernel, outs, *args, scratch=(), spaces=None, flops=2 * 128 * 640 * 512):
    shapes = [jax.ShapeDtypeStruct(shape, dtype) for shape, dtype in outs]
    moved = sum(a.size * a.dtype.itemsize for a in args)
    spaces = spaces or [pltpu.VMEM] * len(args)
    return pl.pallas_call(
        kernel,
        out_shape=shapes,
        in_specs=[pl.BlockSpec(memory_space=space) for space in spaces],
        out_specs=[pl.BlockSpec(memory_space=pltpu.VMEM)] * len(outs),
        scratch_shapes=list(scratch),
        compiler_params=pltpu.CompilerParams(vmem_limit_bytes=32 * 1024 * 1024),
        cost_estimate=pl.CostEstimate(flops=flops, bytes_accessed=moved, transcendentals=0),
    )(*args)


def swaps(conts, nets):
    def pairs(shift):
        found = []
        for c in range(conts):
            for p in range(nets):
                q = p + 1 if p % 2 == shift else p - 1
                if 0 <= q < nets:
                    found.append((c * nets + p, c * nets + q))
                elif (c ^ 1) < conts:
                    found.append((c * nets + p, (c ^ 1) * nets + p))
                else:
                    found.append((c * nets + p, c * nets + p))
        return found

    return pairs(0), pairs(1)


def local(
    angles,
    lam_from,
    lam_to,
    gen_dual,
    base_prev,
    outage,
    from_bus,
    to_ref,
    halo_rows,
    stiffness,
    bus_load,
    gen_cost,
    gen_limit,
):
    conts, buses = angles.shape
    branches = from_bus.shape[0]
    slots = halo_rows.shape[0]
    edges = 2 * slots
    cont_size = lax.axis_size("cont")
    net_size = lax.axis_size("net")
    swap1, swap2 = swaps(cont_size, net_size)
    axes = ("cont", "net")

    def trade_near(value):
        return lax.ppermute(value, axes, swap1)

    def trade_far(value):
        return lax.ppermute(value, axes, swap2)

    def in_hbm(*arrays):
        return [pltpu.with_memory_space_constraint(a, pltpu.HBM) for a in arrays]

    bus = ((conts, buses), F32)
    branch = ((conts, branches), F32)
    half = ((conts, slots), F32)
    edge = ((conts, edges), F32)
    tall = ((conts + 8, slots), F32)
    counts = ((8, slots), F32)
    row = ((8, buses), F32)

    halo_row = halo_rows.reshape(1, slots)
    fetched = [halo_row, angles, from_bus, to_ref, stiffness]
    number = len(fetched)

    def load(*refs):
        load_kernel(number, *refs)

    *here, pick2, own = call(
        load,
        [(a.shape, a.dtype) for a in fetched] + [half, ((buses, edges), BF16)],
        *in_hbm(*fetched),
        spaces=[pltpu.HBM] * number,
        scratch=[pltpu.SemaphoreType.DMA((number,))],
    )
    got2 = trade_far(pick2)
    halo_row, angles = here[:2]
    from_row, to_row, stiff_row = (a.reshape(1, branches) for a in here[2:])
    rows = [a.reshape(1, buses) for a in (base_prev, bus_load, gen_cost, gen_limit)]
    fetched = [lam_from, lam_to, outage, gen_dual, *rows]
    near_args = [angles, from_row, to_row, halo_row, stiff_row, own]
    (
        gen_dual,
        pick1,
        edge_table,
        inner_table,
        gain,
        x,
        p,
        c,
        count_edge,
        count_inner,
        dual_sum,
        rows,
    ) = call(
        prep_kernel,
        [
            bus,
            half,
            ((branches, edges), BF16),
            ((branches, buses), BF16),
            branch,
            bus,
            branch,
            branch,
            ((8, edges), F32),
            row,
            row,
            row,
        ],
        *in_hbm(*fetched),
        *near_args,
        spaces=[pltpu.HBM] * len(fetched) + [pltpu.VMEM] * len(near_args),
        scratch=[pltpu.VMEM(a.shape, a.dtype) for a in (lam_from, lam_to, outage)]
        + [pltpu.VMEM((1, buses), F32)] * 4
        + [pltpu.SemaphoreType.DMA((len(fetched),))],
    )
    got1 = trade_near(pick1)
    z1, p, c = call(near_first_kernel, [half, branch, branch], pick1, got1, edge_table, p, c)
    send2, z2, delta, flow = call(
        far_first_kernel,
        [tall, half, branch, branch],
        pick2,
        got2,
        edge_table,
        p,
        c,
        gain,
        count_edge,
    )
    nets, boths1, boths2 = [], [], []
    for index in range(1, ROUNDS):
        first = index == 1
        got2 = trade_far(send2)
        net, x, p, c, send1 = call(
            beside_kernel,
            [bus, bus, branch, branch, tall if first else half],
            flow,
            delta,
            x,
            count_inner,
            inner_table,
            edge_table,
            *([count_edge] if first else []),
        )
        nets.append(net)
        got1 = trade_near(send1)
        outs = [half, half, branch, branch]
        if first:
            both1, z1, p, c, degree1 = call(
                near_second_kernel, outs + [counts], send1, got1, z1, edge_table, p, c
            )
        else:
            both1, z1, p, c = call(
                near_kernel, outs, send1, got1, z1, degree1, edge_table, p, c
            )
        outs = [half, half, branch, half]
        if index < ROUNDS - 1:
            outs = outs + [branch]
        if first:
            both2, z2, flow, send2, *deltas, degree2 = call(
                far_second_kernel, outs + [counts], send2, got2, z2, edge_table, p, c, gain
            )
        else:
            both2, z2, flow, send2, *deltas = call(
                far_kernel, outs, send2, got2, z2, degree2, edge_table, p, c, gain
            )
        delta = deltas[0] if deltas else None
        boths1.append(both1)
        boths2.append(both2)
    got2 = trade_far(send2)
    (send1,) = call(send_last_kernel, [half], flow, edge_table)
    got1 = trade_near(send1)
    net, x, dual, sums = call(
        beside_last_kernel,
        [bus, bus, bus, row],
        flow,
        x,
        count_inner,
        inner_table,
        own,
        gen_dual,
        rows,
        dual_sum,
        *boths1,
        *boths2,
        *nets,
    )
    both, sums = call(total_kernel, [edge, row], send1, send2, got1, got2, own, sums)
    parts = [sums]
    for shift in range(1, cont_size):
        parts.append(
            lax.ppermute(sums, "cont", [(i, (i + shift) % cont_size) for i in range(cont_size)])
        )

    theta, part_gen = call(
        field_kernel,
        [bus, bus],
        both,
        z1,
        z2,
        degree1,
        degree2,
        own,
        x,
        net,
        dual,
        rows,
    )

    def finish(*refs):
        end_kernel(float(conts * cont_size), *refs)

    generation, base = call(finish, [bus, ((1, buses), F32)], *parts, rows, part_gen)
    return theta, generation, base.reshape(buses)


def solution(mesh):
    placed = (
        P("cont", "net"),
        P("cont", "net"),
        P("cont", "net"),
        P("cont", "net"),
        P("net"),
        P("cont", "net"),
        P("net"),
        P("net"),
        P("net"),
        P("net"),
        P("net"),
        P("net"),
        P("net"),
    )
    return jax.shard_map(
        local,
        mesh=mesh,
        in_specs=placed,
        out_specs=(P("cont", "net"), P("cont", "net"), P("net")),
        check_vma=False,
    )
```

time: 33.5 us -> 37.2 us (1.11)
  waiting for transfers between devices: 7.61 us -> 9.56 us
  Pallas kernels: 8.07 us -> 9.85 us
    ppermute x10, waiting for transfers between devices: 6.23 us -> 8.18 us  [the longest x5 8.17 us: trade_far(): return lax.ppermute(value, axes, swap2)]
    pallas_call x13 -> x18, Pallas kernels: 8.07 us -> 9.85 us  [call(): pl.pallas_call(kernel, out_shape=shapes, in_specs=[pl.BlockSpec(memory_sp...]
  transfers between devices with their start and end apart: 13 -> 13, of which waited for: 6 -> 6; matrix products, arithmetic and copies ran while one was open for 0% -> 0% of each run, Pallas kernels for 12% -> 6%
where the time goes in v3:
time: 37.2 us; the launch traced here: 37 us
  starting transfers between devices  16.9 us (45%)
  Pallas kernels  9.85 us (26%)
  waiting for transfers between devices  9.56 us (26%)
  between operations  0.73 us (2%)
    ppermute x5, starting transfers between devices, trade_far(): return lax.ppermute(value, axes, swap2)  10.6 us
    pallas_call x18, Pallas kernels, call(): pl.pallas_call(kernel, out_shape=shapes, in_specs=[pl.BlockSpec(memory_sp...  9.85 us
    ppermute x5, waiting for transfers between devices, trade_far(): return lax.ppermute(value, axes, swap2)  8.17 us
    ppermute x3, starting transfers between devices, local(): lax.ppermute(sums, 'cont', [(i, (i + shift) % cont_size) for i in range(c...  5 us
    ppermute x3, waiting for transfers between devices, local(): lax.ppermute(sums, 'cont', [(i, (i + shift) % cont_size) for i in range(c...  1.38 us
    ppermute x5, starting transfers between devices, trade_near(): return lax.ppermute(value, axes, swap1)  1.24 us
  transfers between devices with their start and end apart: 13, of which 6 were waited for; matrix products, arithmetic and copies ran while one was open for 0% of the time, Pallas kernels for 6%

profile of v3, /device:TPU:0, one launch (start us, length us, event | category | flops | bytes accessed | tf_op | source)
XLA Modules:
  0.0 37.0 jit_solution(4958125784054090888)
XLA Ops:
  0.6 1.1 %shard_map.148 = (s32[1,128]{1,0:T(1,128)S(1)}, f32[64,512]{1,0:T(8,128)S(1)}, s32[640]{0:T(1024)S(1)}, s32[640]{0:T(1024)S(1)}, f32[640]{0:T(1024)S(1)}, /*inde...) custom-call(s32[1,128]{1,0:T(1,128)} %bitcast.10, f32[64,512]{1,0:T(8,128)} %refs_1_.1, s32[640]{0:T(1024)} %refs_2_.1, ...), custom_call_target="tpu_custom_call" | custom-call | flops 83886080 | bytes 139264 | tf_op jit(solution)/shard_map/pallas_call | solution.py:390
  1.8 2.2 %shard_map.149 = (f32[64,512]{1,0:T(8,128)S(1)}, f32[64,128]{1,0:T(8,128)S(1)}, bf16[640,256]{1,0:T(8,128)(2,1)S(1)}, bf16[640,512]{1,0:T(8,128)(2,1)S(1)}, f32[...) custom-call(f32[64,640]{1,0:T(8,128)} %lam_f_hbm.1, ...), custom_call_target="tpu_custom_call" | custom-call | flops 83886080 | bytes 1032192 | tf_op jit(solution)/shard_map/pallas_call | solution.py:390
  4.0 0.5 %collective-permute-start.1 = (f32[64,128]{1,0:T(8,128)S(1)}, f32[64,128]{1,0:T(8,128)S(1)}, u32[]{:S(2)}, u32[]{:S(2)}) collective-permute-start(f32[64,128]{1,0:T(8,128)S(1)} %get-tuple-element.90.pick_ref), channel_id=1, source_target_pairs={{0,1},{1,0},{2,3},{3,2},{4,5},{5,4},{6,7},{7,6},{8,9},{9,8},{10,11... | collective-permute-start | bytes 98312 | tf_op jit(solution)/shard_map/ppermute | solution.py:443
  4.5 2.6 %collective-permute-start = (f32[64,128]{1,0:T(8,128)S(1)}, f32[64,128]{1,0:T(8,128)S(1)}, u32[]{:S(2)}, u32[]{:S(2)}) collective-permute-start(f32[64,128]{1,0:T(8,128)S(1)} %get-tuple-element.82.pick_ref), channel_id=1, source_target_pairs={{0,8},{1,2},{2,1},{3,4},{4,3},{5,6},{6,5},{7,15},{8,0},{9,10},{10,... | collective-permute-start | bytes 98312 | tf_op jit(solution)/shard_map/ppermute | solution.py:446
  7.3 1.7 %collective-permute-done.got_ref = f32[64,128]{1,0:T(8,128)S(1)} collective-permute-done((f32[64,128]{1,0:T(8,128)S(1)}, f32[64,128]{1,0:T(8,128)S(1)}, u32[]{:S(2)}, u32[]{:S(2)}) %collective-permute-start) | collective-permute-done | bytes 32800 | tf_op jit(solution)/shard_map/ppermute | solution.py:446
  9.4 0.6 %shard_map.152 = (f32[64,512]{1,0:T(8,128)S(1)}, f32[64,512]{1,0:T(8,128)S(1)}, f32[64,640]{1,0:T(8,128)S(1)}, f32[64,640]{1,0:T(8,128)S(1)}, f32[72,128]{1,0:T(8,128)S(1)}) custom-call(f32[64,640]{1,0:T(8,128)S(1)} %get-tuple-element.99.flow_ref, f32[64,640]{1,0:T(8,128)S(1)} %get-tuple-element.100.delta_ref, f32[64,512]{1,0:T(8,128)S(1)} %get-tuple-element.101.x_ref, ...), custom_call_target="tpu_custom_call" | custom-call | flops 83886080 | bytes 1466368 | tf_op jit(solution)/shard_map/pallas_call | solution.py:390
  10.1 2.0 %collective-permute-start.2 = (f32[72,128]{1,0:T(8,128)S(1)}, f32[72,128]{1,0:T(8,128)S(1)}, u32[]{:S(2)}, u32[]{:S(2)}) collective-permute-start(f32[72,128]{1,0:T(8,128)S(1)} %get-tuple-element.97.send_ref), channel_id=1, source_target_pairs={{0,8},{1,2},{2,1},{3,4},{4,3},{5,6},{6,5},{7,15},{8,0},{9,10},{10,... | collective-permute-start | bytes 110600 | tf_op jit(solution)/shard_map/ppermute | solution.py:446
  12.4 1.7 %collective-permute-done.2.got_ref = f32[72,128]{1,0:T(8,128)S(1)} collective-permute-done((f32[72,128]{1,0:T(8,128)S(1)}, f32[72,128]{1,0:T(8,128)S(1)}, u32[]{:S(2)}, u32[]{:S(2)}) %collective-permute-start.2) | collective-permute-done | bytes 36896 | tf_op jit(solution)/shard_map/ppermute | solution.py:446
  14.5 0.6 %shard_map.155 = (f32[64,512]{1,0:T(8,128)S(1)}, f32[64,512]{1,0:T(8,128)S(1)}, f32[64,640]{1,0:T(8,128)S(1)}, f32[64,640]{1,0:T(8,128)S(1)}, f32[64,128]{1,0:T(8,128)S(1)}) custom-call(f32[64,640]{1,0:T(8,128)S(1)} %get-tuple-element.113.flow_ref, f32[64,640]{1,0:T(8,128)S(1)} %get-tuple-element.114.delta_ref, f32[64,512]{1,0:T(8,128)S(1)} %get-tuple-element.115.x_ref, ...), custom_call_target="tpu_custom_call" | custom-call | flops 83886080 | bytes 1458176 | tf_op jit(solution)/shard_map/pallas_call | solution.py:390
  15.2 2.0 %collective-permute-start.4 = (f32[64,128]{1,0:T(8,128)S(1)}, f32[64,128]{1,0:T(8,128)S(1)}, u32[]{:S(2)}, u32[]{:S(2)}) collective-permute-start(f32[64,128]{1,0:T(8,128)S(1)} %get-tuple-element.110.send_ref), channel_id=1, source_target_pairs={{0,8},{1,2},{2,1},{3,4},{4,3},{5,6},{6,5},{7,15},{8,0},{9,10},{10,... | collective-permute-start | bytes 98312 | tf_op jit(solution)/shard_map/ppermute | solution.py:446
  17.5 1.7 %collective-permute-done.4.got_ref = f32[64,128]{1,0:T(8,128)S(1)} collective-permute-done((f32[64,128]{1,0:T(8,128)S(1)}, f32[64,128]{1,0:T(8,128)S(1)}, u32[]{:S(2)}, u32[]{:S(2)}) %collective-permute-start.4) | collective-permute-done | bytes 32800 | tf_op jit(solution)/shard_map/ppermute | solution.py:446
  19.1 0.4 %shard_map.157 = (f32[64,128]{1,0:T(8,128)S(1)}, f32[64,128]{1,0:T(8,128)S(1)}, f32[64,640]{1,0:T(8,128)S(1)}, f32[64,128]{1,0:T(8,128)S(1)}, f32[64,640]{1,0:T(8,128)S(1)}) custom-call(f32[64,128]{1,0:T(8,128)S(1)} %get-tuple-element.110.send_ref, f32[64,128]{1,0:T(8,128)S(1)} %collective-permute-done.4.got_ref, f32[64,128]{1,0:T(8,128)S(1)} %get-tuple-element.111.z_ref, ...), custom_call_target="tpu_custom_call" | custom-call | flops 83886080 | bytes 921600 | tf_op jit(solution)/shard_map/pallas_call | solution.py:390
  19.5 0.6 %shard_map.158 = (f32[64,512]{1,0:T(8,128)S(1)}, f32[64,512]{1,0:T(8,128)S(1)}, f32[64,640]{1,0:T(8,128)S(1)}, f32[64,640]{1,0:T(8,128)S(1)}, f32[64,128]{1,0:T(8,128)S(1)}) custom-call(f32[64,640]{1,0:T(8,128)S(1)} %get-tuple-element.125.flow_ref, f32[64,640]{1,0:T(8,128)S(1)} %get-tuple-element.126.delta_ref, f32[64,512]{1,0:T(8,128)S(1)} %get-tuple-element.127.x_ref, ...), custom_call_target="tpu_custom_call" | custom-call | flops 83886080 | bytes 1458176 | tf_op jit(solution)/shard_map/pallas_call | solution.py:390
  20.3 2.0 %collective-permute-start.6 = (f32[64,128]{1,0:T(8,128)S(1)}, f32[64,128]{1,0:T(8,128)S(1)}, u32[]{:S(2)}, u32[]{:S(2)}) collective-permute-start(f32[64,128]{1,0:T(8,128)S(1)} %get-tuple-element.123.send_ref), channel_id=1, source_target_pairs={{0,8},{1,2},{2,1},{3,4},{4,3},{5,6},{6,5},{7,15},{8,0},{9,10},{10,... | collective-permute-start | bytes 98312 | tf_op jit(solution)/shard_map/ppermute | solution.py:446
  22.5 1.7 %collective-permute-done.6.got_ref = f32[64,128]{1,0:T(8,128)S(1)} collective-permute-done((f32[64,128]{1,0:T(8,128)S(1)}, f32[64,128]{1,0:T(8,128)S(1)}, u32[]{:S(2)}, u32[]{:S(2)}) %collective-permute-start.6) | collective-permute-done | bytes 32800 | tf_op jit(solution)/shard_map/ppermute | solution.py:446
  24.9 2.0 %collective-permute-start.9 = (f32[64,128]{1,0:T(8,128)S(1)}, f32[64,128]{1,0:T(8,128)S(1)}, u32[]{:S(2)}, u32[]{:S(2)}) collective-permute-start(f32[64,128]{1,0:T(8,128)S(1)} %get-tuple-element.135.send2_ref), channel_id=1, source_target_pairs={{0,8},{1,2},{2,1},{3,4},{4,3},{5,6},{6,5},{7,15},{8,0},{9,10},{10,... | collective-permute-start | bytes 98312 | tf_op jit(solution)/shard_map/ppermute | solution.py:446
  26.9 0.5 %shard_map.162 = (f32[64,512]{1,0:T(8,128)S(1)}, f32[64,512]{1,0:T(8,128)S(1)}, f32[64,512]{1,0:T(8,128)S(1)}, f32[8,512]{1,0:T(8,128)S(1)}) custom-call(f32[64,640]{1,0:T(8,128)S(1)} %get-tuple-element.134.flow_ref, f32[64,512]{1,0:T(8,128)S(1)} %get-tuple-element.136.x_ref, f32[8,512]{1,0:T(8,128)S(1)} %get-tuple-element.102.count_ref, ...), custom_call_target="tpu_custom_call" | custom-call | flops 83886080 | bytes 1982464 | tf_op jit(solution)/shard_map/pallas_call | solution.py:390
  27.4 1.4 %collective-permute-done.9.got2_ref = f32[64,128]{1,0:T(8,128)S(1)} collective-permute-done((f32[64,128]{1,0:T(8,128)S(1)}, f32[64,128]{1,0:T(8,128)S(1)}, u32[]{:S(2)}, u32[]{:S(2)}) %collective-permute-start.9) | collective-permute-done | bytes 32800 | tf_op jit(solution)/shard_map/ppermute | solution.py:446
  29.0 2.0 %collective-permute-start.10 = (f32[8,512]{1,0:T(8,128)S(1)}, f32[8,512]{1,0:T(8,128)S(1)}, u32[]{:S(2)}, u32[]{:S(2)}) collective-permute-start(f32[8,512]{1,0:T(8,128)S(1)} %get-tuple-element.157.refs_0_), channel_id=1, source_target_pairs={{0,8},{8,16},{16,24},{24,0},{1,9},{9,17},{17,25},{25,1},{2,10},{10... | collective-permute-start | bytes 49160 | tf_op jit(solution)/shard_map/ppermute | solution.py:590
  31.1 1.5 %collective-permute-start.11 = (f32[8,512]{1,0:T(8,128)S(1)}, f32[8,512]{1,0:T(8,128)S(1)}, u32[]{:S(2)}, u32[]{:S(2)}) collective-permute-start(f32[8,512]{1,0:T(8,128)S(1)} %get-tuple-element.157.refs_0_), channel_id=1, source_target_pairs={{0,16},{8,24},{16,0},{24,8},{1,17},{9,25},{17,1},{25,9},{2,18},{10... | collective-permute-start | bytes 49160 | tf_op jit(solution)/shard_map/ppermute | solution.py:590
  32.6 1.4 %collective-permute-start.12 = (f32[8,512]{1,0:T(8,128)S(1)}, f32[8,512]{1,0:T(8,128)S(1)}, u32[]{:S(2)}, u32[]{:S(2)}) collective-permute-start(f32[8,512]{1,0:T(8,128)S(1)} %get-tuple-element.157.refs_0_), channel_id=1, source_target_pairs={{0,24},{8,0},{16,8},{24,16},{1,25},{9,1},{17,9},{25,17},{2,26},{10... | collective-permute-start | bytes 49160 | tf_op jit(solution)/shard_map/ppermute | solution.py:590
  34.0 0.9 %shard_map.164 = (f32[64,512]{1,0:T(8,128)}, f32[64,512]{1,0:T(8,128)S(1)}) custom-call(f32[64,256]{1,0:T(8,128)S(1)} %get-tuple-element.150.both_ref, f32[64,128]{1,0:T(8,128)S(1)} %get-tuple-element.151.z1_ref, f32[64,128]{1,0:T(8,128)S(1)} %get-tuple-element.152.z2_ref, f32[8,128]{1,0:T(8,128)S(1)} %get-tuple-element.118.degree_ref.degree1_ref, ...), custom_call_target="tpu_custom_call" | custom-call | flops 83886080 | bytes 811008 | tf_op jit(solution)/shard_map/pallas_call | solution.py:390
  34.9 1.4 %collective-permute-done.12.refs_3_ = f32[8,512]{1,0:T(8,128)S(1)} collective-permute-done((f32[8,512]{1,0:T(8,128)S(1)}, f32[8,512]{1,0:T(8,128)S(1)}, u32[]{:S(2)}, u32[]{:S(2)}) %collective-permute-start.12) | collective-permute-done | bytes 16416 | tf_op jit(solution)/shard_map/ppermute | solution.py:590
  36.3 0.7 %shard_map.165 = (f32[64,512]{1,0:T(8,128)}, f32[1,512]{1,0:T(1,128)}) custom-call(f32[8,512]{1,0:T(8,128)S(1)} %get-tuple-element.157.refs_0_, f32[8,512]{1,0:T(8,128)S(1)} %collective-permute-done.10.refs_1_, f32[8,512]{1,0:T(8,128)S(1)} %collective-permute-done.11.refs_2_, f32[8,512]{1,0:T(8,128)S(1)} %collective-permute-done.12.refs_3_, ...), custom_call_target="tpu_custom_call" | custom-call | flops 83886080 | bytes 212992 | tf_op jit(solution)/shard_map/pallas_call | solution.py:390
  (23 shorter events, 3.0 us)
Async XLA Ops:
  4.0 3.1 %collective-permute-start.1 = (f32[64,128]{1,0:T(8,128)S(1)}, f32[64,128]{1,0:T(8,128)S(1)}, u32[]{:S(2)}, u32[]{:S(2)}) collective-permute-start(f32[64,128]{1,0:T(8,128)S(1)} %get-tuple-element.90.pick_ref), channel_id=1, source_target_pairs={{0,1},{1,0},{2,3},{3,2},{4,5},{5,4},{6,7},{7,6},{8,9},{9,8},{10,11... | collective-permute-start | bytes 98312 | tf_op jit(solution)/shard_map/ppermute | solution.py:443
  4.5 4.5 %collective-permute-start = (f32[64,128]{1,0:T(8,128)S(1)}, f32[64,128]{1,0:T(8,128)S(1)}, u32[]{:S(2)}, u32[]{:S(2)}) collective-permute-start(f32[64,128]{1,0:T(8,128)S(1)} %get-tuple-element.82.pick_ref), channel_id=1, source_target_pairs={{0,8},{1,2},{2,1},{3,4},{4,3},{5,6},{6,5},{7,15},{8,0},{9,10},{10,... | collective-permute-start | bytes 98312 | tf_op jit(solution)/shard_map/ppermute | solution.py:446
  9.9 2.2 %collective-permute-start.3 = (f32[72,128]{1,0:T(8,128)S(1)}, f32[72,128]{1,0:T(8,128)S(1)}, u32[]{:S(2)}, u32[]{:S(2)}) collective-permute-start(f32[72,128]{1,0:T(8,128)S(1)} %get-tuple-element.104.send_ref), channel_id=1, source_target_pairs={{0,1},{1,0},{2,3},{3,2},{4,5},{5,4},{6,7},{7,6},{8,9},{9,8},{10,11... | collective-permute-start | bytes 110600 | tf_op jit(solution)/shard_map/ppermute | solution.py:443
  10.1 4.0 %collective-permute-start.2 = (f32[72,128]{1,0:T(8,128)S(1)}, f32[72,128]{1,0:T(8,128)S(1)}, u32[]{:S(2)}, u32[]{:S(2)}) collective-permute-start(f32[72,128]{1,0:T(8,128)S(1)} %get-tuple-element.97.send_ref), channel_id=1, source_target_pairs={{0,8},{1,2},{2,1},{3,4},{4,3},{5,6},{6,5},{7,15},{8,0},{9,10},{10,... | collective-permute-start | bytes 110600 | tf_op jit(solution)/shard_map/ppermute | solution.py:446
  15.0 2.2 %collective-permute-start.5 = (f32[64,128]{1,0:T(8,128)S(1)}, f32[64,128]{1,0:T(8,128)S(1)}, u32[]{:S(2)}, u32[]{:S(2)}) collective-permute-start(f32[64,128]{1,0:T(8,128)S(1)} %get-tuple-element.116.send_ref), channel_id=1, source_target_pairs={{0,1},{1,0},{2,3},{3,2},{4,5},{5,4},{6,7},{7,6},{8,9},{9,8},{10,11... | collective-permute-start | bytes 98312 | tf_op jit(solution)/shard_map/ppermute | solution.py:443
  15.2 3.9 %collective-permute-start.4 = (f32[64,128]{1,0:T(8,128)S(1)}, f32[64,128]{1,0:T(8,128)S(1)}, u32[]{:S(2)}, u32[]{:S(2)}) collective-permute-start(f32[64,128]{1,0:T(8,128)S(1)} %get-tuple-element.110.send_ref), channel_id=1, source_target_pairs={{0,8},{1,2},{2,1},{3,4},{4,3},{5,6},{6,5},{7,15},{8,0},{9,10},{10,... | collective-permute-start | bytes 98312 | tf_op jit(solution)/shard_map/ppermute | solution.py:446
  20.1 2.2 %collective-permute-start.7 = (f32[64,128]{1,0:T(8,128)S(1)}, f32[64,128]{1,0:T(8,128)S(1)}, u32[]{:S(2)}, u32[]{:S(2)}) collective-permute-start(f32[64,128]{1,0:T(8,128)S(1)} %get-tuple-element.128.send_ref), channel_id=1, source_target_pairs={{0,1},{1,0},{2,3},{3,2},{4,5},{5,4},{6,7},{7,6},{8,9},{9,8},{10,11... | collective-permute-start | bytes 98312 | tf_op jit(solution)/shard_map/ppermute | solution.py:443
  20.3 3.9 %collective-permute-start.6 = (f32[64,128]{1,0:T(8,128)S(1)}, f32[64,128]{1,0:T(8,128)S(1)}, u32[]{:S(2)}, u32[]{:S(2)}) collective-permute-start(f32[64,128]{1,0:T(8,128)S(1)} %get-tuple-element.123.send_ref), channel_id=1, source_target_pairs={{0,8},{1,2},{2,1},{3,4},{4,3},{5,6},{6,5},{7,15},{8,0},{9,10},{10,... | collective-permute-start | bytes 98312 | tf_op jit(solution)/shard_map/ppermute | solution.py:446
  24.7 2.7 %collective-permute-start.8 = (f32[64,128]{1,0:T(8,128)S(1)}, f32[64,128]{1,0:T(8,128)S(1)}, u32[]{:S(2)}, u32[]{:S(2)}) collective-permute-start(f32[64,128]{1,0:T(8,128)S(1)} %shard_map.161.send1_ref), channel_id=1, source_target_pairs={{0,1},{1,0},{2,3},{3,2},{4,5},{5,4},{6,7},{7,6},{8,9},{9,8},{10,11... | collective-permute-start | bytes 98312 | tf_op jit(solution)/shard_map/ppermute | solution.py:443
  24.9 3.9 %collective-permute-start.9 = (f32[64,128]{1,0:T(8,128)S(1)}, f32[64,128]{1,0:T(8,128)S(1)}, u32[]{:S(2)}, u32[]{:S(2)}) collective-permute-start(f32[64,128]{1,0:T(8,128)S(1)} %get-tuple-element.135.send2_ref), channel_id=1, source_target_pairs={{0,8},{1,2},{2,1},{3,4},{4,3},{5,6},{6,5},{7,15},{8,0},{9,10},{10,... | collective-permute-start | bytes 98312 | tf_op jit(solution)/shard_map/ppermute | solution.py:446
  29.0 5.9 %collective-permute-start.10 = (f32[8,512]{1,0:T(8,128)S(1)}, f32[8,512]{1,0:T(8,128)S(1)}, u32[]{:S(2)}, u32[]{:S(2)}) collective-permute-start(f32[8,512]{1,0:T(8,128)S(1)} %get-tuple-element.157.refs_0_), channel_id=1, source_target_pairs={{0,8},{8,16},{16,24},{24,0},{1,9},{9,17},{17,25},{25,1},{2,10},{10... | collective-permute-start | bytes 49160 | tf_op jit(solution)/shard_map/ppermute | solution.py:590
  31.1 3.9 %collective-permute-start.11 = (f32[8,512]{1,0:T(8,128)S(1)}, f32[8,512]{1,0:T(8,128)S(1)}, u32[]{:S(2)}, u32[]{:S(2)}) collective-permute-start(f32[8,512]{1,0:T(8,128)S(1)} %get-tuple-element.157.refs_0_), channel_id=1, source_target_pairs={{0,16},{8,24},{16,0},{24,8},{1,17},{9,25},{17,1},{25,9},{2,18},{10... | collective-permute-start | bytes 49160 | tf_op jit(solution)/shard_map/ppermute | solution.py:590
  32.6 3.7 %collective-permute-start.12 = (f32[8,512]{1,0:T(8,128)S(1)}, f32[8,512]{1,0:T(8,128)S(1)}, u32[]{:S(2)}, u32[]{:S(2)}) collective-permute-start(f32[8,512]{1,0:T(8,128)S(1)} %get-tuple-element.157.refs_0_), channel_id=1, source_target_pairs={{0,24},{8,0},{16,8},{24,16},{1,25},{9,1},{17,9},{25,17},{2,26},{10... | collective-permute-start | bytes 49160 | tf_op jit(solution)/shard_map/ppermute | solution.py:590

commit v4 on v3

--- a/solution.py
+++ b/solution.py
@@ -155,19 +155,10 @@
         rows_ref[2 * index : 2 * index + 2, :] = jnp.broadcast_to(ref[...], (2, buses))
 
 
-def near_first_kernel(pick_ref, got_ref, edge_ref, p_ref, c_ref, z_ref, p_out_ref, c_out_ref):
-    slots = pick_ref.shape[1]
-    even = lax.axis_index("net") % 2 == 0
-    z = jnp.where(even, got_ref[...], pick_ref[...])
-    z_ref[...] = z
-    moved = times_t(z, edge_ref[:, :slots])
-    p_out_ref[...] = p_ref[...] + moved
-    c_out_ref[...] = c_ref[...] + moved
-
-
-def far_first_kernel(
-    pick_ref,
-    got_ref,
+def first_kernel(
+    far_ref,
+    got1_ref,
+    pick1_ref,
     edge_ref,
     p_ref,
     c_ref,
@@ -178,108 +169,111 @@
     delta_ref,
     flow_ref,
 ):
-    slots = pick_ref.shape[1]
+    slots = pick1_ref.shape[1]
     conts = p_ref.shape[0]
-    table = edge_ref[:, slots:]
-    even = lax.axis_index("net") % 2 == 0
-    z = jnp.where(even, pick_ref[...], got_ref[...])
+    z = jnp.concatenate([pick1_ref[...] + got1_ref[...], far_ref[...]], axis=1)
     z_ref[...] = z
-    moved = times_t(z, table)
+    moved = times_t(z, edge_ref[...])
     delta_ref[...] = p_ref[...] + moved
     flow = gain_ref[...] * (c_ref[...] + moved)
     flow_ref[...] = flow
-    send_ref[:conts, :] = times(flow, table)
+    send_ref[:conts, :] = times(flow, edge_ref[:, slots:])
     send_ref[conts:, :] = count_ref[:, slots:]
 
 
-def traded(send_ref, got_ref, z_ref, both_ref, z_out_ref, degree):
-    conts = z_ref.shape[0]
-    both = send_ref[:conts, :] + got_ref[:conts, :]
+def both_ends(far_ref, got1_ref, send1_ref, rows):
+    return jnp.concatenate(
+        [send1_ref[rows, :] + got1_ref[rows, :], far_ref[rows, :]], axis=1
+    )
+
+
+def round_step(
+    far_ref, got1_ref, send1_ref, z_ref, degree, edge_ref, p_ref, c_ref, gain_ref, outs
+):
+    both_ref, z_out_ref, flow_ref, out_ref, *deltas = outs
+    slots = out_ref.shape[1]
+    both = both_ends(far_ref, got1_ref, send1_ref, slice(0, z_ref.shape[0]))
     both_ref[...] = both
     z = (degree * z_ref[...] - both) / (degree + 1.0)
     z_out_ref[...] = z
-    return z
-
-
-def near(send_ref, got_ref, z_ref, degree, edge_ref, p_ref, c_ref, outs):
-    both_ref, z_out_ref, p_out_ref, c_out_ref = outs
-    slots = z_ref.shape[1]
-    z = traded(send_ref, got_ref, z_ref, both_ref, z_out_ref, degree)
-    moved = times_t(z, edge_ref[:, :slots])
-    p_out_ref[...] = p_ref[...] + moved
-    c_out_ref[...] = c_ref[...] + 2.0 * moved
-
-
-def near_second_kernel(send_ref, got_ref, z_ref, edge_ref, p_ref, c_ref, *outs):
-    conts = z_ref.shape[0]
-    *outs, degree_ref = outs
-    degree = send_ref[conts:, :] + got_ref[conts:, :]
-    degree_ref[...] = degree
-    near(send_ref, got_ref, z_ref, degree[:1, :], edge_ref, p_ref, c_ref, outs)
-
-
-def near_kernel(send_ref, got_ref, z_ref, degree_ref, edge_ref, p_ref, c_ref, *outs):
-    near(send_ref, got_ref, z_ref, degree_ref[:1, :], edge_ref, p_ref, c_ref, outs)
-
-
-def far(send_ref, got_ref, z_ref, degree, edge_ref, p_ref, c_ref, gain_ref, outs):
-    both_ref, z_out_ref, flow_ref, out_ref, *deltas = outs
-    slots = z_ref.shape[1]
-    table = edge_ref[:, slots:]
-    z = traded(send_ref, got_ref, z_ref, both_ref, z_out_ref, degree)
-    moved = times_t(z, table)
+    moved = times_t(z, edge_ref[...])
     for delta_ref in deltas:
         delta_ref[...] = p_ref[...] + moved
     flow = gain_ref[...] * (c_ref[...] + 2.0 * moved)
     flow_ref[...] = flow
-    out_ref[...] = times(flow, table)
-
-
-def far_second_kernel(send_ref, got_ref, z_ref, edge_ref, p_ref, c_ref, gain_ref, *outs):
-    conts = z_ref.shape[0]
+    out_ref[...] = times(flow, edge_ref[:, slots:])
+
+
+def second_kernel(
+    far_ref, got1_ref, send1_ref, z_ref, edge_ref, p_ref, c_ref, gain_ref, *outs
+):
     *outs, degree_ref = outs
-    degree = send_ref[conts:, :] + got_ref[conts:, :]
+    rows = slice(z_ref.shape[0], send1_ref.shape[0])
+    degree = both_ends(far_ref, got1_ref, send1_ref, rows)
     degree_ref[...] = degree
-    far(send_ref, got_ref, z_ref, degree[:1, :], edge_ref, p_ref, c_ref, gain_ref, outs)
-
-
-def far_kernel(send_ref, got_ref, z_ref, degree_ref, edge_ref, p_ref, c_ref, gain_ref, *outs):
-    far(send_ref, got_ref, z_ref, degree_ref[:1, :], edge_ref, p_ref, c_ref, gain_ref, outs)
-
-
-def inner_step(flow_ref, x_ref, count_ref, inner_ref, edge_ref, send_ref):
-    flow = flow_ref[...]
-    conts = flow.shape[0]
-    slots = send_ref.shape[1]
-    send_ref[:conts, :] = times(flow, edge_ref[:, :slots])
-    net = times(flow, inner_ref[...])
+    round_step(
+        far_ref,
+        got1_ref,
+        send1_ref,
+        z_ref,
+        degree[:1, :],
+        edge_ref,
+        p_ref,
+        c_ref,
+        gain_ref,
+        outs,
+    )
+
+
+def next_kernel(
+    far_ref,
+    got1_ref,
+    send1_ref,
+    z_ref,
+    degree_ref,
+    edge_ref,
+    p_ref,
+    c_ref,
+    gain_ref,
+    *outs,
+):
+    round_step(
+        far_ref,
+        got1_ref,
+        send1_ref,
+        z_ref,
+        degree_ref[:1, :],
+        edge_ref,
+        p_ref,
+        c_ref,
+        gain_ref,
+        outs,
+    )
+
+
+def send_kernel(flow_ref, edge_ref, *refs):
+    *counts, send_ref = refs
+    conts, slots = flow_ref.shape[0], send_ref.shape[1]
+    send_ref[:conts, :] = times(flow_ref[...], edge_ref[:, :slots])
+    for ref in counts:
+        send_ref[conts:, :] = ref[:, :slots]
+
+
+def inner_step(flow_ref, x_ref, count_ref, inner_ref):
+    net = times(flow_ref[...], inner_ref[...])
     count = count_ref[:1, :]
     return net, (count * x_ref[...] - net) / (count + 1.0)
 
 
 def beside_kernel(
-    flow_ref,
-    delta_ref,
-    x_ref,
-    count_ref,
-    inner_ref,
-    edge_ref,
-    *refs,
-):
-    *counts, net_ref, x_out_ref, p_ref, c_ref, send_ref = refs
-    conts, slots = flow_ref.shape[0], send_ref.shape[1]
-    for ref in counts:
-        send_ref[conts:, :] = ref[:, :slots]
-    net, x = inner_step(flow_ref, x_ref, count_ref, inner_ref, edge_ref, send_ref)
+    flow_ref, delta_ref, x_ref, count_ref, inner_ref, net_ref, x_out_ref, p_ref, c_ref
+):
+    net, x = inner_step(flow_ref, x_ref, count_ref, inner_ref)
     net_ref[...] = net
     x_out_ref[...] = x
     p = times_t(x, inner_ref[...])
     p_ref[...] = p
     c_ref[...] = 2.0 * (p + flow_ref[...]) - delta_ref[...]
-
-
-def send_last_kernel(flow_ref, edge_ref, send_ref):
-    send_ref[...] = times(flow_ref[...], edge_ref[:, : send_ref.shape[1]])
 
 
 def beside_last_kernel(
@@ -294,24 +288,17 @@
     *refs,
 ):
     *refs, net_ref, x_out_ref, dual_out_ref, sums_ref = refs
-    rounds = len(refs) // 3
-    net = times(flow_ref[...], inner_ref[...])
-    count = count_ref[:1, :]
+    rounds = len(refs) // 2
+    net, x = inner_step(flow_ref, x_ref, count_ref, inner_ref)
     net_ref[...] = net
-    x_out_ref[...] = (count * x_ref[...] - net) / (count + 1.0)
+    x_out_ref[...] = x
     conts = net.shape[0]
-    edge = jnp.concatenate(
-        [
-            jnp.concatenate([refs[index][...], refs[rounds + index][...]], axis=1)
-            for index in range(rounds)
-        ],
-        axis=0,
-    )
+    edge = jnp.concatenate([ref[...] for ref in refs[:rounds]], axis=0)
     spread = times_t(edge, own_ref[...])
     part = 1.0 / (rows_ref[4:5, :] + PENALTY + BALANCE)
     dual = dual_ref[...]
     sums_ref[0:1, :] = dsum_ref[:1, :]
-    for index, ref in enumerate(refs[2 * rounds :]):
+    for index, ref in enumerate(refs[rounds:]):
         whole = ref[...] + spread[index * conts : (index + 1) * conts]
         sums_ref[index + 1 : index + 2, :] = jnp.sum(whole, axis=0, keepdims=True)
         dual = dual + part * (BALANCE * whole - dual)
@@ -323,11 +310,9 @@
 
 
 def total_kernel(
-    send1_ref, send2_ref, got1_ref, got2_ref, own_ref, sums_in_ref, both_ref, sums_ref
-):
-    both = jnp.concatenate(
-        [send1_ref[...] + got1_ref[...], send2_ref[...] + got2_ref[...]], axis=1
-    )
+    far_ref, got1_ref, send1_ref, own_ref, sums_in_ref, both_ref, sums_ref
+):
+    both = both_ends(far_ref, got1_ref, send1_ref, slice(0, send1_ref.shape[0]))
     both_ref[...] = both
     row = jnp.broadcast_to(jnp.sum(both, axis=0, keepdims=True), (8, both.shape[1]))
     sums_ref[...] = sums_in_ref[...]
@@ -336,24 +321,12 @@
 
 
 def field_kernel(
-    both_ref,
-    z1_ref,
-    z2_ref,
-    degree1_ref,
-    degree2_ref,
-    own_ref,
-    x_ref,
-    net_ref,
-    dual_ref,
-    rows_ref,
-    theta_ref,
-    gen_ref,
+    both_ref, z_ref, degree_ref, own_ref, x_ref, net_ref, dual_ref, rows_ref, theta_ref, gen_ref
 ):
     conts = net_ref.shape[0]
     both = both_ref[...]
-    old = jnp.concatenate([z1_ref[...], z2_ref[...]], axis=1)
-    degree = jnp.concatenate([degree1_ref[:1, :], degree2_ref[:1, :]], axis=1)
-    z = (degree * old - both) / (degree + 1.0)
+    degree = degree_ref[:1, :]
+    z = (degree * z_ref[...] - both) / (degree + 1.0)
     spread = times_t(jnp.concatenate([both, z], axis=0), own_ref[...])
     theta_ref[...] = x_ref[...] + spread[conts:]
     part = 1.0 / (rows_ref[4:5, :] + PENALTY + BALANCE)
@@ -453,7 +426,6 @@
     half = ((conts, slots), F32)
     edge = ((conts, edges), F32)
     tall = ((conts + 8, slots), F32)
-    counts = ((8, slots), F32)
     row = ((8, buses), F32)
 
     halo_row = halo_rows.reshape(1, slots)
@@ -513,60 +485,50 @@
         + [pltpu.SemaphoreType.DMA((len(fetched),))],
     )
     got1 = trade_near(pick1)
-    z1, p, c = call(near_first_kernel, [half, branch, branch], pick1, got1, edge_table, p, c)
-    send2, z2, delta, flow = call(
-        far_first_kernel,
-        [tall, half, branch, branch],
-        pick2,
-        got2,
+    send2, z, delta, flow = call(
+        first_kernel,
+        [tall, edge, branch, branch],
+        pick2 + got2,
+        got1,
+        pick1,
         edge_table,
         p,
         c,
         gain,
         count_edge,
     )
-    nets, boths1, boths2 = [], [], []
+    nets, boths = [], []
     for index in range(1, ROUNDS):
         first = index == 1
         got2 = trade_far(send2)
-        net, x, p, c, send1 = call(
+        counts = [count_edge] if first else []
+        (send1,) = call(send_kernel, [tall if first else half], flow, edge_table, *counts)
+        got1 = trade_near(send1)
+        net, x, p, c = call(
             beside_kernel,
-            [bus, bus, branch, branch, tall if first else half],
+            [bus, bus, branch, branch],
             flow,
             delta,
             x,
             count_inner,
             inner_table,
-            edge_table,
-            *([count_edge] if first else []),
         )
         nets.append(net)
-        got1 = trade_near(send1)
-        outs = [half, half, branch, branch]
+        outs = [edge, edge, branch, half]
+        if index < ROUNDS - 1:
+            outs = outs + [branch]
+        ends = [send2 + got2, got1, send1, z]
+        tables = [edge_table, p, c, gain]
         if first:
-            both1, z1, p, c, degree1 = call(
-                near_second_kernel, outs + [counts], send1, got1, z1, edge_table, p, c
+            both, z, flow, send2, *deltas, degree = call(
+                second_kernel, outs + [((8, edges), F32)], *ends, *tables
             )
         else:
-            both1, z1, p, c = call(
-                near_kernel, outs, send1, got1, z1, degree1, edge_table, p, c
-            )
-        outs = [half, half, branch, half]
-        if index < ROUNDS - 1:
-            outs = outs + [branch]
-        if first:
-            both2, z2, flow, send2, *deltas, degree2 = call(
-                far_second_kernel, outs + [counts], send2, got2, z2, edge_table, p, c, gain
-            )
-        else:
-            both2, z2, flow, send2, *deltas = call(
-                far_kernel, outs, send2, got2, z2, degree2, edge_table, p, c, gain
-            )
+            both, z, flow, send2, *deltas = call(next_kernel, outs, *ends, degree, *tables)
         delta = deltas[0] if deltas else None
-        boths1.append(both1)
-        boths2.append(both2)
+        boths.append(both)
     got2 = trade_far(send2)
-    (send1,) = call(send_last_kernel, [half], flow, edge_table)
+    (send1,) = call(send_kernel, [half], flow, edge_table)
     got1 = trade_near(send1)
     net, x, dual, sums = call(
         beside_last_kernel,
@@ -579,11 +541,10 @@
         gen_dual,
         rows,
         dual_sum,
-        *boths1,
-        *boths2,
+        *boths,
         *nets,
     )
-    both, sums = call(total_kernel, [edge, row], send1, send2, got1, got2, own, sums)
+    both, sums = call(total_kernel, [edge, row], send2 + got2, got1, send1, own, sums)
     parts = [sums]
     for shift in range(1, cont_size):
         parts.append(
@@ -594,10 +555,8 @@
         field_kernel,
         [bus, bus],
         both,
-        z1,
-        z2,
-        degree1,
-        degree2,
+        z,
+        degree,
         own,
         x,
         net,

time: 37.2 us -> 33.6 us (0.903)
  starting transfers between devices: 16.9 us -> 13.8 us
  waiting for transfers between devices: 9.56 us -> 9.14 us
    ppermute x5, starting transfers between devices: 10.6 us -> 8.59 us  [trade_far(): return lax.ppermute(value, axes, swap2)]
    ppermute x5, waiting for transfers between devices: 8.17 us -> 6.91 us  [trade_far(): return lax.ppermute(value, axes, swap2)]
    ppermute x5, waiting for transfers between devices: 0.01 us -> 1 us  [trade_near(): return lax.ppermute(value, axes, swap1)]
    ppermute x3, starting transfers between devices: 5 us -> 4.46 us  [local(): lax.ppermute(sums, 'cont', [(i, (i + shift) % cont_size) for i in range(c...]
    ppermute x5, starting transfers between devices: 1.24 us -> 0.75 us  [trade_near(): return lax.ppermute(value, axes, swap1)]
    pallas_call x18 -> x17, Pallas kernels: 9.85 us -> 9.69 us  [call(): pl.pallas_call(kernel, out_shape=shapes, in_specs=[pl.BlockSpec(memory_sp...]
  transfers between devices with their start and end apart: 13 -> 13, of which waited for: 6 -> 6; matrix products, arithmetic and copies ran while one was open for 0% -> 0% of each run, Pallas kernels for 6% -> 18%
where the time goes in v4:
time: 33.6 us; the launch traced here: 33.4 us
  starting transfers between devices  13.8 us (41%)
  Pallas kernels  9.69 us (29%)
  waiting for transfers between devices  9.14 us (27%)
  between operations  0.73 us (2%)
    pallas_call x17, Pallas kernels, call(): pl.pallas_call(kernel, out_shape=shapes, in_specs=[pl.BlockSpec(memory_sp...  9.69 us
    ppermute x5, starting transfers between devices, trade_far(): return lax.ppermute(value, axes, swap2)  8.59 us
    ppermute x5, waiting for transfers between devices, trade_far(): return lax.ppermute(value, axes, swap2)  6.91 us
    ppermute x3, starting transfers between devices, local(): lax.ppermute(sums, 'cont', [(i, (i + shift) % cont_size) for i in range(c...  4.46 us
    ppermute x3, waiting for transfers between devices, local(): lax.ppermute(sums, 'cont', [(i, (i + shift) % cont_size) for i in range(c...  1.23 us
    ppermute x5, waiting for transfers between devices, trade_near(): return lax.ppermute(value, axes, swap1)  1 us
    ppermute x5, starting transfers between devices, trade_near(): return lax.ppermute(value, axes, swap1)  0.75 us
  transfers between devices with their start and end apart: 13, of which 6 were waited for; matrix products, arithmetic and copies ran while one was open for 0% of the time, Pallas kernels for 18%

profile of v4, /device:TPU:0, one launch (start us, length us, event | category | flops | bytes accessed | tf_op | source)
XLA Modules:
  0.0 33.4 jit_solution(16942158639989549510)
XLA Ops:
  0.6 1.1 %shard_map.148 = (s32[1,128]{1,0:T(1,128)S(1)}, f32[64,512]{1,0:T(8,128)S(1)}, s32[640]{0:T(1024)S(1)}, s32[640]{0:T(1024)S(1)}, f32[640]{0:T(1024)S(1)}, /*inde...) custom-call(s32[1,128]{1,0:T(1,128)} %bitcast.10, f32[64,512]{1,0:T(8,128)} %refs_1_.1, s32[640]{0:T(1024)} %refs_2_.1, ...), custom_call_target="tpu_custom_call" | custom-call | flops 83886080 | bytes 139264 | tf_op jit(solution)/shard_map/pallas_call | solution.py:363
  1.8 3.0 %collective-permute-start = (f32[64,128]{1,0:T(8,128)S(1)}, f32[64,128]{1,0:T(8,128)S(1)}, u32[]{:S(2)}, u32[]{:S(2)}) collective-permute-start(f32[64,128]{1,0:T(8,128)S(1)} %get-tuple-element.63), channel_id=1, source_target_pairs={{0,8},{1,2},{2,1},{3,4},{4,3},{5,6},{6,5},{7,15},{8,0},{9,10},{10,... | collective-permute-start | bytes 98312 | tf_op jit(solution)/shard_map/ppermute | solution.py:419
  4.8 2.2 %shard_map.149 = (f32[64,512]{1,0:T(8,128)S(1)}, f32[64,128]{1,0:T(8,128)S(1)}, bf16[640,256]{1,0:T(8,128)(2,1)S(1)}, bf16[640,512]{1,0:T(8,128)(2,1)S(1)}, f32[...) custom-call(f32[64,640]{1,0:T(8,128)} %lam_f_hbm.1, ...), custom_call_target="tpu_custom_call" | custom-call | flops 83886080 | bytes 1032192 | tf_op jit(solution)/shard_map/pallas_call | solution.py:363
  7.3 1.0 %collective-permute-done.1.got1_ref = f32[64,128]{1,0:T(8,128)S(1)} collective-permute-done((f32[64,128]{1,0:T(8,128)S(1)}, f32[64,128]{1,0:T(8,128)S(1)}, u32[]{:S(2)}, u32[]{:S(2)}) %collective-permute-start.1) | collective-permute-done | bytes 32800 | tf_op jit(solution)/shard_map/ppermute | solution.py:416
  8.7 1.4 %collective-permute-start.2 = (f32[72,128]{1,0:T(8,128)S(1)}, f32[72,128]{1,0:T(8,128)S(1)}, u32[]{:S(2)}, u32[]{:S(2)}) collective-permute-start(f32[72,128]{1,0:T(8,128)S(1)} %get-tuple-element.76), channel_id=1, source_target_pairs={{0,8},{1,2},{2,1},{3,4},{4,3},{5,6},{6,5},{7,15},{8,0},{9,10},{10,... | collective-permute-start | bytes 110600 | tf_op jit(solution)/shard_map/ppermute | solution.py:419
  10.5 0.5 %shard_map.152 = (f32[64,512]{1,0:T(8,128)S(1)}, f32[64,512]{1,0:T(8,128)S(1)}, f32[64,640]{1,0:T(8,128)S(1)}, f32[64,640]{1,0:T(8,128)S(1)}) custom-call(f32[64,640]{1,0:T(8,128)S(1)} %get-tuple-element.77.flow_ref, f32[64,640]{1,0:T(8,128)S(1)} %get-tuple-element.79.delta_ref, f32[64,512]{1,0:T(8,128)S(1)} %get-tuple-element.80.x_ref, ...), custom_call_target="tpu_custom_call" | custom-call | flops 83886080 | bytes 1130496 | tf_op jit(solution)/shard_map/pallas_call | solution.py:363
  11.1 1.6 %collective-permute-done.2 = f32[72,128]{1,0:T(8,128)S(1)} collective-permute-done((f32[72,128]{1,0:T(8,128)S(1)}, f32[72,128]{1,0:T(8,128)S(1)}, u32[]{:S(2)}, u32[]{:S(2)}) %collective-permute-start.2) | collective-permute-done | bytes 36896 | tf_op jit(solution)/shard_map/ppermute | solution.py:419
  12.7 0.4 %shard_map.153 = (f32[64,256]{1,0:T(8,128)S(1)}, f32[64,256]{1,0:T(8,128)S(1)}, f32[64,640]{1,0:T(8,128)S(1)}, f32[64,128]{1,0:T(8,128)S(1)}, f32[64,640]{1,0:T(8,128)S(1)}, /*index=5*/f32[8,256]{1,0:T(8,128)S(1)}) custom-call(f32[72,128]{1,0:T(8,128)S(1)} %add.16.far_ref, f32[72,128]{1,0:T(8,128)S(1)} %collective-permute-done.3.got1_ref, ...), custom_call_target="tpu_custom_call" | custom-call | flops 83886080 | bytes 995328 | tf_op jit(solution)/shard_map/pallas_call | solution.py:363
  13.1 1.4 %collective-permute-start.4 = (f32[64,128]{1,0:T(8,128)S(1)}, f32[64,128]{1,0:T(8,128)S(1)}, u32[]{:S(2)}, u32[]{:S(2)}) collective-permute-start(f32[64,128]{1,0:T(8,128)S(1)} %get-tuple-element.85), channel_id=1, source_target_pairs={{0,8},{1,2},{2,1},{3,4},{4,3},{5,6},{6,5},{7,15},{8,0},{9,10},{10,... | collective-permute-start | bytes 98312 | tf_op jit(solution)/shard_map/ppermute | solution.py:419
  14.8 0.6 %shard_map.155 = (f32[64,512]{1,0:T(8,128)S(1)}, f32[64,512]{1,0:T(8,128)S(1)}, f32[64,640]{1,0:T(8,128)S(1)}, f32[64,640]{1,0:T(8,128)S(1)}) custom-call(f32[64,640]{1,0:T(8,128)S(1)} %get-tuple-element.86.flow_ref, f32[64,640]{1,0:T(8,128)S(1)} %get-tuple-element.89.delta_ref, f32[64,512]{1,0:T(8,128)S(1)} %get-tuple-element.90.x_ref, ...), custom_call_target="tpu_custom_call" | custom-call | flops 83886080 | bytes 1130496 | tf_op jit(solution)/shard_map/pallas_call | solution.py:363
  15.3 1.7 %collective-permute-done.4 = f32[64,128]{1,0:T(8,128)S(1)} collective-permute-done((f32[64,128]{1,0:T(8,128)S(1)}, f32[64,128]{1,0:T(8,128)S(1)}, u32[]{:S(2)}, u32[]{:S(2)}) %collective-permute-start.4) | collective-permute-done | bytes 32800 | tf_op jit(solution)/shard_map/ppermute | solution.py:419
  17.5 1.4 %collective-permute-start.6 = (f32[64,128]{1,0:T(8,128)S(1)}, f32[64,128]{1,0:T(8,128)S(1)}, u32[]{:S(2)}, u32[]{:S(2)}) collective-permute-start(f32[64,128]{1,0:T(8,128)S(1)} %get-tuple-element.93), channel_id=1, source_target_pairs={{0,8},{1,2},{2,1},{3,4},{4,3},{5,6},{6,5},{7,15},{8,0},{9,10},{10,... | collective-permute-start | bytes 98312 | tf_op jit(solution)/shard_map/ppermute | solution.py:419
  19.2 0.6 %shard_map.158 = (f32[64,512]{1,0:T(8,128)S(1)}, f32[64,512]{1,0:T(8,128)S(1)}, f32[64,640]{1,0:T(8,128)S(1)}, f32[64,640]{1,0:T(8,128)S(1)}) custom-call(f32[64,640]{1,0:T(8,128)S(1)} %get-tuple-element.94.flow_ref, f32[64,640]{1,0:T(8,128)S(1)} %get-tuple-element.96.delta_ref, f32[64,512]{1,0:T(8,128)S(1)} %get-tuple-element.97.x_ref, ...), custom_call_target="tpu_custom_call" | custom-call | flops 83886080 | bytes 1130496 | tf_op jit(solution)/shard_map/pallas_call | solution.py:363
  19.7 1.7 %collective-permute-done.6 = f32[64,128]{1,0:T(8,128)S(1)} collective-permute-done((f32[64,128]{1,0:T(8,128)S(1)}, f32[64,128]{1,0:T(8,128)S(1)}, u32[]{:S(2)}, u32[]{:S(2)}) %collective-permute-start.6) | collective-permute-done | bytes 32800 | tf_op jit(solution)/shard_map/ppermute | solution.py:419
  21.5 0.4 %shard_map.159 = (f32[64,256]{1,0:T(8,128)S(1)}, f32[64,256]{1,0:T(8,128)S(1)}, f32[64,640]{1,0:T(8,128)S(1)}, f32[64,128]{1,0:T(8,128)S(1)}) custom-call(f32[64,128]{1,0:T(8,128)S(1)} %add.18.far_ref, f32[64,128]{1,0:T(8,128)S(1)} %collective-permute-done.7.got1_ref, f32[64,128]{1,0:T(8,128)S(1)} %shard_map.157.send1_ref, ...), custom_call_target="tpu_custom_call" | custom-call | flops 83886080 | bytes 991232 | tf_op jit(solution)/shard_map/pallas_call | solution.py:363
  21.9 1.4 %collective-permute-start.8 = (f32[64,128]{1,0:T(8,128)S(1)}, f32[64,128]{1,0:T(8,128)S(1)}, u32[]{:S(2)}, u32[]{:S(2)}) collective-permute-start(f32[64,128]{1,0:T(8,128)S(1)} %get-tuple-element.100), channel_id=1, source_target_pairs={{0,8},{1,2},{2,1},{3,4},{4,3},{5,6},{6,5},{7,15},{8,0},{9,10},{10,... | collective-permute-start | bytes 98312 | tf_op jit(solution)/shard_map/ppermute | solution.py:419
  23.6 0.5 %shard_map.161 = (f32[64,512]{1,0:T(8,128)S(1)}, f32[64,512]{1,0:T(8,128)S(1)}, f32[64,512]{1,0:T(8,128)S(1)}, f32[8,512]{1,0:T(8,128)S(1)}) custom-call(f32[64,640]{1,0:T(8,128)S(1)} %get-tuple-element.101.flow_ref, f32[64,512]{1,0:T(8,128)S(1)} %get-tuple-element.102.x_ref, f32[8,512]{1,0:T(8,128)S(1)} %get-tuple-element.81.count_ref, ...), custom_call_target="tpu_custom_call" | custom-call | flops 83886080 | bytes 1982464 | tf_op jit(solution)/shard_map/pallas_call | solution.py:363
  24.1 1.8 %collective-permute-done.8 = f32[64,128]{1,0:T(8,128)S(1)} collective-permute-done((f32[64,128]{1,0:T(8,128)S(1)}, f32[64,128]{1,0:T(8,128)S(1)}, u32[]{:S(2)}, u32[]{:S(2)}) %collective-permute-start.8) | collective-permute-done | bytes 32800 | tf_op jit(solution)/shard_map/ppermute | solution.py:419
  26.1 1.4 %collective-permute-start.10 = (f32[8,512]{1,0:T(8,128)S(1)}, f32[8,512]{1,0:T(8,128)S(1)}, u32[]{:S(2)}, u32[]{:S(2)}) collective-permute-start(f32[8,512]{1,0:T(8,128)S(1)} %get-tuple-element.119.refs_0_), channel_id=1, source_target_pairs={{0,8},{8,16},{16,24},{24,0},{1,9},{9,17},{17,25},{25,1},{2,10},{10... | collective-permute-start | bytes 49160 | tf_op jit(solution)/shard_map/ppermute | solution.py:551
  27.4 1.5 %collective-permute-start.11 = (f32[8,512]{1,0:T(8,128)S(1)}, f32[8,512]{1,0:T(8,128)S(1)}, u32[]{:S(2)}, u32[]{:S(2)}) collective-permute-start(f32[8,512]{1,0:T(8,128)S(1)} %get-tuple-element.119.refs_0_), channel_id=1, source_target_pairs={{0,16},{8,24},{16,0},{24,8},{1,17},{9,25},{17,1},{25,9},{2,18},{10... | collective-permute-start | bytes 49160 | tf_op jit(solution)/shard_map/ppermute | solution.py:551
  28.9 1.6 %collective-permute-start.12 = (f32[8,512]{1,0:T(8,128)S(1)}, f32[8,512]{1,0:T(8,128)S(1)}, u32[]{:S(2)}, u32[]{:S(2)}) collective-permute-start(f32[8,512]{1,0:T(8,128)S(1)} %get-tuple-element.119.refs_0_), channel_id=1, source_target_pairs={{0,24},{8,0},{16,8},{24,16},{1,25},{9,1},{17,9},{25,17},{2,26},{10... | collective-permute-start | bytes 49160 | tf_op jit(solution)/shard_map/ppermute | solution.py:551
  30.5 0.9 %shard_map.163 = (f32[64,512]{1,0:T(8,128)}, f32[64,512]{1,0:T(8,128)S(1)}) custom-call(f32[64,256]{1,0:T(8,128)S(1)} %get-tuple-element.113.both_ref, f32[64,256]{1,0:T(8,128)S(1)} %get-tuple-element.114.z_ref, f32[8,256]{1,0:T(8,128)S(1)} %get-tuple-element.88.degree_ref, bf16[512,256]{1,0:T(8,128)(2,1)S(1)} %get-tuple-element.69.own_ref, ...), custom_call_target="tpu_custom_call" | custom-call | flops 83886080 | bytes 811008 | tf_op jit(solution)/shard_map/pallas_call | solution.py:363
  31.4 1.2 %collective-permute-done.12.refs_3_ = f32[8,512]{1,0:T(8,128)S(1)} collective-permute-done((f32[8,512]{1,0:T(8,128)S(1)}, f32[8,512]{1,0:T(8,128)S(1)}, u32[]{:S(2)}, u32[]{:S(2)}) %collective-permute-start.12) | collective-permute-done | bytes 16416 | tf_op jit(solution)/shard_map/ppermute | solution.py:551
  32.7 0.7 %shard_map.164 = (f32[64,512]{1,0:T(8,128)}, f32[1,512]{1,0:T(1,128)}) custom-call(f32[8,512]{1,0:T(8,128)S(1)} %get-tuple-element.119.refs_0_, f32[8,512]{1,0:T(8,128)S(1)} %collective-permute-done.10.refs_1_, f32[8,512]{1,0:T(8,128)S(1)} %collective-permute-done.11.refs_2_, f32[8,512]{1,0:T(8,128)S(1)} %collective-permute-done.12.refs_3_, ...), custom_call_target="tpu_custom_call" | custom-call | flops 83886080 | bytes 212992 | tf_op jit(solution)/shard_map/pallas_call | solution.py:363
  (27 shorter events, 2.5 us)
Async XLA Ops:
  1.8 5.5 %collective-permute-start = (f32[64,128]{1,0:T(8,128)S(1)}, f32[64,128]{1,0:T(8,128)S(1)}, u32[]{:S(2)}, u32[]{:S(2)}) collective-permute-start(f32[64,128]{1,0:T(8,128)S(1)} %get-tuple-element.63), channel_id=1, source_target_pairs={{0,8},{1,2},{2,1},{3,4},{4,3},{5,6},{6,5},{7,15},{8,0},{9,10},{10,... | collective-permute-start | bytes 98312 | tf_op jit(solution)/shard_map/ppermute | solution.py:419
  7.0 1.3 %collective-permute-start.1 = (f32[64,128]{1,0:T(8,128)S(1)}, f32[64,128]{1,0:T(8,128)S(1)}, u32[]{:S(2)}, u32[]{:S(2)}) collective-permute-start(f32[64,128]{1,0:T(8,128)S(1)} %get-tuple-element.70.pick1_ref), channel_id=1, source_target_pairs={{0,1},{1,0},{2,3},{3,2},{4,5},{5,4},{6,7},{7,6},{8,9},{9,8},{10,11... | collective-permute-start | bytes 98312 | tf_op jit(solution)/shard_map/ppermute | solution.py:416
  8.7 4.0 %collective-permute-start.2 = (f32[72,128]{1,0:T(8,128)S(1)}, f32[72,128]{1,0:T(8,128)S(1)}, u32[]{:S(2)}, u32[]{:S(2)}) collective-permute-start(f32[72,128]{1,0:T(8,128)S(1)} %get-tuple-element.76), channel_id=1, source_target_pairs={{0,8},{1,2},{2,1},{3,4},{4,3},{5,6},{6,5},{7,15},{8,0},{9,10},{10,... | collective-permute-start | bytes 110600 | tf_op jit(solution)/shard_map/ppermute | solution.py:419
  10.3 2.4 %collective-permute-start.3 = (f32[72,128]{1,0:T(8,128)S(1)}, f32[72,128]{1,0:T(8,128)S(1)}, u32[]{:S(2)}, u32[]{:S(2)}) collective-permute-start(f32[72,128]{1,0:T(8,128)S(1)} %shard_map.151.send1_ref), channel_id=1, source_target_pairs={{0,1},{1,0},{2,3},{3,2},{4,5},{5,4},{6,7},{7,6},{8,9},{9,8},{10,11... | collective-permute-start | bytes 110600 | tf_op jit(solution)/shard_map/ppermute | solution.py:416
  13.1 4.0 %collective-permute-start.4 = (f32[64,128]{1,0:T(8,128)S(1)}, f32[64,128]{1,0:T(8,128)S(1)}, u32[]{:S(2)}, u32[]{:S(2)}) collective-permute-start(f32[64,128]{1,0:T(8,128)S(1)} %get-tuple-element.85), channel_id=1, source_target_pairs={{0,8},{1,2},{2,1},{3,4},{4,3},{5,6},{6,5},{7,15},{8,0},{9,10},{10,... | collective-permute-start | bytes 98312 | tf_op jit(solution)/shard_map/ppermute | solution.py:419
  14.7 2.4 %collective-permute-start.5 = (f32[64,128]{1,0:T(8,128)S(1)}, f32[64,128]{1,0:T(8,128)S(1)}, u32[]{:S(2)}, u32[]{:S(2)}) collective-permute-start(f32[64,128]{1,0:T(8,128)S(1)} %shard_map.154.send1_ref), channel_id=1, source_target_pairs={{0,1},{1,0},{2,3},{3,2},{4,5},{5,4},{6,7},{7,6},{8,9},{9,8},{10,11... | collective-permute-start | bytes 98312 | tf_op jit(solution)/shard_map/ppermute | solution.py:416
  17.5 4.0 %collective-permute-start.6 = (f32[64,128]{1,0:T(8,128)S(1)}, f32[64,128]{1,0:T(8,128)S(1)}, u32[]{:S(2)}, u32[]{:S(2)}) collective-permute-start(f32[64,128]{1,0:T(8,128)S(1)} %get-tuple-element.93), channel_id=1, source_target_pairs={{0,8},{1,2},{2,1},{3,4},{4,3},{5,6},{6,5},{7,15},{8,0},{9,10},{10,... | collective-permute-start | bytes 98312 | tf_op jit(solution)/shard_map/ppermute | solution.py:419
  19.1 2.4 %collective-permute-start.7 = (f32[64,128]{1,0:T(8,128)S(1)}, f32[64,128]{1,0:T(8,128)S(1)}, u32[]{:S(2)}, u32[]{:S(2)}) collective-permute-start(f32[64,128]{1,0:T(8,128)S(1)} %shard_map.157.send1_ref), channel_id=1, source_target_pairs={{0,1},{1,0},{2,3},{3,2},{4,5},{5,4},{6,7},{7,6},{8,9},{9,8},{10,11... | collective-permute-start | bytes 98312 | tf_op jit(solution)/shard_map/ppermute | solution.py:416
  21.9 4.0 %collective-permute-start.8 = (f32[64,128]{1,0:T(8,128)S(1)}, f32[64,128]{1,0:T(8,128)S(1)}, u32[]{:S(2)}, u32[]{:S(2)}) collective-permute-start(f32[64,128]{1,0:T(8,128)S(1)} %get-tuple-element.100), channel_id=1, source_target_pairs={{0,8},{1,2},{2,1},{3,4},{4,3},{5,6},{6,5},{7,15},{8,0},{9,10},{10,... | collective-permute-start | bytes 98312 | tf_op jit(solution)/shard_map/ppermute | solution.py:419
  23.5 2.4 %collective-permute-start.9 = (f32[64,128]{1,0:T(8,128)S(1)}, f32[64,128]{1,0:T(8,128)S(1)}, u32[]{:S(2)}, u32[]{:S(2)}) collective-permute-start(f32[64,128]{1,0:T(8,128)S(1)} %shard_map.160.send1_ref), channel_id=1, source_target_pairs={{0,1},{1,0},{2,3},{3,2},{4,5},{5,4},{6,7},{7,6},{8,9},{9,8},{10,11... | collective-permute-start | bytes 98312 | tf_op jit(solution)/shard_map/ppermute | solution.py:416
  26.1 5.4 %collective-permute-start.10 = (f32[8,512]{1,0:T(8,128)S(1)}, f32[8,512]{1,0:T(8,128)S(1)}, u32[]{:S(2)}, u32[]{:S(2)}) collective-permute-start(f32[8,512]{1,0:T(8,128)S(1)} %get-tuple-element.119.refs_0_), channel_id=1, source_target_pairs={{0,8},{8,16},{16,24},{24,0},{1,9},{9,17},{17,25},{25,1},{2,10},{10... | collective-permute-start | bytes 49160 | tf_op jit(solution)/shard_map/ppermute | solution.py:551
  27.4 4.0 %collective-permute-start.11 = (f32[8,512]{1,0:T(8,128)S(1)}, f32[8,512]{1,0:T(8,128)S(1)}, u32[]{:S(2)}, u32[]{:S(2)}) collective-permute-start(f32[8,512]{1,0:T(8,128)S(1)} %get-tuple-element.119.refs_0_), channel_id=1, source_target_pairs={{0,16},{8,24},{16,0},{24,8},{1,17},{9,25},{17,1},{25,9},{2,18},{10... | collective-permute-start | bytes 49160 | tf_op jit(solution)/shard_map/ppermute | solution.py:551
  28.9 3.7 %collective-permute-start.12 = (f32[8,512]{1,0:T(8,128)S(1)}, f32[8,512]{1,0:T(8,128)S(1)}, u32[]{:S(2)}, u32[]{:S(2)}) collective-permute-start(f32[8,512]{1,0:T(8,128)S(1)} %get-tuple-element.119.refs_0_), channel_id=1, source_target_pairs={{0,24},{8,0},{16,8},{24,16},{1,25},{9,1},{17,9},{25,17},{2,26},{10... | collective-permute-start | bytes 49160 | tf_op jit(solution)/shard_map/ppermute | solution.py:551

commit v5 on v4

--- a/solution.py
+++ b/solution.py
@@ -54,7 +54,7 @@
 
 def load_kernel(count, *refs):
     sources, targets = refs[:count], refs[count : 2 * count]
-    pick_ref, own_ref, semaphores = refs[2 * count :]
+    pick1_ref, pick2_ref, own_ref, semaphores = refs[2 * count :]
     copies = fetch(sources, targets, semaphores)
     halo_ref, theta_ref = targets[:2]
     buses = theta_ref.shape[1]
@@ -65,7 +65,9 @@
     table = jnp.where(rows == ids, 1.0, 0.0).astype(BF16)
     own_ref[...] = table
     copies[1].wait()
-    pick_ref[...] = times(theta_ref[...], table[:, slots:])
+    pick = times(theta_ref[...], table)
+    pick1_ref[...] = pick[:, :slots]
+    pick2_ref[...] = pick[:, slots:]
     for copy in copies[2:]:
         copy.wait()
 
@@ -84,9 +86,7 @@
     to_ref,
     halo_ref,
     stiff_ref,
-    own_ref,
     dual_ref,
-    pick_ref,
     edge_ref,
     inner_ref,
     gain_ref,
@@ -115,10 +115,8 @@
     copies = fetch(sources, targets, semaphores)
     buses = theta_ref.shape[1]
     branches = from_ref.shape[1]
-    slots = halo_ref.shape[1]
     ids = column_ids(halo_ref[...], buses)
     edges = ids.shape[1]
-    pick_ref[...] = times(theta_ref[...], own_ref[:, :slots])
     lanes = lax.broadcasted_iota(jnp.int32, (edges, buses), 1)
     ids_col = jnp.broadcast_to(ids, (edges, edges)).T[:, :1]
     inner = 1.0 - jnp.max(jnp.where(lanes == ids_col, 1.0, 0.0), axis=0, keepdims=True)
@@ -155,6 +153,29 @@
         rows_ref[2 * index : 2 * index + 2, :] = jnp.broadcast_to(ref[...], (2, buses))
 
 
+def gap_step(z, scale, edge_ref, p_ref, c_ref, gain_ref, flow_ref, send_ref, deltas):
+    conts, slots = z.shape[0], send_ref.shape[1]
+    place, places = lax.axis_index("net"), lax.axis_size("net")
+    has_far = jnp.where(place % 2 == 0, place > 0, place < places - 1)
+
+    def finish(moved):
+        for delta_ref in deltas:
+            delta_ref[...] = p_ref[...] + moved
+        flow = gain_ref[...] * (c_ref[...] + scale * moved)
+        flow_ref[...] = flow
+        return flow
+
+    @pl.when(has_far)
+    def _():
+        flow = finish(times_t(z, edge_ref[...]))
+        send_ref[:conts, :] = times(flow, edge_ref[:, slots:])
+
+    @pl.when(jnp.logical_not(has_far))
+    def _():
+        finish(times_t(z[:, :slots], edge_ref[:, :slots]))
+        send_ref[:conts, :] = jnp.zeros((conts, slots), F32)
+
+
 def first_kernel(
     far_ref,
     got1_ref,
@@ -173,11 +194,7 @@
     conts = p_ref.shape[0]
     z = jnp.concatenate([pick1_ref[...] + got1_ref[...], far_ref[...]], axis=1)
     z_ref[...] = z
-    moved = times_t(z, edge_ref[...])
-    delta_ref[...] = p_ref[...] + moved
-    flow = gain_ref[...] * (c_ref[...] + moved)
-    flow_ref[...] = flow
-    send_ref[:conts, :] = times(flow, edge_ref[:, slots:])
+    gap_step(z, 1.0, edge_ref, p_ref, c_ref, gain_ref, flow_ref, send_ref, [delta_ref])
     send_ref[conts:, :] = count_ref[:, slots:]
 
 
@@ -191,17 +208,11 @@
     far_ref, got1_ref, send1_ref, z_ref, degree, edge_ref, p_ref, c_ref, gain_ref, outs
 ):
     both_ref, z_out_ref, flow_ref, out_ref, *deltas = outs
-    slots = out_ref.shape[1]
     both = both_ends(far_ref, got1_ref, send1_ref, slice(0, z_ref.shape[0]))
     both_ref[...] = both
     z = (degree * z_ref[...] - both) / (degree + 1.0)
     z_out_ref[...] = z
-    moved = times_t(z, edge_ref[...])
-    for delta_ref in deltas:
-        delta_ref[...] = p_ref[...] + moved
-    flow = gain_ref[...] * (c_ref[...] + 2.0 * moved)
-    flow_ref[...] = flow
-    out_ref[...] = times(flow, edge_ref[:, slots:])
+    gap_step(z, 2.0, edge_ref, p_ref, c_ref, gain_ref, flow_ref, out_ref, deltas)
 
 
 def second_kernel(
@@ -435,22 +446,22 @@
     def load(*refs):
         load_kernel(number, *refs)
 
-    *here, pick2, own = call(
+    *here, pick1, pick2, own = call(
         load,
-        [(a.shape, a.dtype) for a in fetched] + [half, ((buses, edges), BF16)],
+        [(a.shape, a.dtype) for a in fetched] + [half, half, ((buses, edges), BF16)],
         *in_hbm(*fetched),
         spaces=[pltpu.HBM] * number,
         scratch=[pltpu.SemaphoreType.DMA((number,))],
     )
     got2 = trade_far(pick2)
+    got1 = trade_near(pick1)
     halo_row, angles = here[:2]
     from_row, to_row, stiff_row = (a.reshape(1, branches) for a in here[2:])
     rows = [a.reshape(1, buses) for a in (base_prev, bus_load, gen_cost, gen_limit)]
     fetched = [lam_from, lam_to, outage, gen_dual, *rows]
-    near_args = [angles, from_row, to_row, halo_row, stiff_row, own]
+    near_args = [angles, from_row, to_row, halo_row, stiff_row]
     (
         gen_dual,
-        pick1,
         edge_table,
         inner_table,
         gain,
@@ -465,7 +476,6 @@
         prep_kernel,
         [
             bus,
-            half,
             ((branches, edges), BF16),
             ((branches, buses), BF16),
             branch,
@@ -484,7 +494,6 @@
         + [pltpu.VMEM((1, buses), F32)] * 4
         + [pltpu.SemaphoreType.DMA((len(fetched),))],
     )
-    got1 = trade_near(pick1)
     send2, z, delta, flow = call(
         first_kernel,
         [tall, edge, branch, branch],

time: 33.6 us -> 32 us (0.952)
  waiting for transfers between devices: 9.14 us -> 6.56 us
  starting transfers between devices: 13.8 us -> 15.9 us
  Pallas kernels: 9.69 us -> 8.61 us
    ppermute x5, starting transfers between devices: 8.59 us -> 10.5 us  [trade_far(): return lax.ppermute(value, axes, swap2)]
    ppermute x5, waiting for transfers between devices: 6.91 us -> 5.17 us  [trade_far(): return lax.ppermute(value, axes, swap2)]
    pallas_call x17, Pallas kernels: 9.69 us -> 8.61 us  [call(): pl.pallas_call(kernel, out_shape=shapes, in_specs=[pl.BlockSpec(memory_sp...]
    ppermute x5, waiting for transfers between devices: 1 us -> 0.01 us  [trade_near(): return lax.ppermute(value, axes, swap1)]
  transfers between devices with their start and end apart: 13 -> 13, of which waited for: 6 -> 5; matrix products, arithmetic and copies ran while one was open for 0% -> 0% of each run, Pallas kernels for 18% -> 18%
where the time goes in v5:
time: 32 us; the launch traced here: 31.8 us
  starting transfers between devices  15.9 us (50%)
  Pallas kernels  8.61 us (27%)
  waiting for transfers between devices  6.56 us (20%)
  between operations  0.78 us (2%)
    ppermute x5, starting transfers between devices, trade_far(): return lax.ppermute(value, axes, swap2)  10.5 us
    pallas_call x17, Pallas kernels, call(): pl.pallas_call(kernel, out_shape=shapes, in_specs=[pl.BlockSpec(memory_sp...  8.61 us
    ppermute x5, waiting for transfers between devices, trade_far(): return lax.ppermute(value, axes, swap2)  5.17 us
    ppermute x3, starting transfers between devices, local(): lax.ppermute(sums, 'cont', [(i, (i + shift) % cont_size) for i in range(c...  4.79 us
    ppermute x3, waiting for transfers between devices, local(): lax.ppermute(sums, 'cont', [(i, (i + shift) % cont_size) for i in range(c...  1.37 us
  transfers between devices with their start and end apart: 13, of which 5 were waited for; matrix products, arithmetic and copies ran while one was open for 0% of the time, Pallas kernels for 18%

profile of v5, /device:TPU:0, one launch (start us, length us, event | category | flops | bytes accessed | tf_op | source)
XLA Modules:
  0.0 31.8 jit_solution(17907281795600678869)
XLA Ops:
  0.6 1.1 %shard_map.148 = (s32[1,128]{1,0:T(1,128)S(1)}, f32[64,512]{1,0:T(8,128)S(1)}, s32[640]{0:T(1024)S(1)}, s32[640]{0:T(1024)S(1)}, f32[640]{0:T(1024)S(1)}, /*inde...) custom-call(s32[1,128]{1,0:T(1,128)} %bitcast.10, f32[64,512]{1,0:T(8,128)} %refs_1_.1, ...), custom_call_target="tpu_custom_call" | custom-call | flops 83886080 | bytes 139264 | tf_op jit(solution)/shard_map/pallas_call | solution.py:374
  1.8 3.0 %collective-permute-start = (f32[64,128]{1,0:T(8,128)S(1)}, f32[64,128]{1,0:T(8,128)S(1)}, u32[]{:S(2)}, u32[]{:S(2)}) collective-permute-start(f32[64,128]{1,0:T(8,128)S(1)} %get-tuple-element.63), channel_id=1, source_target_pairs={{0,8},{1,2},{2,1},{3,4},{4,3},{5,6},{6,5},{7,15},{8,0},{9,10},{10,... | collective-permute-start | bytes 98312 | tf_op jit(solution)/shard_map/ppermute | solution.py:430
  5.0 1.9 %shard_map.149 = (f32[64,512]{1,0:T(8,128)S(1)}, bf16[640,256]{1,0:T(8,128)(2,1)S(1)}, bf16[640,512]{1,0:T(8,128)(2,1)S(1)}, f32[64,640]{1,0:T(8,128)S(1)}, f32[...) custom-call(f32[64,640]{1,0:T(8,128)} %lam_f_hbm.1, ...), custom_call_target="tpu_custom_call" | custom-call | flops 83886080 | bytes 770048 | tf_op jit(solution)/shard_map/pallas_call | solution.py:374
  7.1 1.9 %collective-permute-start.2 = (f32[72,128]{1,0:T(8,128)S(1)}, f32[72,128]{1,0:T(8,128)S(1)}, u32[]{:S(2)}, u32[]{:S(2)}) collective-permute-start(f32[72,128]{1,0:T(8,128)S(1)} %get-tuple-element.75), channel_id=1, source_target_pairs={{0,8},{1,2},{2,1},{3,4},{4,3},{5,6},{6,5},{7,15},{8,0},{9,10},{10,... | collective-permute-start | bytes 110600 | tf_op jit(solution)/shard_map/ppermute | solution.py:430
  9.3 0.5 %shard_map.152 = (f32[64,512]{1,0:T(8,128)S(1)}, f32[64,512]{1,0:T(8,128)S(1)}, f32[64,640]{1,0:T(8,128)S(1)}, f32[64,640]{1,0:T(8,128)S(1)}) custom-call(f32[64,640]{1,0:T(8,128)S(1)} %get-tuple-element.76.flow_ref, f32[64,640]{1,0:T(8,128)S(1)} %get-tuple-element.78.delta_ref, f32[64,512]{1,0:T(8,128)S(1)} %get-tuple-element.79.x_ref, ...), custom_call_target="tpu_custom_call" | custom-call | flops 83886080 | bytes 1130496 | tf_op jit(solution)/shard_map/pallas_call | solution.py:374
  9.9 1.3 %collective-permute-done.2 = f32[72,128]{1,0:T(8,128)S(1)} collective-permute-done((f32[72,128]{1,0:T(8,128)S(1)}, f32[72,128]{1,0:T(8,128)S(1)}, u32[]{:S(2)}, u32[]{:S(2)}) %collective-permute-start.2) | collective-permute-done | bytes 36896 | tf_op jit(solution)/shard_map/ppermute | solution.py:430
  11.2 0.2 shard_map.153
  11.4 1.9 %collective-permute-start.4 = (f32[64,128]{1,0:T(8,128)S(1)}, f32[64,128]{1,0:T(8,128)S(1)}, u32[]{:S(2)}, u32[]{:S(2)}) collective-permute-start(f32[64,128]{1,0:T(8,128)S(1)} %get-tuple-element.84), channel_id=1, source_target_pairs={{0,8},{1,2},{2,1},{3,4},{4,3},{5,6},{6,5},{7,15},{8,0},{9,10},{10,... | collective-permute-start | bytes 98312 | tf_op jit(solution)/shard_map/ppermute | solution.py:430
  13.6 0.5 %shard_map.155 = (f32[64,512]{1,0:T(8,128)S(1)}, f32[64,512]{1,0:T(8,128)S(1)}, f32[64,640]{1,0:T(8,128)S(1)}, f32[64,640]{1,0:T(8,128)S(1)}) custom-call(f32[64,640]{1,0:T(8,128)S(1)} %get-tuple-element.85.flow_ref, f32[64,640]{1,0:T(8,128)S(1)} %get-tuple-element.88.delta_ref, f32[64,512]{1,0:T(8,128)S(1)} %get-tuple-element.89.x_ref, ...), custom_call_target="tpu_custom_call" | custom-call | flops 83886080 | bytes 1130496 | tf_op jit(solution)/shard_map/pallas_call | solution.py:374
  14.1 1.3 %collective-permute-done.4 = f32[64,128]{1,0:T(8,128)S(1)} collective-permute-done((f32[64,128]{1,0:T(8,128)S(1)}, f32[64,128]{1,0:T(8,128)S(1)}, u32[]{:S(2)}, u32[]{:S(2)}) %collective-permute-start.4) | collective-permute-done | bytes 32800 | tf_op jit(solution)/shard_map/ppermute | solution.py:430
  15.4 0.2 shard_map.156
  15.6 1.9 %collective-permute-start.6 = (f32[64,128]{1,0:T(8,128)S(1)}, f32[64,128]{1,0:T(8,128)S(1)}, u32[]{:S(2)}, u32[]{:S(2)}) collective-permute-start(f32[64,128]{1,0:T(8,128)S(1)} %get-tuple-element.92), channel_id=1, source_target_pairs={{0,8},{1,2},{2,1},{3,4},{4,3},{5,6},{6,5},{7,15},{8,0},{9,10},{10,... | collective-permute-start | bytes 98312 | tf_op jit(solution)/shard_map/ppermute | solution.py:430
  17.8 0.5 %shard_map.158 = (f32[64,512]{1,0:T(8,128)S(1)}, f32[64,512]{1,0:T(8,128)S(1)}, f32[64,640]{1,0:T(8,128)S(1)}, f32[64,640]{1,0:T(8,128)S(1)}) custom-call(f32[64,640]{1,0:T(8,128)S(1)} %get-tuple-element.93.flow_ref, f32[64,640]{1,0:T(8,128)S(1)} %get-tuple-element.95.delta_ref, f32[64,512]{1,0:T(8,128)S(1)} %get-tuple-element.96.x_ref, ...), custom_call_target="tpu_custom_call" | custom-call | flops 83886080 | bytes 1130496 | tf_op jit(solution)/shard_map/pallas_call | solution.py:374
  18.3 1.3 %collective-permute-done.6 = f32[64,128]{1,0:T(8,128)S(1)} collective-permute-done((f32[64,128]{1,0:T(8,128)S(1)}, f32[64,128]{1,0:T(8,128)S(1)}, u32[]{:S(2)}, u32[]{:S(2)}) %collective-permute-start.6) | collective-permute-done | bytes 32800 | tf_op jit(solution)/shard_map/ppermute | solution.py:430
  19.6 0.2 shard_map.159
  19.9 1.9 %collective-permute-start.8 = (f32[64,128]{1,0:T(8,128)S(1)}, f32[64,128]{1,0:T(8,128)S(1)}, u32[]{:S(2)}, u32[]{:S(2)}) collective-permute-start(f32[64,128]{1,0:T(8,128)S(1)} %get-tuple-element.99), channel_id=1, source_target_pairs={{0,8},{1,2},{2,1},{3,4},{4,3},{5,6},{6,5},{7,15},{8,0},{9,10},{10,... | collective-permute-start | bytes 98312 | tf_op jit(solution)/shard_map/ppermute | solution.py:430
  22.0 0.5 %shard_map.161 = (f32[64,512]{1,0:T(8,128)S(1)}, f32[64,512]{1,0:T(8,128)S(1)}, f32[64,512]{1,0:T(8,128)S(1)}, f32[8,512]{1,0:T(8,128)S(1)}) custom-call(f32[64,640]{1,0:T(8,128)S(1)} %get-tuple-element.100.flow_ref, f32[64,512]{1,0:T(8,128)S(1)} %get-tuple-element.102.x_ref, f32[8,512]{1,0:T(8,128)S(1)} %get-tuple-element.80.count_ref, ...), custom_call_target="tpu_custom_call" | custom-call | flops 83886080 | bytes 1982464 | tf_op jit(solution)/shard_map/pallas_call | solution.py:374
  22.5 1.3 %collective-permute-done.8 = f32[64,128]{1,0:T(8,128)S(1)} collective-permute-done((f32[64,128]{1,0:T(8,128)S(1)}, f32[64,128]{1,0:T(8,128)S(1)}, u32[]{:S(2)}, u32[]{:S(2)}) %collective-permute-start.8) | collective-permute-done | bytes 32800 | tf_op jit(solution)/shard_map/ppermute | solution.py:430
  24.0 1.8 %collective-permute-start.10 = (f32[8,512]{1,0:T(8,128)S(1)}, f32[8,512]{1,0:T(8,128)S(1)}, u32[]{:S(2)}, u32[]{:S(2)}) collective-permute-start(f32[8,512]{1,0:T(8,128)S(1)} %get-tuple-element.119.refs_0_), channel_id=1, source_target_pairs={{0,8},{8,16},{16,24},{24,0},{1,9},{9,17},{17,25},{25,1},{2,10},{10... | collective-permute-start | bytes 49160 | tf_op jit(solution)/shard_map/ppermute | solution.py:560
  25.9 1.5 %collective-permute-start.11 = (f32[8,512]{1,0:T(8,128)S(1)}, f32[8,512]{1,0:T(8,128)S(1)}, u32[]{:S(2)}, u32[]{:S(2)}) collective-permute-start(f32[8,512]{1,0:T(8,128)S(1)} %get-tuple-element.119.refs_0_), channel_id=1, source_target_pairs={{0,16},{8,24},{16,0},{24,8},{1,17},{9,25},{17,1},{25,9},{2,18},{10... | collective-permute-start | bytes 49160 | tf_op jit(solution)/shard_map/ppermute | solution.py:560
  27.4 1.4 %collective-permute-start.12 = (f32[8,512]{1,0:T(8,128)S(1)}, f32[8,512]{1,0:T(8,128)S(1)}, u32[]{:S(2)}, u32[]{:S(2)}) collective-permute-start(f32[8,512]{1,0:T(8,128)S(1)} %get-tuple-element.119.refs_0_), channel_id=1, source_target_pairs={{0,24},{8,0},{16,8},{24,16},{1,25},{9,1},{17,9},{25,17},{2,26},{10... | collective-permute-start | bytes 49160 | tf_op jit(solution)/shard_map/ppermute | solution.py:560
  28.8 0.9 %shard_map.163 = (f32[64,512]{1,0:T(8,128)}, f32[64,512]{1,0:T(8,128)S(1)}) custom-call(f32[64,256]{1,0:T(8,128)S(1)} %get-tuple-element.113.both_ref, f32[64,256]{1,0:T(8,128)S(1)} %get-tuple-element.114.z_ref, f32[8,256]{1,0:T(8,128)S(1)} %get-tuple-element.87.degree_ref, bf16[512,256]{1,0:T(8,128)(2,1)S(1)} %get-tuple-element.101.own_ref, ...), custom_call_target="tpu_custom_call" | custom-call | flops 83886080 | bytes 811008 | tf_op jit(solution)/shard_map/pallas_call | solution.py:374
  29.7 1.4 %collective-permute-done.12.refs_3_ = f32[8,512]{1,0:T(8,128)S(1)} collective-permute-done((f32[8,512]{1,0:T(8,128)S(1)}, f32[8,512]{1,0:T(8,128)S(1)}, u32[]{:S(2)}, u32[]{:S(2)}) %collective-permute-start.12) | collective-permute-done | bytes 16416 | tf_op jit(solution)/shard_map/ppermute | solution.py:560
  31.1 0.7 %shard_map.164 = (f32[64,512]{1,0:T(8,128)}, f32[1,512]{1,0:T(1,128)}) custom-call(f32[8,512]{1,0:T(8,128)S(1)} %get-tuple-element.119.refs_0_, f32[8,512]{1,0:T(8,128)S(1)} %collective-permute-done.10.refs_1_, f32[8,512]{1,0:T(8,128)S(1)} %collective-permute-done.11.refs_2_, f32[8,512]{1,0:T(8,128)S(1)} %collective-permute-done.12.refs_3_, ...), custom_call_target="tpu_custom_call" | custom-call | flops 83886080 | bytes 212992 | tf_op jit(solution)/shard_map/pallas_call | solution.py:374
  (27 shorter events, 1.8 us)
Async XLA Ops:
  1.8 5.1 %collective-permute-start = (f32[64,128]{1,0:T(8,128)S(1)}, f32[64,128]{1,0:T(8,128)S(1)}, u32[]{:S(2)}, u32[]{:S(2)}) collective-permute-start(f32[64,128]{1,0:T(8,128)S(1)} %get-tuple-element.63), channel_id=1, source_target_pairs={{0,8},{1,2},{2,1},{3,4},{4,3},{5,6},{6,5},{7,15},{8,0},{9,10},{10,... | collective-permute-start | bytes 98312 | tf_op jit(solution)/shard_map/ppermute | solution.py:430
  4.8 2.1 %collective-permute-start.1 = (f32[64,128]{1,0:T(8,128)S(1)}, f32[64,128]{1,0:T(8,128)S(1)}, u32[]{:S(2)}, u32[]{:S(2)}) collective-permute-start(f32[64,128]{1,0:T(8,128)S(1)} %get-tuple-element.64.pick1_ref), channel_id=1, source_target_pairs={{0,1},{1,0},{2,3},{3,2},{4,5},{5,4},{6,7},{7,6},{8,9},{9,8},{10,11... | collective-permute-start | bytes 98312 | tf_op jit(solution)/shard_map/ppermute | solution.py:427
  7.1 4.0 %collective-permute-start.2 = (f32[72,128]{1,0:T(8,128)S(1)}, f32[72,128]{1,0:T(8,128)S(1)}, u32[]{:S(2)}, u32[]{:S(2)}) collective-permute-start(f32[72,128]{1,0:T(8,128)S(1)} %get-tuple-element.75), channel_id=1, source_target_pairs={{0,8},{1,2},{2,1},{3,4},{4,3},{5,6},{6,5},{7,15},{8,0},{9,10},{10,... | collective-permute-start | bytes 110600 | tf_op jit(solution)/shard_map/ppermute | solution.py:430
  9.2 2.0 %collective-permute-start.3 = (f32[72,128]{1,0:T(8,128)S(1)}, f32[72,128]{1,0:T(8,128)S(1)}, u32[]{:S(2)}, u32[]{:S(2)}) collective-permute-start(f32[72,128]{1,0:T(8,128)S(1)} %shard_map.151.send1_ref), channel_id=1, source_target_pairs={{0,1},{1,0},{2,3},{3,2},{4,5},{5,4},{6,7},{7,6},{8,9},{9,8},{10,11... | collective-permute-start | bytes 110600 | tf_op jit(solution)/shard_map/ppermute | solution.py:427
  11.4 4.0 %collective-permute-start.4 = (f32[64,128]{1,0:T(8,128)S(1)}, f32[64,128]{1,0:T(8,128)S(1)}, u32[]{:S(2)}, u32[]{:S(2)}) collective-permute-start(f32[64,128]{1,0:T(8,128)S(1)} %get-tuple-element.84), channel_id=1, source_target_pairs={{0,8},{1,2},{2,1},{3,4},{4,3},{5,6},{6,5},{7,15},{8,0},{9,10},{10,... | collective-permute-start | bytes 98312 | tf_op jit(solution)/shard_map/ppermute | solution.py:430
  13.5 1.9 %collective-permute-start.5 = (f32[64,128]{1,0:T(8,128)S(1)}, f32[64,128]{1,0:T(8,128)S(1)}, u32[]{:S(2)}, u32[]{:S(2)}) collective-permute-start(f32[64,128]{1,0:T(8,128)S(1)} %shard_map.154.send1_ref), channel_id=1, source_target_pairs={{0,1},{1,0},{2,3},{3,2},{4,5},{5,4},{6,7},{7,6},{8,9},{9,8},{10,11... | collective-permute-start | bytes 98312 | tf_op jit(solution)/shard_map/ppermute | solution.py:427
  15.6 4.0 %collective-permute-start.6 = (f32[64,128]{1,0:T(8,128)S(1)}, f32[64,128]{1,0:T(8,128)S(1)}, u32[]{:S(2)}, u32[]{:S(2)}) collective-permute-start(f32[64,128]{1,0:T(8,128)S(1)} %get-tuple-element.92), channel_id=1, source_target_pairs={{0,8},{1,2},{2,1},{3,4},{4,3},{5,6},{6,5},{7,15},{8,0},{9,10},{10,... | collective-permute-start | bytes 98312 | tf_op jit(solution)/shard_map/ppermute | solution.py:430
  17.7 1.9 %collective-permute-start.7 = (f32[64,128]{1,0:T(8,128)S(1)}, f32[64,128]{1,0:T(8,128)S(1)}, u32[]{:S(2)}, u32[]{:S(2)}) collective-permute-start(f32[64,128]{1,0:T(8,128)S(1)} %shard_map.157.send1_ref), channel_id=1, source_target_pairs={{0,1},{1,0},{2,3},{3,2},{4,5},{5,4},{6,7},{7,6},{8,9},{9,8},{10,11... | collective-permute-start | bytes 98312 | tf_op jit(solution)/shard_map/ppermute | solution.py:427
  19.9 4.0 %collective-permute-start.8 = (f32[64,128]{1,0:T(8,128)S(1)}, f32[64,128]{1,0:T(8,128)S(1)}, u32[]{:S(2)}, u32[]{:S(2)}) collective-permute-start(f32[64,128]{1,0:T(8,128)S(1)} %get-tuple-element.99), channel_id=1, source_target_pairs={{0,8},{1,2},{2,1},{3,4},{4,3},{5,6},{6,5},{7,15},{8,0},{9,10},{10,... | collective-permute-start | bytes 98312 | tf_op jit(solution)/shard_map/ppermute | solution.py:430
  21.9 1.9 %collective-permute-start.9 = (f32[64,128]{1,0:T(8,128)S(1)}, f32[64,128]{1,0:T(8,128)S(1)}, u32[]{:S(2)}, u32[]{:S(2)}) collective-permute-start(f32[64,128]{1,0:T(8,128)S(1)} %shard_map.160.send1_ref), channel_id=1, source_target_pairs={{0,1},{1,0},{2,3},{3,2},{4,5},{5,4},{6,7},{7,6},{8,9},{9,8},{10,11... | collective-permute-start | bytes 98312 | tf_op jit(solution)/shard_map/ppermute | solution.py:427
  24.0 5.7 %collective-permute-start.10 = (f32[8,512]{1,0:T(8,128)S(1)}, f32[8,512]{1,0:T(8,128)S(1)}, u32[]{:S(2)}, u32[]{:S(2)}) collective-permute-start(f32[8,512]{1,0:T(8,128)S(1)} %get-tuple-element.119.refs_0_), channel_id=1, source_target_pairs={{0,8},{8,16},{16,24},{24,0},{1,9},{9,17},{17,25},{25,1},{2,10},{10... | collective-permute-start | bytes 49160 | tf_op jit(solution)/shard_map/ppermute | solution.py:560
  25.9 3.9 %collective-permute-start.11 = (f32[8,512]{1,0:T(8,128)S(1)}, f32[8,512]{1,0:T(8,128)S(1)}, u32[]{:S(2)}, u32[]{:S(2)}) collective-permute-start(f32[8,512]{1,0:T(8,128)S(1)} %get-tuple-element.119.refs_0_), channel_id=1, source_target_pairs={{0,16},{8,24},{16,0},{24,8},{1,17},{9,25},{17,1},{25,9},{2,18},{10... | collective-permute-start | bytes 49160 | tf_op jit(solution)/shard_map/ppermute | solution.py:560
  27.4 3.7 %collective-permute-start.12 = (f32[8,512]{1,0:T(8,128)S(1)}, f32[8,512]{1,0:T(8,128)S(1)}, u32[]{:S(2)}, u32[]{:S(2)}) collective-permute-start(f32[8,512]{1,0:T(8,128)S(1)} %get-tuple-element.119.refs_0_), channel_id=1, source_target_pairs={{0,24},{8,0},{16,8},{24,16},{1,25},{9,1},{17,9},{25,17},{2,26},{10... | collective-permute-start | bytes 49160 | tf_op jit(solution)/shard_map/ppermute | solution.py:560

commit v6 on v5

--- a/solution.py
+++ b/solution.py
@@ -54,7 +54,7 @@
 
 def load_kernel(count, *refs):
     sources, targets = refs[:count], refs[count : 2 * count]
-    pick1_ref, pick2_ref, own_ref, semaphores = refs[2 * count :]
+    pick1_ref, pick2_ref, semaphores = refs[2 * count :]
     copies = fetch(sources, targets, semaphores)
     halo_ref, theta_ref = targets[:2]
     buses = theta_ref.shape[1]
@@ -63,7 +63,6 @@
     ids = column_ids(halo_ref[...], buses)
     rows = lax.broadcasted_iota(jnp.int32, (buses, ids.shape[1]), 0)
     table = jnp.where(rows == ids, 1.0, 0.0).astype(BF16)
-    own_ref[...] = table
     copies[1].wait()
     pick = times(theta_ref[...], table)
     pick1_ref[...] = pick[:, :slots]
@@ -88,6 +87,8 @@
     stiff_ref,
     dual_ref,
     edge_ref,
+    edge_t_ref,
+    own_t_ref,
     inner_ref,
     gain_ref,
     x_ref,
@@ -119,7 +120,11 @@
     edges = ids.shape[1]
     lanes = lax.broadcasted_iota(jnp.int32, (edges, buses), 1)
     ids_col = jnp.broadcast_to(ids, (edges, edges)).T[:, :1]
-    inner = 1.0 - jnp.max(jnp.where(lanes == ids_col, 1.0, 0.0), axis=0, keepdims=True)
+    own = jnp.where(lanes == ids_col, 1.0, 0.0)
+    own_t_ref[...] = own.astype(BF16)
+    inner = 1.0 - jnp.max(own, axis=0, keepdims=True)
+    starts = jnp.where(ids_col == from_ref[...], 1.0, 0.0)
+    edge_t_ref[...] = (starts - jnp.where(ids_col == to_ref[...], 1.0, 0.0)).astype(BF16)
     bus_ids = lax.broadcasted_iota(jnp.int32, (1, buses), 1)
     inner_ids = jnp.where(inner > 0.0, bus_ids, -1)
     all_ids = jnp.concatenate([ids, inner_ids], axis=1)
@@ -153,26 +158,30 @@
         rows_ref[2 * index : 2 * index + 2, :] = jnp.broadcast_to(ref[...], (2, buses))
 
 
-def gap_step(z, scale, edge_ref, p_ref, c_ref, gain_ref, flow_ref, send_ref, deltas):
+def has_far():
+    place, places = lax.axis_index("net"), lax.axis_size("net")
+    return jnp.where(place % 2 == 0, place > 0, place < places - 1)
+
+
+def gaps(moved, scale, p_ref, c_ref, gain_ref, flow_ref, deltas):
+    for delta_ref in deltas:
+        delta_ref[...] = p_ref[...] + moved
+    flow = gain_ref[...] * (c_ref[...] + scale * moved)
+    flow_ref[...] = flow
+    return flow
+
+
+def gap_step(z, scale, edge_ref, turned_ref, p_ref, c_ref, gain_ref, flow_ref, send_ref, deltas):
     conts, slots = z.shape[0], send_ref.shape[1]
-    place, places = lax.axis_index("net"), lax.axis_size("net")
-    has_far = jnp.where(place % 2 == 0, place > 0, place < places - 1)
-
-    def finish(moved):
-        for delta_ref in deltas:
-            delta_ref[...] = p_ref[...] + moved
-        flow = gain_ref[...] * (c_ref[...] + scale * moved)
-        flow_ref[...] = flow
-        return flow
-
-    @pl.when(has_far)
+
+    @pl.when(has_far())
     def _():
-        flow = finish(times_t(z, edge_ref[...]))
+        moved = times(z, turned_ref[...])
+        flow = gaps(moved, scale, p_ref, c_ref, gain_ref, flow_ref, deltas)
         send_ref[:conts, :] = times(flow, edge_ref[:, slots:])
 
-    @pl.when(jnp.logical_not(has_far))
+    @pl.when(jnp.logical_not(has_far()))
     def _():
-        finish(times_t(z[:, :slots], edge_ref[:, :slots]))
         send_ref[:conts, :] = jnp.zeros((conts, slots), F32)
 
 
@@ -181,6 +190,7 @@
     got1_ref,
     pick1_ref,
     edge_ref,
+    turned_ref,
     p_ref,
     c_ref,
     gain_ref,
@@ -194,7 +204,7 @@
     conts = p_ref.shape[0]
     z = jnp.concatenate([pick1_ref[...] + got1_ref[...], far_ref[...]], axis=1)
     z_ref[...] = z
-    gap_step(z, 1.0, edge_ref, p_ref, c_ref, gain_ref, flow_ref, send_ref, [delta_ref])
+    gap_step(z, 1.0, edge_ref, turned_ref, p_ref, c_ref, gain_ref, flow_ref, send_ref, [delta_ref])
     send_ref[conts:, :] = count_ref[:, slots:]
 
 
@@ -205,18 +215,18 @@
 
 
 def round_step(
-    far_ref, got1_ref, send1_ref, z_ref, degree, edge_ref, p_ref, c_ref, gain_ref, outs
+    far_ref, got1_ref, send1_ref, z_ref, degree, edge_ref, turned_ref, p_ref, c_ref, gain_ref, outs
 ):
     both_ref, z_out_ref, flow_ref, out_ref, *deltas = outs
     both = both_ends(far_ref, got1_ref, send1_ref, slice(0, z_ref.shape[0]))
     both_ref[...] = both
     z = (degree * z_ref[...] - both) / (degree + 1.0)
     z_out_ref[...] = z
-    gap_step(z, 2.0, edge_ref, p_ref, c_ref, gain_ref, flow_ref, out_ref, deltas)
+    gap_step(z, 2.0, edge_ref, turned_ref, p_ref, c_ref, gain_ref, flow_ref, out_ref, deltas)
 
 
 def second_kernel(
-    far_ref, got1_ref, send1_ref, z_ref, edge_ref, p_ref, c_ref, gain_ref, *outs
+    far_ref, got1_ref, send1_ref, z_ref, edge_ref, turned_ref, p_ref, c_ref, gain_ref, *outs
 ):
     *outs, degree_ref = outs
     rows = slice(z_ref.shape[0], send1_ref.shape[0])
@@ -229,6 +239,7 @@
         z_ref,
         degree[:1, :],
         edge_ref,
+        turned_ref,
         p_ref,
         c_ref,
         gain_ref,
@@ -243,6 +254,7 @@
     z_ref,
     degree_ref,
     edge_ref,
+    turned_ref,
     p_ref,
     c_ref,
     gain_ref,
@@ -255,6 +267,7 @@
         z_ref,
         degree_ref[:1, :],
         edge_ref,
+        turned_ref,
         p_ref,
         c_ref,
         gain_ref,
@@ -262,10 +275,24 @@
     )
 
 
-def send_kernel(flow_ref, edge_ref, *refs):
-    *counts, send_ref = refs
-    conts, slots = flow_ref.shape[0], send_ref.shape[1]
-    send_ref[:conts, :] = times(flow_ref[...], edge_ref[:, :slots])
+def send_kernel(scale, number, *refs):
+    z_ref, edge_ref, turned_ref, p_ref, c_ref, gain_ref, flow_in_ref = refs[:7]
+    counts = refs[6 + number : -1 - number]
+    outs = refs[-1 - number : -1]
+    send_ref = refs[-1]
+    conts, slots = z_ref.shape[0], send_ref.shape[1]
+    table = edge_ref[:, :slots]
+
+    @pl.when(has_far())
+    def _():
+        send_ref[:conts, :] = times(flow_in_ref[...], table)
+
+    @pl.when(jnp.logical_not(has_far()))
+    def _():
+        moved = times(z_ref[:, :slots], turned_ref[:slots, :])
+        flow = gaps(moved, scale, p_ref, c_ref, gain_ref, outs[0], outs[1:])
+        send_ref[:conts, :] = times(flow, table)
+
     for ref in counts:
         send_ref[conts:, :] = ref[:, :slots]
 
@@ -305,7 +332,7 @@
     x_out_ref[...] = x
     conts = net.shape[0]
     edge = jnp.concatenate([ref[...] for ref in refs[:rounds]], axis=0)
-    spread = times_t(edge, own_ref[...])
+    spread = times(edge, own_ref[...])
     part = 1.0 / (rows_ref[4:5, :] + PENALTY + BALANCE)
     dual = dual_ref[...]
     sums_ref[0:1, :] = dsum_ref[:1, :]
@@ -328,7 +355,7 @@
     row = jnp.broadcast_to(jnp.sum(both, axis=0, keepdims=True), (8, both.shape[1]))
     sums_ref[...] = sums_in_ref[...]
     last = slice(ROUNDS, ROUNDS + 1)
-    sums_ref[last, :] = sums_in_ref[last, :] + times_t(row, own_ref[...])[:1]
+    sums_ref[last, :] = sums_in_ref[last, :] + times(row, own_ref[...])[:1]
 
 
 def field_kernel(
@@ -338,7 +365,7 @@
     both = both_ref[...]
     degree = degree_ref[:1, :]
     z = (degree * z_ref[...] - both) / (degree + 1.0)
-    spread = times_t(jnp.concatenate([both, z], axis=0), own_ref[...])
+    spread = times(jnp.concatenate([both, z], axis=0), own_ref[...])
     theta_ref[...] = x_ref[...] + spread[conts:]
     part = 1.0 / (rows_ref[4:5, :] + PENALTY + BALANCE)
     gen_ref[...] = part * (BALANCE * (net_ref[...] + spread[:conts]) - dual_ref[...])
@@ -367,7 +394,7 @@
     base_out_ref[...] = base
 
 
-def call(kernel, outs, *args, scratch=(), spaces=None, flops=2 * 128 * 640 * 512):
+def call(kernel, outs, *args, scratch=(), spaces=None, aliases=None, flops=2 * 128 * 640 * 512):
     shapes = [jax.ShapeDtypeStruct(shape, dtype) for shape, dtype in outs]
     moved = sum(a.size * a.dtype.itemsize for a in args)
     spaces = spaces or [pltpu.VMEM] * len(args)
@@ -377,6 +404,7 @@
         in_specs=[pl.BlockSpec(memory_space=space) for space in spaces],
         out_specs=[pl.BlockSpec(memory_space=pltpu.VMEM)] * len(outs),
         scratch_shapes=list(scratch),
+        input_output_aliases=aliases or {},
         compiler_params=pltpu.CompilerParams(vmem_limit_bytes=32 * 1024 * 1024),
         cost_estimate=pl.CostEstimate(flops=flops, bytes_accessed=moved, transcendentals=0),
     )(*args)
@@ -446,9 +474,9 @@
     def load(*refs):
         load_kernel(number, *refs)
 
-    *here, pick1, pick2, own = call(
+    *here, pick1, pick2 = call(
         load,
-        [(a.shape, a.dtype) for a in fetched] + [half, half, ((buses, edges), BF16)],
+        [(a.shape, a.dtype) for a in fetched] + [half, half],
         *in_hbm(*fetched),
         spaces=[pltpu.HBM] * number,
         scratch=[pltpu.SemaphoreType.DMA((number,))],
@@ -463,6 +491,8 @@
     (
         gen_dual,
         edge_table,
+        edge_turned,
+        own,
         inner_table,
         gain,
         x,
@@ -477,6 +507,8 @@
         [
             bus,
             ((branches, edges), BF16),
+            ((edges, branches), BF16),
+            ((edges, buses), BF16),
             ((branches, buses), BF16),
             branch,
             bus,
@@ -501,17 +533,31 @@
         got1,
         pick1,
         edge_table,
+        edge_turned,
         p,
         c,
         gain,
         count_edge,
     )
     nets, boths = [], []
+
+    def make_near(first, held, z, p, c, counts):
+        def kernel(*refs):
+            send_kernel(1.0 if first else 2.0, len(held), *refs)
+
+        args = [z, edge_table, edge_turned, p, c, gain, *held, *counts]
+        return call(
+            kernel,
+            [branch] * len(held) + [tall if first else half],
+            *args,
+            aliases={6 + index: index for index in range(len(held))},
+        )
+
     for index in range(1, ROUNDS):
         first = index == 1
         got2 = trade_far(send2)
         counts = [count_edge] if first else []
-        (send1,) = call(send_kernel, [tall if first else half], flow, edge_table, *counts)
+        flow, delta, send1 = make_near(first, [flow, delta], z, p, c, counts)
         got1 = trade_near(send1)
         net, x, p, c = call(
             beside_kernel,
@@ -527,7 +573,7 @@
         if index < ROUNDS - 1:
             outs = outs + [branch]
         ends = [send2 + got2, got1, send1, z]
-        tables = [edge_table, p, c, gain]
+        tables = [edge_table, edge_turned, p, c, gain]
         if first:
             both, z, flow, send2, *deltas, degree = call(
                 second_kernel, outs + [((8, edges), F32)], *ends, *tables
@@ -537,7 +583,7 @@
         delta = deltas[0] if deltas else None
         boths.append(both)
     got2 = trade_far(send2)
-    (send1,) = call(send_kernel, [half], flow, edge_table)
+    flow, send1 = make_near(False, [flow], z, p, c, [])
     got1 = trade_near(send1)
     net, x, dual, sums = call(
         beside_last_kernel,
@@ -555,7 +601,7 @@
     )
     both, sums = call(total_kernel, [edge, row], send2 + got2, got1, send1, own, sums)
     parts = [sums]
-    for shift in range(1, cont_size):
+    for shift in reversed(range(1, cont_size)):
         parts.append(
             lax.ppermute(sums, "cont", [(i, (i + shift) % cont_size) for i in range(cont_size)])
         )

time: 32 us -> 31.2 us (0.975)
  starting transfers between devices: 15.9 us -> 15.3 us
    ppermute x5, starting transfers between devices: 10.5 us -> 9.99 us  [trade_far(): return lax.ppermute(value, axes, swap2)]
  transfers between devices with their start and end apart: 13 -> 13, of which waited for: 5 -> 5; matrix products, arithmetic and copies ran while one was open for 0% -> 0% of each run, Pallas kernels for 18% -> 21%
where the time goes in v6:
time: 31.2 us; the launch traced here: 31 us
  starting transfers between devices  15.3 us (49%)
  Pallas kernels  8.58 us (28%)
  waiting for transfers between devices  6.33 us (20%)
  between operations  0.78 us (2%)
    ppermute x5, starting transfers between devices, trade_far(): return lax.ppermute(value, axes, swap2)  9.99 us
    pallas_call x17, Pallas kernels, call(): pl.pallas_call(kernel, out_shape=shapes, in_specs=[pl.BlockSpec(memory_sp...  8.58 us
    ppermute x5, waiting for transfers between devices, trade_far(): return lax.ppermute(value, axes, swap2)  4.9 us
    ppermute x3, starting transfers between devices, local(): lax.ppermute(sums, 'cont', [(i, (i + shift) % cont_size) for i in range(c...  4.64 us
    ppermute x3, waiting for transfers between devices, local(): lax.ppermute(sums, 'cont', [(i, (i + shift) % cont_size) for i in range(c...  1.41 us
    ppermute x5, starting transfers between devices, trade_near(): return lax.ppermute(value, axes, swap1)  0.66 us
  transfers between devices with their start and end apart: 13, of which 5 were waited for; matrix products, arithmetic and copies ran while one was open for 0% of the time, Pallas kernels for 21%

profile of v6, /device:TPU:0, one launch (start us, length us, event | category | flops | bytes accessed | tf_op | source)
XLA Modules:
  0.0 31.0 jit_solution(17414809390363484081)
XLA Ops:
  0.6 1.1 %shard_map.148 = (s32[1,128]{1,0:T(1,128)S(1)}, f32[64,512]{1,0:T(8,128)S(1)}, s32[640]{0:T(1024)S(1)}, s32[640]{0:T(1024)S(1)}, f32[640]{0:T(1024)S(1)}, /*index=5*/f32[64,128]{1,0:T(8,128)S(1)}, f32[64,128]{1,0:T(8,128)S(1)}) custom-call(s32[1,128]{1,0:T(1,128)} %bitcast.10, f32[64,512]{1,0:T(8,128)} %refs_1_.1, s32[640]{0:T(1024)} %refs_2_.1, ...), custom_call_target="tpu_custom_call" | custom-call | flops 83886080 | bytes 139264 | tf_op jit(solution)/shard_map/pallas_call | solution.py:401
  1.8 3.0 %collective-permute-start = (f32[64,128]{1,0:T(8,128)S(1)}, f32[64,128]{1,0:T(8,128)S(1)}, u32[]{:S(2)}, u32[]{:S(2)}) collective-permute-start(f32[64,128]{1,0:T(8,128)S(1)} %get-tuple-element.75), channel_id=1, source_target_pairs={{0,8},{1,2},{2,1},{3,4},{4,3},{5,6},{6,5},{7,15},{8,0},{9,10},{10,... | collective-permute-start | bytes 98312 | tf_op jit(solution)/shard_map/ppermute | solution.py:458
  5.0 2.0 %shard_map.149 = (f32[64,512]{1,0:T(8,128)S(1)}, bf16[640,256]{1,0:T(8,128)(2,1)S(1)}, bf16[256,640]{1,0:T(8,128)(2,1)S(1)}, bf16[256,512]{1,0:T(8,128)(2,1)S(1)...) custom-call(f32[64,640]{1,0:T(8,128)} %lam_f_hbm.1, ...), custom_call_target="tpu_custom_call" | custom-call | flops 83886080 | bytes 770048 | tf_op jit(solution)/shard_map/pallas_call | solution.py:401
  7.1 1.7 %collective-permute-start.2 = (f32[72,128]{1,0:T(8,128)S(1)}, f32[72,128]{1,0:T(8,128)S(1)}, u32[]{:S(2)}, u32[]{:S(2)}) collective-permute-start(f32[72,128]{1,0:T(8,128)S(1)} %get-tuple-element.88), channel_id=1, source_target_pairs={{0,8},{1,2},{2,1},{3,4},{4,3},{5,6},{6,5},{7,15},{8,0},{9,10},{10,... | collective-permute-start | bytes 110600 | tf_op jit(solution)/shard_map/ppermute | solution.py:458
  8.8 0.4 %shard_map.151 = (f32[64,640]{1,0:T(8,128)S(1)}, f32[64,640]{1,0:T(8,128)S(1)}, f32[72,128]{1,0:T(8,128)S(1)}) custom-call(f32[64,256]{1,0:T(8,128)S(1)} %get-tuple-element.89.refs_0_.z_ref, bf16[640,256]{1,0:T(8,128)(2,1)S(1)} %get-tuple-element.82.edge_ref.refs_1_, ...), custom_call_target="tpu_custom_call", output_to_operand_aliasing={{0}: (6, {}), {1}: (7, {})} | custom-call | flops 83886080 | bytes 1548288 | tf_op jit(solution)/shard_map/pallas_call | solution.py:401
  9.5 0.5 %shard_map.152 = (f32[64,512]{1,0:T(8,128)S(1)}, f32[64,512]{1,0:T(8,128)S(1)}, f32[64,640]{1,0:T(8,128)S(1)}, f32[64,640]{1,0:T(8,128)S(1)}) custom-call(f32[64,640]{1,0:T(8,128)S(1)} %get-tuple-element.93.flow_ref, f32[64,640]{1,0:T(8,128)S(1)} %get-tuple-element.94.delta_ref, f32[64,512]{1,0:T(8,128)S(1)} %get-tuple-element.95.x_ref, ...), custom_call_target="tpu_custom_call" | custom-call | flops 83886080 | bytes 1130496 | tf_op jit(solution)/shard_map/pallas_call | solution.py:401
  10.0 1.1 %collective-permute-done.2 = f32[72,128]{1,0:T(8,128)S(1)} collective-permute-done((f32[72,128]{1,0:T(8,128)S(1)}, f32[72,128]{1,0:T(8,128)S(1)}, u32[]{:S(2)}, u32[]{:S(2)}) %collective-permute-start.2) | collective-permute-done | bytes 36896 | tf_op jit(solution)/shard_map/ppermute | solution.py:458
  11.1 1.7 %collective-permute-start.4 = (f32[64,128]{1,0:T(8,128)S(1)}, f32[64,128]{1,0:T(8,128)S(1)}, u32[]{:S(2)}, u32[]{:S(2)}) collective-permute-start(f32[64,128]{1,0:T(8,128)S(1)} %get-tuple-element.100), channel_id=1, source_target_pairs={{0,8},{1,2},{2,1},{3,4},{4,3},{5,6},{6,5},{7,15},{8,0},{9,10},{10,... | collective-permute-start | bytes 98312 | tf_op jit(solution)/shard_map/ppermute | solution.py:458
  12.9 0.4 %shard_map.154 = (f32[64,640]{1,0:T(8,128)S(1)}, f32[64,640]{1,0:T(8,128)S(1)}, f32[64,128]{1,0:T(8,128)S(1)}) custom-call(f32[64,256]{1,0:T(8,128)S(1)} %get-tuple-element.101.refs_0_.z_ref, bf16[640,256]{1,0:T(8,128)(2,1)S(1)} %get-tuple-element.82.edge_ref.refs_1_, ...), custom_call_target="tpu_custom_call", output_to_operand_aliasing={{0}: (6, {}), {1}: (7, {})} | custom-call | flops 83886080 | bytes 1540096 | tf_op jit(solution)/shard_map/pallas_call | solution.py:401
  13.3 0.5 %shard_map.155 = (f32[64,512]{1,0:T(8,128)S(1)}, f32[64,512]{1,0:T(8,128)S(1)}, f32[64,640]{1,0:T(8,128)S(1)}, f32[64,640]{1,0:T(8,128)S(1)}) custom-call(f32[64,640]{1,0:T(8,128)S(1)} %get-tuple-element.106.flow_ref, f32[64,640]{1,0:T(8,128)S(1)} %get-tuple-element.107.delta_ref, f32[64,512]{1,0:T(8,128)S(1)} %get-tuple-element.108.x_ref, ...), custom_call_target="tpu_custom_call" | custom-call | flops 83886080 | bytes 1130496 | tf_op jit(solution)/shard_map/pallas_call | solution.py:401
  13.9 1.2 %collective-permute-done.4 = f32[64,128]{1,0:T(8,128)S(1)} collective-permute-done((f32[64,128]{1,0:T(8,128)S(1)}, f32[64,128]{1,0:T(8,128)S(1)}, u32[]{:S(2)}, u32[]{:S(2)}) %collective-permute-start.4) | collective-permute-done | bytes 32800 | tf_op jit(solution)/shard_map/ppermute | solution.py:458
  15.2 1.7 %collective-permute-start.6 = (f32[64,128]{1,0:T(8,128)S(1)}, f32[64,128]{1,0:T(8,128)S(1)}, u32[]{:S(2)}, u32[]{:S(2)}) collective-permute-start(f32[64,128]{1,0:T(8,128)S(1)} %get-tuple-element.111), channel_id=1, source_target_pairs={{0,8},{1,2},{2,1},{3,4},{4,3},{5,6},{6,5},{7,15},{8,0},{9,10},{10,... | collective-permute-start | bytes 98312 | tf_op jit(solution)/shard_map/ppermute | solution.py:458
  16.9 0.4 %shard_map.157 = (f32[64,640]{1,0:T(8,128)S(1)}, f32[64,640]{1,0:T(8,128)S(1)}, f32[64,128]{1,0:T(8,128)S(1)}) custom-call(f32[64,256]{1,0:T(8,128)S(1)} %get-tuple-element.112.refs_0_.z_ref, bf16[640,256]{1,0:T(8,128)(2,1)S(1)} %get-tuple-element.82.edge_ref.refs_1_, ...), custom_call_target="tpu_custom_call", output_to_operand_aliasing={{0}: (6, {}), {1}: (7, {})} | custom-call | flops 83886080 | bytes 1540096 | tf_op jit(solution)/shard_map/pallas_call | solution.py:401
  17.4 0.5 %shard_map.158 = (f32[64,512]{1,0:T(8,128)S(1)}, f32[64,512]{1,0:T(8,128)S(1)}, f32[64,640]{1,0:T(8,128)S(1)}, f32[64,640]{1,0:T(8,128)S(1)}) custom-call(f32[64,640]{1,0:T(8,128)S(1)} %get-tuple-element.116.flow_ref, f32[64,640]{1,0:T(8,128)S(1)} %get-tuple-element.117.delta_ref, f32[64,512]{1,0:T(8,128)S(1)} %get-tuple-element.118.x_ref, ...), custom_call_target="tpu_custom_call" | custom-call | flops 83886080 | bytes 1130496 | tf_op jit(solution)/shard_map/pallas_call | solution.py:401
  17.9 1.2 %collective-permute-done.6 = f32[64,128]{1,0:T(8,128)S(1)} collective-permute-done((f32[64,128]{1,0:T(8,128)S(1)}, f32[64,128]{1,0:T(8,128)S(1)}, u32[]{:S(2)}, u32[]{:S(2)}) %collective-permute-start.6) | collective-permute-done | bytes 32800 | tf_op jit(solution)/shard_map/ppermute | solution.py:458
  19.2 1.7 %collective-permute-start.8 = (f32[64,128]{1,0:T(8,128)S(1)}, f32[64,128]{1,0:T(8,128)S(1)}, u32[]{:S(2)}, u32[]{:S(2)}) collective-permute-start(f32[64,128]{1,0:T(8,128)S(1)} %get-tuple-element.121), channel_id=1, source_target_pairs={{0,8},{1,2},{2,1},{3,4},{4,3},{5,6},{6,5},{7,15},{8,0},{9,10},{10,... | collective-permute-start | bytes 98312 | tf_op jit(solution)/shard_map/ppermute | solution.py:458
  21.4 0.4 %shard_map.161 = (f32[64,512]{1,0:T(8,128)S(1)}, f32[64,512]{1,0:T(8,128)S(1)}, f32[64,512]{1,0:T(8,128)S(1)}, f32[8,512]{1,0:T(8,128)S(1)}) custom-call(f32[64,640]{1,0:T(8,128)S(1)} %get-tuple-element.126.flow_ref, f32[64,512]{1,0:T(8,128)S(1)} %get-tuple-element.127.x_ref, f32[8,512]{1,0:T(8,128)S(1)} %get-tuple-element.96.count_ref, ...), custom_call_target="tpu_custom_call" | custom-call | flops 83886080 | bytes 1982464 | tf_op jit(solution)/shard_map/pallas_call | solution.py:401
  21.8 1.4 %collective-permute-done.8 = f32[64,128]{1,0:T(8,128)S(1)} collective-permute-done((f32[64,128]{1,0:T(8,128)S(1)}, f32[64,128]{1,0:T(8,128)S(1)}, u32[]{:S(2)}, u32[]{:S(2)}) %collective-permute-start.8) | collective-permute-done | bytes 32800 | tf_op jit(solution)/shard_map/ppermute | solution.py:458
  23.3 1.7 %collective-permute-start.12 = (f32[8,512]{1,0:T(8,128)S(1)}, f32[8,512]{1,0:T(8,128)S(1)}, u32[]{:S(2)}, u32[]{:S(2)}) collective-permute-start(f32[8,512]{1,0:T(8,128)S(1)} %get-tuple-element.143.refs_0_), channel_id=1, source_target_pairs={{0,8},{8,16},{16,24},{24,0},{1,9},{9,17},{17,25},{25,1},{2,10},{10... | collective-permute-start | bytes 49160 | tf_op jit(solution)/shard_map/ppermute | solution.py:606
  25.0 1.5 %collective-permute-start.11 = (f32[8,512]{1,0:T(8,128)S(1)}, f32[8,512]{1,0:T(8,128)S(1)}, u32[]{:S(2)}, u32[]{:S(2)}) collective-permute-start(f32[8,512]{1,0:T(8,128)S(1)} %get-tuple-element.143.refs_0_), channel_id=1, source_target_pairs={{0,16},{8,24},{16,0},{24,8},{1,17},{9,25},{17,1},{25,9},{2,18},{10... | collective-permute-start | bytes 49160 | tf_op jit(solution)/shard_map/ppermute | solution.py:606
  26.5 1.4 %collective-permute-start.10 = (f32[8,512]{1,0:T(8,128)S(1)}, f32[8,512]{1,0:T(8,128)S(1)}, u32[]{:S(2)}, u32[]{:S(2)}) collective-permute-start(f32[8,512]{1,0:T(8,128)S(1)} %get-tuple-element.143.refs_0_), channel_id=1, source_target_pairs={{0,24},{8,0},{16,8},{24,16},{1,25},{9,1},{17,9},{25,17},{2,26},{10... | collective-permute-start | bytes 49160 | tf_op jit(solution)/shard_map/ppermute | solution.py:606
  28.0 0.9 %shard_map.163 = (f32[64,512]{1,0:T(8,128)}, f32[64,512]{1,0:T(8,128)S(1)}) custom-call(f32[64,256]{1,0:T(8,128)S(1)} %get-tuple-element.138.both_ref, f32[64,256]{1,0:T(8,128)S(1)} %get-tuple-element.122.refs_0_.z_ref, f32[8,256]{1,0:T(8,128)S(1)} %get-tuple-element.105.degree_ref, bf16[256,512]{1,0:T(8,128)(2,1)S(1)} %get-tuple-element.125.own_ref, ...), custom_call_target="tpu_custom_call" | custom-call | flops 83886080 | bytes 811008 | tf_op jit(solution)/shard_map/pallas_call | solution.py:401
  28.9 1.4 %collective-permute-done.10.refs_1_ = f32[8,512]{1,0:T(8,128)S(1)} collective-permute-done((f32[8,512]{1,0:T(8,128)S(1)}, f32[8,512]{1,0:T(8,128)S(1)}, u32[]{:S(2)}, u32[]{:S(2)}) %collective-permute-start.10) | collective-permute-done | bytes 16416 | tf_op jit(solution)/shard_map/ppermute | solution.py:606
  30.3 0.7 %shard_map.164 = (f32[64,512]{1,0:T(8,128)}, f32[1,512]{1,0:T(1,128)}) custom-call(f32[8,512]{1,0:T(8,128)S(1)} %get-tuple-element.143.refs_0_, f32[8,512]{1,0:T(8,128)S(1)} %collective-permute-done.10.refs_1_, f32[8,512]{1,0:T(8,128)S(1)} %collective-permute-done.11.refs_2_, f32[8,512]{1,0:T(8,128)S(1)} %collective-permute-done.12.refs_3_, ...), custom_call_target="tpu_custom_call" | custom-call | flops 83886080 | bytes 212992 | tf_op jit(solution)/shard_map/pallas_call | solution.py:401
  (27 shorter events, 1.4 us)
Async XLA Ops:
  1.8 5.2 %collective-permute-start = (f32[64,128]{1,0:T(8,128)S(1)}, f32[64,128]{1,0:T(8,128)S(1)}, u32[]{:S(2)}, u32[]{:S(2)}) collective-permute-start(f32[64,128]{1,0:T(8,128)S(1)} %get-tuple-element.75), channel_id=1, source_target_pairs={{0,8},{1,2},{2,1},{3,4},{4,3},{5,6},{6,5},{7,15},{8,0},{9,10},{10,... | collective-permute-start | bytes 98312 | tf_op jit(solution)/shard_map/ppermute | solution.py:458
  4.8 2.2 %collective-permute-start.1 = (f32[64,128]{1,0:T(8,128)S(1)}, f32[64,128]{1,0:T(8,128)S(1)}, u32[]{:S(2)}, u32[]{:S(2)}) collective-permute-start(f32[64,128]{1,0:T(8,128)S(1)} %get-tuple-element.76.pick1_ref), channel_id=1, source_target_pairs={{0,1},{1,0},{2,3},{3,2},{4,5},{5,4},{6,7},{7,6},{8,9},{9,8},{10,11... | collective-permute-start | bytes 98312 | tf_op jit(solution)/shard_map/ppermute | solution.py:455
  7.1 4.0 %collective-permute-start.2 = (f32[72,128]{1,0:T(8,128)S(1)}, f32[72,128]{1,0:T(8,128)S(1)}, u32[]{:S(2)}, u32[]{:S(2)}) collective-permute-start(f32[72,128]{1,0:T(8,128)S(1)} %get-tuple-element.88), channel_id=1, source_target_pairs={{0,8},{1,2},{2,1},{3,4},{4,3},{5,6},{6,5},{7,15},{8,0},{9,10},{10,... | collective-permute-start | bytes 110600 | tf_op jit(solution)/shard_map/ppermute | solution.py:458
  9.2 1.9 %collective-permute-start.3 = (f32[72,128]{1,0:T(8,128)S(1)}, f32[72,128]{1,0:T(8,128)S(1)}, u32[]{:S(2)}, u32[]{:S(2)}) collective-permute-start(f32[72,128]{1,0:T(8,128)S(1)} %get-tuple-element.92.send1_ref), channel_id=1, source_target_pairs={{0,1},{1,0},{2,3},{3,2},{4,5},{5,4},{6,7},{7,6},{8,9},{9,8},{10,11... | collective-permute-start | bytes 110600 | tf_op jit(solution)/shard_map/ppermute | solution.py:455
  11.1 4.0 %collective-permute-start.4 = (f32[64,128]{1,0:T(8,128)S(1)}, f32[64,128]{1,0:T(8,128)S(1)}, u32[]{:S(2)}, u32[]{:S(2)}) collective-permute-start(f32[64,128]{1,0:T(8,128)S(1)} %get-tuple-element.100), channel_id=1, source_target_pairs={{0,8},{1,2},{2,1},{3,4},{4,3},{5,6},{6,5},{7,15},{8,0},{9,10},{10,... | collective-permute-start | bytes 98312 | tf_op jit(solution)/shard_map/ppermute | solution.py:458
  13.3 1.9 %collective-permute-start.5 = (f32[64,128]{1,0:T(8,128)S(1)}, f32[64,128]{1,0:T(8,128)S(1)}, u32[]{:S(2)}, u32[]{:S(2)}) collective-permute-start(f32[64,128]{1,0:T(8,128)S(1)} %get-tuple-element.104.send1_ref), channel_id=1, source_target_pairs={{0,1},{1,0},{2,3},{3,2},{4,5},{5,4},{6,7},{7,6},{8,9},{9,8},{10,11... | collective-permute-start | bytes 98312 | tf_op jit(solution)/shard_map/ppermute | solution.py:455
  15.2 4.0 %collective-permute-start.6 = (f32[64,128]{1,0:T(8,128)S(1)}, f32[64,128]{1,0:T(8,128)S(1)}, u32[]{:S(2)}, u32[]{:S(2)}) collective-permute-start(f32[64,128]{1,0:T(8,128)S(1)} %get-tuple-element.111), channel_id=1, source_target_pairs={{0,8},{1,2},{2,1},{3,4},{4,3},{5,6},{6,5},{7,15},{8,0},{9,10},{10,... | collective-permute-start | bytes 98312 | tf_op jit(solution)/shard_map/ppermute | solution.py:458
  17.3 1.9 %collective-permute-start.7 = (f32[64,128]{1,0:T(8,128)S(1)}, f32[64,128]{1,0:T(8,128)S(1)}, u32[]{:S(2)}, u32[]{:S(2)}) collective-permute-start(f32[64,128]{1,0:T(8,128)S(1)} %get-tuple-element.115.send1_ref), channel_id=1, source_target_pairs={{0,1},{1,0},{2,3},{3,2},{4,5},{5,4},{6,7},{7,6},{8,9},{9,8},{10,11... | collective-permute-start | bytes 98312 | tf_op jit(solution)/shard_map/ppermute | solution.py:455
  19.2 4.0 %collective-permute-start.8 = (f32[64,128]{1,0:T(8,128)S(1)}, f32[64,128]{1,0:T(8,128)S(1)}, u32[]{:S(2)}, u32[]{:S(2)}) collective-permute-start(f32[64,128]{1,0:T(8,128)S(1)} %get-tuple-element.121), channel_id=1, source_target_pairs={{0,8},{1,2},{2,1},{3,4},{4,3},{5,6},{6,5},{7,15},{8,0},{9,10},{10,... | collective-permute-start | bytes 98312 | tf_op jit(solution)/shard_map/ppermute | solution.py:458
  21.3 1.9 %collective-permute-start.9 = (f32[64,128]{1,0:T(8,128)S(1)}, f32[64,128]{1,0:T(8,128)S(1)}, u32[]{:S(2)}, u32[]{:S(2)}) collective-permute-start(f32[64,128]{1,0:T(8,128)S(1)} %get-tuple-element.124.send1_ref), channel_id=1, source_target_pairs={{0,1},{1,0},{2,3},{3,2},{4,5},{5,4},{6,7},{7,6},{8,9},{9,8},{10,11... | collective-permute-start | bytes 98312 | tf_op jit(solution)/shard_map/ppermute | solution.py:455
  23.3 5.5 %collective-permute-start.12 = (f32[8,512]{1,0:T(8,128)S(1)}, f32[8,512]{1,0:T(8,128)S(1)}, u32[]{:S(2)}, u32[]{:S(2)}) collective-permute-start(f32[8,512]{1,0:T(8,128)S(1)} %get-tuple-element.143.refs_0_), channel_id=1, source_target_pairs={{0,8},{8,16},{16,24},{24,0},{1,9},{9,17},{17,25},{25,1},{2,10},{10... | collective-permute-start | bytes 49160 | tf_op jit(solution)/shard_map/ppermute | solution.py:606
  25.0 3.9 %collective-permute-start.11 = (f32[8,512]{1,0:T(8,128)S(1)}, f32[8,512]{1,0:T(8,128)S(1)}, u32[]{:S(2)}, u32[]{:S(2)}) collective-permute-start(f32[8,512]{1,0:T(8,128)S(1)} %get-tuple-element.143.refs_0_), channel_id=1, source_target_pairs={{0,16},{8,24},{16,0},{24,8},{1,17},{9,25},{17,1},{25,9},{2,18},{10... | collective-permute-start | bytes 49160 | tf_op jit(solution)/shard_map/ppermute | solution.py:606
  26.5 3.7 %collective-permute-start.10 = (f32[8,512]{1,0:T(8,128)S(1)}, f32[8,512]{1,0:T(8,128)S(1)}, u32[]{:S(2)}, u32[]{:S(2)}) collective-permute-start(f32[8,512]{1,0:T(8,128)S(1)} %get-tuple-element.143.refs_0_), channel_id=1, source_target_pairs={{0,24},{8,0},{16,8},{24,16},{1,25},{9,1},{17,9},{25,17},{2,26},{10... | collective-permute-start | bytes 49160 | tf_op jit(solution)/shard_map/ppermute | solution.py:606

commit v7 on v6

--- a/solution.py
+++ b/solution.py
@@ -54,66 +54,52 @@
 
 def load_kernel(count, *refs):
     sources, targets = refs[:count], refs[count : 2 * count]
-    pick1_ref, pick2_ref, semaphores = refs[2 * count :]
-    copies = fetch(sources, targets, semaphores)
-    halo_ref, theta_ref = targets[:2]
-    buses = theta_ref.shape[1]
-    slots = halo_ref.shape[1]
-    copies[0].wait()
-    ids = column_ids(halo_ref[...], buses)
-    rows = lax.broadcasted_iota(jnp.int32, (buses, ids.shape[1]), 0)
-    table = jnp.where(rows == ids, 1.0, 0.0).astype(BF16)
-    copies[1].wait()
-    pick = times(theta_ref[...], table)
-    pick1_ref[...] = pick[:, :slots]
-    pick2_ref[...] = pick[:, slots:]
-    for copy in copies[2:]:
-        copy.wait()
-
-
-def prep_kernel(
-    lam_f_hbm,
-    lam_t_hbm,
-    outage_hbm,
-    dual_hbm,
-    base_hbm,
-    load_hbm,
-    cost_hbm,
-    limit_hbm,
-    theta_ref,
-    from_ref,
-    to_ref,
-    halo_ref,
-    stiff_ref,
-    dual_ref,
-    edge_ref,
-    edge_t_ref,
-    own_t_ref,
-    inner_ref,
-    gain_ref,
-    x_ref,
-    p_ref,
-    c_ref,
-    count_edge_ref,
-    count_inner_ref,
-    sum_ref,
-    rows_ref,
-    lam_f_ref,
-    lam_t_ref,
-    outage_ref,
-    base_ref,
-    load_ref,
-    cost_ref,
-    limit_ref,
-    semaphores,
-):
-    sources = (
-        lam_f_hbm, lam_t_hbm, outage_hbm, dual_hbm, base_hbm, load_hbm, cost_hbm, limit_hbm
-    )
-    targets = (
-        lam_f_ref, lam_t_ref, outage_ref, dual_ref, base_ref, load_ref, cost_ref, limit_ref
-    )
-    copies = fetch(sources, targets, semaphores)
+    pick1_ref, pick2_ref, table_ref, semaphores = refs[2 * count :]
+    place = lax.axis_index("net")
+
+    @pl.when(place == 0)
+    def _():
+        pick1_ref[...] = jnp.zeros_like(pick1_ref)
+        pick2_ref[...] = jnp.zeros_like(pick2_ref)
+
+    @pl.when(place > 0)
+    def _():
+        copies = fetch(sources, targets, semaphores)
+        halo_ref, theta_ref = targets[:2]
+        buses, edges = table_ref.shape
+        copies[0].wait()
+        ids = column_ids(halo_ref[...], buses)
+        rows = lax.broadcasted_iota(jnp.int32, (buses, edges), 0)
+        table_ref[...] = jnp.where(rows == ids, 1.0, 0.0).astype(BF16)
+        copies[1].wait()
+        pick = times(theta_ref[...], table_ref[...])
+        pick1_ref[...] = pick[:, : edges // 2]
+        pick2_ref[...] = pick[:, edges // 2 :]
+        for copy in copies[2:]:
+            copy.wait()
+
+
+def late_kernel(count, *refs):
+    sources, semaphores = refs[:count], refs[-1]
+    targets = refs[2 * count + 1 : 3 * count + 1]
+
+    @pl.when(lax.axis_index("net") == 0)
+    def _():
+        for copy in fetch(sources, targets, semaphores):
+            copy.wait()
+
+
+def tables(refs, theta_ref, halo_ref, from_ref, to_ref):
+    (
+        edge_ref,
+        edge_t_ref,
+        own_t_ref,
+        inner_ref,
+        x_ref,
+        p_ref,
+        count_edge_ref,
+        count_inner_ref,
+    ) = refs
     buses = theta_ref.shape[1]
     branches = from_ref.shape[1]
     ids = column_ids(halo_ref[...], buses)
@@ -146,16 +132,33 @@
     count_inner_ref[...] = count[:, edges:]
     x = theta_ref[...] * inner
     x_ref[...] = x
-    p = times_t(x, inner_ref[...])
-    p_ref[...] = p
+    p_ref[...] = times_t(x, inner_ref[...])
+
+
+def prep_kernel(number, *refs):
+    sources, refs = refs[:number], refs[number:]
+    theta_ref, halo_ref, from_ref, to_ref, stiff_ref = refs[:5]
+    dual_ref, gain_ref, c_ref, rows_ref = refs[5:9]
+    outs = refs[9:17]
+    targets, semaphores = (*refs[17:-1], dual_ref), refs[-1]
+    copies = fetch(sources, targets, semaphores)
+    lam_f_ref, lam_t_ref, outage_ref = targets[:3]
+    per_bus = targets[3:7]
+
+    @pl.when(lax.axis_index("net") >= 0)
+    def _():
+        tables(outs, theta_ref, halo_ref, from_ref, to_ref)
+
     for copy in copies:
         copy.wait()
+    p_ref = outs[5]
     weight = stiff_ref[...] * (1.0 - outage_ref[...].astype(F32))
     gain_ref[...] = PENALTY * weight / (PENALTY + 2.0 * weight)
-    c_ref[...] = p - (lam_f_ref[...] - lam_t_ref[...]) / PENALTY
-    sum_ref[...] = jnp.broadcast_to(jnp.sum(dual_ref[...], axis=0, keepdims=True), sum_ref.shape)
-    for index, ref in enumerate((base_ref, load_ref, cost_ref, limit_ref)):
-        rows_ref[2 * index : 2 * index + 2, :] = jnp.broadcast_to(ref[...], (2, buses))
+    c_ref[...] = p_ref[...] - (lam_f_ref[...] - lam_t_ref[...]) / PENALTY
+    for index, ref in enumerate(per_bus):
+        rows_ref[2 * index : 2 * index + 2, :] = jnp.broadcast_to(
+            ref[...], (2, rows_ref.shape[1])
+        )
 
 
 def has_far():
@@ -322,7 +325,6 @@
     own_ref,
     dual_ref,
     rows_ref,
-    dsum_ref,
     *refs,
 ):
     *refs, net_ref, x_out_ref, dual_out_ref, sums_ref = refs
@@ -335,27 +337,29 @@
     spread = times(edge, own_ref[...])
     part = 1.0 / (rows_ref[4:5, :] + PENALTY + BALANCE)
     dual = dual_ref[...]
-    sums_ref[0:1, :] = dsum_ref[:1, :]
-    for index, ref in enumerate(refs[rounds:]):
-        whole = ref[...] + spread[index * conts : (index + 1) * conts]
-        sums_ref[index + 1 : index + 2, :] = jnp.sum(whole, axis=0, keepdims=True)
-        dual = dual + part * (BALANCE * whole - dual)
-    tail = sums_ref.shape[0] - rounds - 1
-    sums_ref[rounds + 1 :, :] = jnp.broadcast_to(
-        jnp.sum(net, axis=0, keepdims=True), (tail, net.shape[1])
-    )
+    wholes = [
+        ref[...] + spread[index * conts : (index + 1) * conts]
+        for index, ref in enumerate(refs[rounds:])
+    ]
+    for index, whole in enumerate([*wholes, net]):
+        term = 2.0 * part * (BALANCE * whole - dual) + dual
+        sums_ref[index : index + 1, :] = jnp.sum(term, axis=0, keepdims=True)
+        if index < rounds:
+            dual = dual + part * (BALANCE * whole - dual)
     dual_out_ref[...] = dual
 
 
 def total_kernel(
-    far_ref, got1_ref, send1_ref, own_ref, sums_in_ref, both_ref, sums_ref
+    far_ref, got1_ref, send1_ref, own_ref, rows_ref, sums_in_ref, both_ref, sums_ref
 ):
     both = both_ends(far_ref, got1_ref, send1_ref, slice(0, send1_ref.shape[0]))
     both_ref[...] = both
     row = jnp.broadcast_to(jnp.sum(both, axis=0, keepdims=True), (8, both.shape[1]))
     sums_ref[...] = sums_in_ref[...]
-    last = slice(ROUNDS, ROUNDS + 1)
-    sums_ref[last, :] = sums_in_ref[last, :] + times(row, own_ref[...])[:1]
+    last = slice(ROUNDS - 1, ROUNDS)
+    part = 1.0 / (rows_ref[4:5, :] + PENALTY + BALANCE)
+    late = times(row, own_ref[...])[:1]
+    sums_ref[last, :] = sums_in_ref[last, :] + 2.0 * BALANCE * part * late
 
 
 def field_kernel(
@@ -380,17 +384,14 @@
     base, load = rows_ref[0:1, :], rows_ref[2:3, :]
     limit = rows_ref[6:7, :]
     part = 1.0 / (rows_ref[4:5, :] + PENALTY + BALANCE)
-    dual_mean = mean[0:1, :]
     shared = jnp.zeros_like(base)
     for index in range(ROUNDS):
-        net_mean = mean[index + 1 : index + 2, :]
         gen_shared = part * (PENALTY * base - shared + BALANCE * load)
         if index == ROUNDS - 1:
             gen_ref[...] = part_gen_ref[...] + gen_shared
-        gen_mean = part * (PENALTY * base - dual_mean + BALANCE * (load + net_mean))
-        dual_mean = dual_mean + PENALTY * (gen_mean - base)
+        total_mean = mean[index : index + 1, :] + 2.0 * gen_shared + shared - base
         shared = shared + PENALTY * (gen_shared - base)
-        base = jnp.clip(gen_mean + dual_mean / PENALTY, 0.0, limit)
+        base = jnp.clip(total_mean, 0.0, limit)
     base_out_ref[...] = base
 
 
@@ -466,65 +467,82 @@
     edge = ((conts, edges), F32)
     tall = ((conts + 8, slots), F32)
     row = ((8, buses), F32)
+    total = ((ROUNDS, buses), F32)
 
     halo_row = halo_rows.reshape(1, slots)
     fetched = [halo_row, angles, from_bus, to_ref, stiffness]
-    number = len(fetched)
+    count = len(fetched)
 
     def load(*refs):
-        load_kernel(number, *refs)
-
+        load_kernel(count, *refs)
+
+    def late(*refs):
+        late_kernel(count, *refs)
+
+    arrived = [(a.shape, a.dtype) for a in fetched]
     *here, pick1, pick2 = call(
         load,
-        [(a.shape, a.dtype) for a in fetched] + [half, half],
+        arrived + [half, half],
         *in_hbm(*fetched),
-        spaces=[pltpu.HBM] * number,
-        scratch=[pltpu.SemaphoreType.DMA((number,))],
+        spaces=[pltpu.HBM] * count,
+        scratch=[pltpu.VMEM((buses, edges), BF16), pltpu.SemaphoreType.DMA((count,))],
     )
     got2 = trade_far(pick2)
+    *here, pick1 = call(
+        late,
+        arrived + [half],
+        *in_hbm(*fetched),
+        *here,
+        pick1,
+        spaces=[pltpu.HBM] * count + [pltpu.VMEM] * (count + 1),
+        scratch=[pltpu.SemaphoreType.DMA((count,))],
+        aliases={count + index: index for index in range(count + 1)},
+    )
     got1 = trade_near(pick1)
     halo_row, angles = here[:2]
     from_row, to_row, stiff_row = (a.reshape(1, branches) for a in here[2:])
     rows = [a.reshape(1, buses) for a in (base_prev, bus_load, gen_cost, gen_limit)]
-    fetched = [lam_from, lam_to, outage, gen_dual, *rows]
-    near_args = [angles, from_row, to_row, halo_row, stiff_row]
+    fetched = [lam_from, lam_to, outage, *rows, gen_dual]
+    near_args = [angles, halo_row, from_row, to_row, stiff_row]
+    number = len(fetched)
+
+    def prep(*refs):
+        prep_kernel(number, *refs)
+
     (
         gen_dual,
+        gain,
+        c,
+        rows,
         edge_table,
         edge_turned,
         own,
         inner_table,
-        gain,
         x,
         p,
-        c,
         count_edge,
         count_inner,
-        dual_sum,
-        rows,
     ) = call(
-        prep_kernel,
+        prep,
         [
             bus,
+            branch,
+            branch,
+            row,
             ((branches, edges), BF16),
             ((edges, branches), BF16),
             ((edges, buses), BF16),
             ((branches, buses), BF16),
-            branch,
             bus,
             branch,
-            branch,
             ((8, edges), F32),
-            row,
-            row,
             row,
         ],
         *in_hbm(*fetched),
         *near_args,
-        spaces=[pltpu.HBM] * len(fetched) + [pltpu.VMEM] * len(near_args),
-        scratch=[pltpu.VMEM(a.shape, a.dtype) for a in (lam_from, lam_to, outage)]
-        + [pltpu.VMEM((1, buses), F32)] * 4
-        + [pltpu.SemaphoreType.DMA((len(fetched),))],
+        spaces=[pltpu.HBM] * number + [pltpu.VMEM] * len(near_args),
+        scratch=[pltpu.VMEM(a.shape, a.dtype) for a in fetched[:-1]]
+        + [pltpu.SemaphoreType.DMA((number,))],
     )
     send2, z, delta, flow = call(
         first_kernel,
@@ -587,7 +605,7 @@
     got1 = trade_near(send1)
     net, x, dual, sums = call(
         beside_last_kernel,
-        [bus, bus, bus, row],
+        [bus, bus, bus, total],
         flow,
         x,
         count_inner,
@@ -595,11 +613,12 @@
         own,
         gen_dual,
         rows,
-        dual_sum,
         *boths,
         *nets,
     )
-    both, sums = call(total_kernel, [edge, row], send2 + got2, got1, send1, own, sums)
+    both, sums = call(
+        total_kernel, [edge, total], send2 + got2, got1, send1, own, rows, sums
+    )
     parts = [sums]
     for shift in reversed(range(1, cont_size)):
         parts.append(

time: 31.2 us -> 30.4 us (0.974)
  Pallas kernels: 8.58 us -> 7.88 us
    ppermute x5, starting transfers between devices: 0.66 us -> 1.61 us  [trade_near(): return lax.ppermute(value, axes, swap1)]
    ppermute x5, starting transfers between devices: 9.99 us -> 9.22 us  [trade_far(): return lax.ppermute(value, axes, swap2)]
    pallas_call x17 -> x18, Pallas kernels: 8.58 us -> 7.88 us  [call(): pl.pallas_call(kernel, out_shape=shapes, in_specs=[pl.BlockSpec(memory_sp...]
  transfers between devices with their start and end apart: 13 -> 13, of which waited for: 5 -> 5; matrix products, arithmetic and copies ran while one was open for 0% -> 0% of each run, Pallas kernels for 21% -> 23%
where the time goes in v7:
time: 30.4 us; the launch traced here: 30.2 us
  starting transfers between devices  15.3 us (50%)
  Pallas kernels  7.88 us (26%)
  waiting for transfers between devices  6.26 us (21%)
  between operations  0.77 us (3%)
    ppermute x5, starting transfers between devices, trade_far(): return lax.ppermute(value, axes, swap2)  9.22 us
    pallas_call x18, Pallas kernels, call(): pl.pallas_call(kernel, out_shape=shapes, in_specs=[pl.BlockSpec(memory_sp...  7.88 us
    ppermute x5, waiting for transfers between devices, trade_far(): return lax.ppermute(value, axes, swap2)  4.92 us
    ppermute x3, starting transfers between devices, local(): lax.ppermute(sums, 'cont', [(i, (i + shift) % cont_size) for i in range(c...  4.45 us
    ppermute x5, starting transfers between devices, trade_near(): return lax.ppermute(value, axes, swap1)  1.61 us
    ppermute x3, waiting for transfers between devices, local(): lax.ppermute(sums, 'cont', [(i, (i + shift) % cont_size) for i in range(c...  1.32 us
  transfers between devices with their start and end apart: 13, of which 5 were waited for; matrix products, arithmetic and copies ran while one was open for 0% of the time, Pallas kernels for 23%

profile of v7, /device:TPU:0, one launch (start us, length us, event | category | flops | bytes accessed | tf_op | source)
XLA Modules:
  0.0 30.2 jit_solution(3382393661924941126)
XLA Ops:
  0.7 3.0 %collective-permute-start = (f32[64,128]{1,0:T(8,128)S(1)}, f32[64,128]{1,0:T(8,128)S(1)}, u32[]{:S(2)}, u32[]{:S(2)}) collective-permute-start(f32[64,128]{1,0:T(8,128)S(1)} %get-tuple-element.80), channel_id=1, source_target_pairs={{0,8},{1,2},{2,1},{3,4},{4,3},{5,6},{6,5},{7,15},{8,0},{9,10},{10,... | collective-permute-start | bytes 98312 | tf_op jit(solution)/shard_map/ppermute | solution.py:459
  3.7 1.0 %shard_map.149 = (s32[1,128]{1,0:T(1,128)S(1)}, f32[64,512]{1,0:T(8,128)S(1)}, s32[640]{0:T(1024)S(1)}, s32[640]{0:T(1024)S(1)}, f32[640]{0:T(1024)S(1)}, /*index=5*/f32[64,128]{1,0:T(8,128)S(1)}) custom-call(s32[1,128]{1,0:T(1,128)} %bitcast.11, f32[64,512]{1,0:T(8,128)} %refs_1_.4, ...), custom_call_target="tpu_custom_call", output_to_operand_aliasing={{0}: (5, {}), {1}: (6, {}), {2}: (7, {}), {3}: (8, {}), {4}... | custom-call | flops 83886080 | bytes 311296 | tf_op jit(solution)/shard_map/pallas_call | solution.py:402
  4.7 0.4 %collective-permute-start.1 = (f32[64,128]{1,0:T(8,128)S(1)}, f32[64,128]{1,0:T(8,128)S(1)}, u32[]{:S(2)}, u32[]{:S(2)}) collective-permute-start(f32[64,128]{1,0:T(8,128)S(1)} %get-tuple-element.87.pick1_ref), channel_id=1, source_target_pairs={{0,1},{1,0},{2,3},{3,2},{4,5},{5,4},{6,7},{7,6},{8,9},{9,8},{10,11... | collective-permute-start | bytes 98312 | tf_op jit(solution)/shard_map/ppermute | solution.py:456
  5.1 1.4 %shard_map.150 = (f32[64,512]{1,0:T(8,128)S(1)}, f32[64,640]{1,0:T(8,128)S(1)}, f32[64,640]{1,0:T(8,128)S(1)}, f32[8,512]{1,0:T(8,128)S(1)}, bf16[640,256]{1,0:T...) custom-call(f32[64,640]{1,0:T(8,128)} %refs_0_.1, ...), custom_call_target="tpu_custom_call" | custom-call | flops 83886080 | bytes 770048 | tf_op jit(solution)/shard_map/pallas_call | solution.py:402
  6.6 1.6 %collective-permute-start.2 = (f32[72,128]{1,0:T(8,128)S(1)}, f32[72,128]{1,0:T(8,128)S(1)}, u32[]{:S(2)}, u32[]{:S(2)}) collective-permute-start(f32[72,128]{1,0:T(8,128)S(1)} %get-tuple-element.99), channel_id=1, source_target_pairs={{0,8},{1,2},{2,1},{3,4},{4,3},{5,6},{6,5},{7,15},{8,0},{9,10},{10,... | collective-permute-start | bytes 110600 | tf_op jit(solution)/shard_map/ppermute | solution.py:459
  8.1 0.4 %shard_map.152 = (f32[64,640]{1,0:T(8,128)S(1)}, f32[64,640]{1,0:T(8,128)S(1)}, f32[72,128]{1,0:T(8,128)S(1)}) custom-call(f32[64,256]{1,0:T(8,128)S(1)} %get-tuple-element.100.refs_0_.z_ref, bf16[640,256]{1,0:T(8,128)(2,1)S(1)} %get-tuple-element.93.edge_ref.refs_1_, ...), custom_call_target="tpu_custom_call", output_to_operand_aliasing={{0}: (6, {}), {1}: (7, {})} | custom-call | flops 83886080 | bytes 1548288 | tf_op jit(solution)/shard_map/pallas_call | solution.py:402
  8.5 0.6 %collective-permute-start.3 = (f32[72,128]{1,0:T(8,128)S(1)}, f32[72,128]{1,0:T(8,128)S(1)}, u32[]{:S(2)}, u32[]{:S(2)}) collective-permute-start(f32[72,128]{1,0:T(8,128)S(1)} %get-tuple-element.103.send1_ref), channel_id=1, source_target_pairs={{0,1},{1,0},{2,3},{3,2},{4,5},{5,4},{6,7},{7,6},{8,9},{9,8},{10,11... | collective-permute-start | bytes 110600 | tf_op jit(solution)/shard_map/ppermute | solution.py:456
  9.1 0.5 %shard_map.153 = (f32[64,512]{1,0:T(8,128)S(1)}, f32[64,512]{1,0:T(8,128)S(1)}, f32[64,640]{1,0:T(8,128)S(1)}, f32[64,640]{1,0:T(8,128)S(1)}) custom-call(f32[64,640]{1,0:T(8,128)S(1)} %get-tuple-element.104.flow_ref, f32[64,640]{1,0:T(8,128)S(1)} %get-tuple-element.105.delta_ref, f32[64,512]{1,0:T(8,128)S(1)} %get-tuple-element.106.x_ref, ...), custom_call_target="tpu_custom_call" | custom-call | flops 83886080 | bytes 1130496 | tf_op jit(solution)/shard_map/pallas_call | solution.py:402
  9.6 0.9 %collective-permute-done.2 = f32[72,128]{1,0:T(8,128)S(1)} collective-permute-done((f32[72,128]{1,0:T(8,128)S(1)}, f32[72,128]{1,0:T(8,128)S(1)}, u32[]{:S(2)}, u32[]{:S(2)}) %collective-permute-start.2) | collective-permute-done | bytes 36896 | tf_op jit(solution)/shard_map/ppermute | solution.py:459
  10.6 1.6 %collective-permute-start.4 = (f32[64,128]{1,0:T(8,128)S(1)}, f32[64,128]{1,0:T(8,128)S(1)}, u32[]{:S(2)}, u32[]{:S(2)}) collective-permute-start(f32[64,128]{1,0:T(8,128)S(1)} %get-tuple-element.111), channel_id=1, source_target_pairs={{0,8},{1,2},{2,1},{3,4},{4,3},{5,6},{6,5},{7,15},{8,0},{9,10},{10,... | collective-permute-start | bytes 98312 | tf_op jit(solution)/shard_map/ppermute | solution.py:459
  12.9 0.5 %shard_map.156 = (f32[64,512]{1,0:T(8,128)S(1)}, f32[64,512]{1,0:T(8,128)S(1)}, f32[64,640]{1,0:T(8,128)S(1)}, f32[64,640]{1,0:T(8,128)S(1)}) custom-call(f32[64,640]{1,0:T(8,128)S(1)} %get-tuple-element.117.flow_ref, f32[64,640]{1,0:T(8,128)S(1)} %get-tuple-element.118.delta_ref, f32[64,512]{1,0:T(8,128)S(1)} %get-tuple-element.119.x_ref, ...), custom_call_target="tpu_custom_call" | custom-call | flops 83886080 | bytes 1130496 | tf_op jit(solution)/shard_map/pallas_call | solution.py:402
  13.5 1.1 %collective-permute-done.4 = f32[64,128]{1,0:T(8,128)S(1)} collective-permute-done((f32[64,128]{1,0:T(8,128)S(1)}, f32[64,128]{1,0:T(8,128)S(1)}, u32[]{:S(2)}, u32[]{:S(2)}) %collective-permute-start.4) | collective-permute-done | bytes 32800 | tf_op jit(solution)/shard_map/ppermute | solution.py:459
  14.7 1.6 %collective-permute-start.6 = (f32[64,128]{1,0:T(8,128)S(1)}, f32[64,128]{1,0:T(8,128)S(1)}, u32[]{:S(2)}, u32[]{:S(2)}) collective-permute-start(f32[64,128]{1,0:T(8,128)S(1)} %get-tuple-element.122), channel_id=1, source_target_pairs={{0,8},{1,2},{2,1},{3,4},{4,3},{5,6},{6,5},{7,15},{8,0},{9,10},{10,... | collective-permute-start | bytes 98312 | tf_op jit(solution)/shard_map/ppermute | solution.py:459
  16.7 0.5 %shard_map.159 = (f32[64,512]{1,0:T(8,128)S(1)}, f32[64,512]{1,0:T(8,128)S(1)}, f32[64,640]{1,0:T(8,128)S(1)}, f32[64,640]{1,0:T(8,128)S(1)}) custom-call(f32[64,640]{1,0:T(8,128)S(1)} %get-tuple-element.127.flow_ref, f32[64,640]{1,0:T(8,128)S(1)} %get-tuple-element.128.delta_ref, f32[64,512]{1,0:T(8,128)S(1)} %get-tuple-element.129.x_ref, ...), custom_call_target="tpu_custom_call" | custom-call | flops 83886080 | bytes 1130496 | tf_op jit(solution)/shard_map/pallas_call | solution.py:402
  17.3 1.3 %collective-permute-done.6 = f32[64,128]{1,0:T(8,128)S(1)} collective-permute-done((f32[64,128]{1,0:T(8,128)S(1)}, f32[64,128]{1,0:T(8,128)S(1)}, u32[]{:S(2)}, u32[]{:S(2)}) %collective-permute-start.6) | collective-permute-done | bytes 32800 | tf_op jit(solution)/shard_map/ppermute | solution.py:459
  18.7 1.6 %collective-permute-start.8 = (f32[64,128]{1,0:T(8,128)S(1)}, f32[64,128]{1,0:T(8,128)S(1)}, u32[]{:S(2)}, u32[]{:S(2)}) collective-permute-start(f32[64,128]{1,0:T(8,128)S(1)} %get-tuple-element.132), channel_id=1, source_target_pairs={{0,8},{1,2},{2,1},{3,4},{4,3},{5,6},{6,5},{7,15},{8,0},{9,10},{10,... | collective-permute-start | bytes 98312 | tf_op jit(solution)/shard_map/ppermute | solution.py:459
  20.7 0.5 %shard_map.162 = (f32[64,512]{1,0:T(8,128)S(1)}, f32[64,512]{1,0:T(8,128)S(1)}, f32[64,512]{1,0:T(8,128)S(1)}, f32[4,512]{1,0:T(4,128)S(1)}) custom-call(f32[64,640]{1,0:T(8,128)S(1)} %get-tuple-element.138.flow_ref, f32[64,512]{1,0:T(8,128)S(1)} %get-tuple-element.139.x_ref, f32[8,512]{1,0:T(8,128)S(1)} %get-tuple-element.107.count_ref, ...), custom_call_target="tpu_custom_call" | custom-call | flops 83886080 | bytes 1966080 | tf_op jit(solution)/shard_map/pallas_call | solution.py:402
  21.2 1.5 %collective-permute-done.8 = f32[64,128]{1,0:T(8,128)S(1)} collective-permute-done((f32[64,128]{1,0:T(8,128)S(1)}, f32[64,128]{1,0:T(8,128)S(1)}, u32[]{:S(2)}, u32[]{:S(2)}) %collective-permute-start.8) | collective-permute-done | bytes 32800 | tf_op jit(solution)/shard_map/ppermute | solution.py:459
  22.8 1.5 %collective-permute-start.12 = (f32[4,512]{1,0:T(4,128)S(1)}, f32[4,512]{1,0:T(4,128)S(1)}, u32[]{:S(2)}, u32[]{:S(2)}) collective-permute-start(f32[4,512]{1,0:T(4,128)S(1)} %get-tuple-element.153.refs_0_), channel_id=1, source_target_pairs={{0,8},{8,16},{16,24},{24,0},{1,9},{9,17},{17,25},{25,1},{2,10},{10... | collective-permute-start | bytes 24584 | tf_op jit(solution)/shard_map/ppermute | solution.py:625
  24.3 1.5 %collective-permute-start.11 = (f32[4,512]{1,0:T(4,128)S(1)}, f32[4,512]{1,0:T(4,128)S(1)}, u32[]{:S(2)}, u32[]{:S(2)}) collective-permute-start(f32[4,512]{1,0:T(4,128)S(1)} %get-tuple-element.153.refs_0_), channel_id=1, source_target_pairs={{0,16},{8,24},{16,0},{24,8},{1,17},{9,25},{17,1},{25,9},{2,18},{10... | collective-permute-start | bytes 24584 | tf_op jit(solution)/shard_map/ppermute | solution.py:625
  25.8 1.4 %collective-permute-start.10 = (f32[4,512]{1,0:T(4,128)S(1)}, f32[4,512]{1,0:T(4,128)S(1)}, u32[]{:S(2)}, u32[]{:S(2)}) collective-permute-start(f32[4,512]{1,0:T(4,128)S(1)} %get-tuple-element.153.refs_0_), channel_id=1, source_target_pairs={{0,24},{8,0},{16,8},{24,16},{1,25},{9,1},{17,9},{25,17},{2,26},{10... | collective-permute-start | bytes 24584 | tf_op jit(solution)/shard_map/ppermute | solution.py:625
  27.3 0.9 %shard_map.164 = (f32[64,512]{1,0:T(8,128)}, f32[64,512]{1,0:T(8,128)S(1)}) custom-call(f32[64,256]{1,0:T(8,128)S(1)} %get-tuple-element.148.both_ref, f32[64,256]{1,0:T(8,128)S(1)} %get-tuple-element.133.refs_0_.z_ref, f32[8,256]{1,0:T(8,128)S(1)} %get-tuple-element.116.degree_ref, bf16[256,512]{1,0:T(8,128)(2,1)S(1)} %get-tuple-element.136.own_ref, ...), custom_call_target="tpu_custom_call" | custom-call | flops 83886080 | bytes 811008 | tf_op jit(solution)/shard_map/pallas_call | solution.py:402
  28.2 1.3 %collective-permute-done.10.refs_1_ = f32[4,512]{1,0:T(4,128)S(1)} collective-permute-done((f32[4,512]{1,0:T(4,128)S(1)}, f32[4,512]{1,0:T(4,128)S(1)}, u32[]{:S(2)}, u32[]{:S(2)}) %collective-permute-start.10) | collective-permute-done | bytes 8224 | tf_op jit(solution)/shard_map/ppermute | solution.py:625
  29.5 0.7 %shard_map.165 = (f32[64,512]{1,0:T(8,128)}, f32[1,512]{1,0:T(1,128)}) custom-call(f32[4,512]{1,0:T(4,128)S(1)} %get-tuple-element.153.refs_0_, f32[4,512]{1,0:T(4,128)S(1)} %collective-permute-done.10.refs_1_, f32[4,512]{1,0:T(4,128)S(1)} %collective-permute-done.11.refs_2_, f32[4,512]{1,0:T(4,128)S(1)} %collective-permute-done.12.refs_3_, ...), custom_call_target="tpu_custom_call" | custom-call | flops 83886080 | bytes 180224 | tf_op jit(solution)/shard_map/pallas_call | solution.py:402
  (28 shorter events, 2.1 us)
Async XLA Ops:
  0.7 5.8 %collective-permute-start = (f32[64,128]{1,0:T(8,128)S(1)}, f32[64,128]{1,0:T(8,128)S(1)}, u32[]{:S(2)}, u32[]{:S(2)}) collective-permute-start(f32[64,128]{1,0:T(8,128)S(1)} %get-tuple-element.80), channel_id=1, source_target_pairs={{0,8},{1,2},{2,1},{3,4},{4,3},{5,6},{6,5},{7,15},{8,0},{9,10},{10,... | collective-permute-start | bytes 98312 | tf_op jit(solution)/shard_map/ppermute | solution.py:459
  4.7 1.8 %collective-permute-start.1 = (f32[64,128]{1,0:T(8,128)S(1)}, f32[64,128]{1,0:T(8,128)S(1)}, u32[]{:S(2)}, u32[]{:S(2)}) collective-permute-start(f32[64,128]{1,0:T(8,128)S(1)} %get-tuple-element.87.pick1_ref), channel_id=1, source_target_pairs={{0,1},{1,0},{2,3},{3,2},{4,5},{5,4},{6,7},{7,6},{8,9},{9,8},{10,11... | collective-permute-start | bytes 98312 | tf_op jit(solution)/shard_map/ppermute | solution.py:456
  6.6 4.0 %collective-permute-start.2 = (f32[72,128]{1,0:T(8,128)S(1)}, f32[72,128]{1,0:T(8,128)S(1)}, u32[]{:S(2)}, u32[]{:S(2)}) collective-permute-start(f32[72,128]{1,0:T(8,128)S(1)} %get-tuple-element.99), channel_id=1, source_target_pairs={{0,8},{1,2},{2,1},{3,4},{4,3},{5,6},{6,5},{7,15},{8,0},{9,10},{10,... | collective-permute-start | bytes 110600 | tf_op jit(solution)/shard_map/ppermute | solution.py:459
  8.5 2.1 %collective-permute-start.3 = (f32[72,128]{1,0:T(8,128)S(1)}, f32[72,128]{1,0:T(8,128)S(1)}, u32[]{:S(2)}, u32[]{:S(2)}) collective-permute-start(f32[72,128]{1,0:T(8,128)S(1)} %get-tuple-element.103.send1_ref), channel_id=1, source_target_pairs={{0,1},{1,0},{2,3},{3,2},{4,5},{5,4},{6,7},{7,6},{8,9},{9,8},{10,11... | collective-permute-start | bytes 110600 | tf_op jit(solution)/shard_map/ppermute | solution.py:456
  10.6 4.0 %collective-permute-start.4 = (f32[64,128]{1,0:T(8,128)S(1)}, f32[64,128]{1,0:T(8,128)S(1)}, u32[]{:S(2)}, u32[]{:S(2)}) collective-permute-start(f32[64,128]{1,0:T(8,128)S(1)} %get-tuple-element.111), channel_id=1, source_target_pairs={{0,8},{1,2},{2,1},{3,4},{4,3},{5,6},{6,5},{7,15},{8,0},{9,10},{10,... | collective-permute-start | bytes 98312 | tf_op jit(solution)/shard_map/ppermute | solution.py:459
  12.6 2.1 %collective-permute-start.5 = (f32[64,128]{1,0:T(8,128)S(1)}, f32[64,128]{1,0:T(8,128)S(1)}, u32[]{:S(2)}, u32[]{:S(2)}) collective-permute-start(f32[64,128]{1,0:T(8,128)S(1)} %get-tuple-element.115.send1_ref), channel_id=1, source_target_pairs={{0,1},{1,0},{2,3},{3,2},{4,5},{5,4},{6,7},{7,6},{8,9},{9,8},{10,11... | collective-permute-start | bytes 98312 | tf_op jit(solution)/shard_map/ppermute | solution.py:456
  14.7 4.0 %collective-permute-start.6 = (f32[64,128]{1,0:T(8,128)S(1)}, f32[64,128]{1,0:T(8,128)S(1)}, u32[]{:S(2)}, u32[]{:S(2)}) collective-permute-start(f32[64,128]{1,0:T(8,128)S(1)} %get-tuple-element.122), channel_id=1, source_target_pairs={{0,8},{1,2},{2,1},{3,4},{4,3},{5,6},{6,5},{7,15},{8,0},{9,10},{10,... | collective-permute-start | bytes 98312 | tf_op jit(solution)/shard_map/ppermute | solution.py:459
  16.6 2.1 %collective-permute-start.7 = (f32[64,128]{1,0:T(8,128)S(1)}, f32[64,128]{1,0:T(8,128)S(1)}, u32[]{:S(2)}, u32[]{:S(2)}) collective-permute-start(f32[64,128]{1,0:T(8,128)S(1)} %get-tuple-element.126.send1_ref), channel_id=1, source_target_pairs={{0,1},{1,0},{2,3},{3,2},{4,5},{5,4},{6,7},{7,6},{8,9},{9,8},{10,11... | collective-permute-start | bytes 98312 | tf_op jit(solution)/shard_map/ppermute | solution.py:456
  18.7 4.0 %collective-permute-start.8 = (f32[64,128]{1,0:T(8,128)S(1)}, f32[64,128]{1,0:T(8,128)S(1)}, u32[]{:S(2)}, u32[]{:S(2)}) collective-permute-start(f32[64,128]{1,0:T(8,128)S(1)} %get-tuple-element.132), channel_id=1, source_target_pairs={{0,8},{1,2},{2,1},{3,4},{4,3},{5,6},{6,5},{7,15},{8,0},{9,10},{10,... | collective-permute-start | bytes 98312 | tf_op jit(solution)/shard_map/ppermute | solution.py:459
  20.6 2.1 %collective-permute-start.9 = (f32[64,128]{1,0:T(8,128)S(1)}, f32[64,128]{1,0:T(8,128)S(1)}, u32[]{:S(2)}, u32[]{:S(2)}) collective-permute-start(f32[64,128]{1,0:T(8,128)S(1)} %get-tuple-element.135.send1_ref), channel_id=1, source_target_pairs={{0,1},{1,0},{2,3},{3,2},{4,5},{5,4},{6,7},{7,6},{8,9},{9,8},{10,11... | collective-permute-start | bytes 98312 | tf_op jit(solution)/shard_map/ppermute | solution.py:456
  22.8 5.3 %collective-permute-start.12 = (f32[4,512]{1,0:T(4,128)S(1)}, f32[4,512]{1,0:T(4,128)S(1)}, u32[]{:S(2)}, u32[]{:S(2)}) collective-permute-start(f32[4,512]{1,0:T(4,128)S(1)} %get-tuple-element.153.refs_0_), channel_id=1, source_target_pairs={{0,8},{8,16},{16,24},{24,0},{1,9},{9,17},{17,25},{25,1},{2,10},{10... | collective-permute-start | bytes 24584 | tf_op jit(solution)/shard_map/ppermute | solution.py:625
  24.3 3.9 %collective-permute-start.11 = (f32[4,512]{1,0:T(4,128)S(1)}, f32[4,512]{1,0:T(4,128)S(1)}, u32[]{:S(2)}, u32[]{:S(2)}) collective-permute-start(f32[4,512]{1,0:T(4,128)S(1)} %get-tuple-element.153.refs_0_), channel_id=1, source_target_pairs={{0,16},{8,24},{16,0},{24,8},{1,17},{9,25},{17,1},{25,9},{2,18},{10... | collective-permute-start | bytes 24584 | tf_op jit(solution)/shard_map/ppermute | solution.py:625
  25.8 3.7 %collective-permute-start.10 = (f32[4,512]{1,0:T(4,128)S(1)}, f32[4,512]{1,0:T(4,128)S(1)}, u32[]{:S(2)}, u32[]{:S(2)}) collective-permute-start(f32[4,512]{1,0:T(4,128)S(1)} %get-tuple-element.153.refs_0_), channel_id=1, source_target_pairs={{0,24},{8,0},{16,8},{24,16},{1,25},{9,1},{17,9},{25,17},{2,26},{10... | collective-permute-start | bytes 24584 | tf_op jit(solution)/shard_map/ppermute | solution.py:625

commit v8 on v7

--- a/solution.py
+++ b/solution.py
@@ -80,13 +80,20 @@
 
 
 def late_kernel(count, *refs):
-    sources, semaphores = refs[:count], refs[-1]
+    sources, here, semaphores = refs[:count], refs[count : 2 * count], refs[-1]
     targets = refs[2 * count + 1 : 3 * count + 1]
-
-    @pl.when(lax.axis_index("net") == 0)
+    refs[3 * count + 1][...] = refs[2 * count][...]
+    place = lax.axis_index("net")
+
+    @pl.when(place == 0)
     def _():
         for copy in fetch(sources, targets, semaphores):
             copy.wait()
+
+    @pl.when(place > 0)
+    def _():
+        for target, source in zip(targets, here):
+            target[...] = source[...]
 
 
 def tables(refs, theta_ref, halo_ref, from_ref, to_ref):
@@ -279,7 +286,8 @@
 
 
 def send_kernel(scale, number, *refs):
-    z_ref, edge_ref, turned_ref, p_ref, c_ref, gain_ref, flow_in_ref = refs[:7]
+    z_ref, edge_ref, turned_ref, p_ref, c_ref, gain_ref = refs[:6]
+    held = refs[6 : 6 + number]
     counts = refs[6 + number : -1 - number]
     outs = refs[-1 - number : -1]
     send_ref = refs[-1]
@@ -288,7 +296,9 @@
 
     @pl.when(has_far())
     def _():
-        send_ref[:conts, :] = times(flow_in_ref[...], table)
+        send_ref[:conts, :] = times(held[0][...], table)
+        for target, source in zip(outs, held):
+            target[...] = source[...]
 
     @pl.when(jnp.logical_not(has_far()))
     def _():
@@ -395,7 +405,7 @@
     base_out_ref[...] = base
 
 
-def call(kernel, outs, *args, scratch=(), spaces=None, aliases=None, flops=2 * 128 * 640 * 512):
+def call(kernel, outs, *args, scratch=(), spaces=None, flops=2 * 128 * 640 * 512):
     shapes = [jax.ShapeDtypeStruct(shape, dtype) for shape, dtype in outs]
     moved = sum(a.size * a.dtype.itemsize for a in args)
     spaces = spaces or [pltpu.VMEM] * len(args)
@@ -405,7 +415,6 @@
         in_specs=[pl.BlockSpec(memory_space=space) for space in spaces],
         out_specs=[pl.BlockSpec(memory_space=pltpu.VMEM)] * len(outs),
         scratch_shapes=list(scratch),
-        input_output_aliases=aliases or {},
         compiler_params=pltpu.CompilerParams(vmem_limit_bytes=32 * 1024 * 1024),
         cost_estimate=pl.CostEstimate(flops=flops, bytes_accessed=moved, transcendentals=0),
     )(*args)
@@ -496,7 +505,6 @@
         pick1,
         spaces=[pltpu.HBM] * count + [pltpu.VMEM] * (count + 1),
         scratch=[pltpu.SemaphoreType.DMA((count,))],
-        aliases={count + index: index for index in range(count + 1)},
     )
     got1 = trade_near(pick1)
     halo_row, angles = here[:2]
@@ -568,7 +576,6 @@
             kernel,
             [branch] * len(held) + [tall if first else half],
             *args,
-            aliases={6 + index: index for index in range(len(held))},
         )
 
     for index in range(1, ROUNDS):

time: 30.4 us -> 30.4 us (level)
  no operation moved by 1% of the time
where the time goes in v8:
time: 30.4 us; the launch traced here: 30.2 us
  starting transfers between devices  15.3 us (50%)
  Pallas kernels  7.88 us (26%)
  waiting for transfers between devices  6.29 us (21%)
  between operations  0.77 us (3%)
    ppermute x5, starting transfers between devices, trade_far(): return lax.ppermute(value, axes, swap2)  9.22 us
    pallas_call x18, Pallas kernels, call(): pl.pallas_call(kernel, out_shape=shapes, in_specs=[pl.BlockSpec(memory_sp...  7.88 us
    ppermute x5, waiting for transfers between devices, trade_far(): return lax.ppermute(value, axes, swap2)  4.95 us
    ppermute x3, starting transfers between devices, local(): lax.ppermute(sums, 'cont', [(i, (i + shift) % cont_size) for i in range(c...  4.44 us
    ppermute x5, starting transfers between devices, trade_near(): return lax.ppermute(value, axes, swap1)  1.59 us
    ppermute x3, waiting for transfers between devices, local(): lax.ppermute(sums, 'cont', [(i, (i + shift) % cont_size) for i in range(c...  1.33 us
  transfers between devices with their start and end apart: 13, of which 5 were waited for; matrix products, arithmetic and copies ran while one was open for 0% of the time, Pallas kernels for 23%

profile of v8, /device:TPU:0, one launch (start us, length us, event | category | flops | bytes accessed | tf_op | source)
XLA Modules:
  0.0 30.2 jit_solution(13143390694954779212)
XLA Ops:
  0.7 3.0 %collective-permute-start = (f32[64,128]{1,0:T(8,128)S(1)}, f32[64,128]{1,0:T(8,128)S(1)}, u32[]{:S(2)}, u32[]{:S(2)}) collective-permute-start(f32[64,128]{1,0:T(8,128)S(1)} %get-tuple-element.80), channel_id=1, source_target_pairs={{0,8},{1,2},{2,1},{3,4},{4,3},{5,6},{6,5},{7,15},{8,0},{9,10},{10,... | collective-permute-start | bytes 98312 | tf_op jit(solution)/shard_map/ppermute | solution.py:468
  3.7 1.0 %shard_map.149 = (s32[1,128]{1,0:T(1,128)S(1)}, f32[64,512]{1,0:T(8,128)S(1)}, s32[640]{0:T(1024)S(1)}, s32[640]{0:T(1024)S(1)}, f32[640]{0:T(1024)S(1)}, /*index=5*/f32[64,128]{1,0:T(8,128)S(1)}) custom-call(s32[1,128]{1,0:T(1,128)} %bitcast.11, f32[64,512]{1,0:T(8,128)} %refs_1_.4, s32[640]{0:T(1024)} %refs_2_.4, s32[640]{0:T(1024)} %refs_3_.3, ...), custom_call_target="tpu_custom_call" | custom-call | flops 83886080 | bytes 311296 | tf_op jit(solution)/shard_map/pallas_call | solution.py:412
  4.7 0.4 %collective-permute-start.1 = (f32[64,128]{1,0:T(8,128)S(1)}, f32[64,128]{1,0:T(8,128)S(1)}, u32[]{:S(2)}, u32[]{:S(2)}) collective-permute-start(f32[64,128]{1,0:T(8,128)S(1)} %get-tuple-element.87.pick1_ref), channel_id=1, source_target_pairs={{0,1},{1,0},{2,3},{3,2},{4,5},{5,4},{6,7},{7,6},{8,9},{9,8},{10,11... | collective-permute-start | bytes 98312 | tf_op jit(solution)/shard_map/ppermute | solution.py:465
  5.1 1.4 %shard_map.150 = (f32[64,512]{1,0:T(8,128)S(1)}, f32[64,640]{1,0:T(8,128)S(1)}, f32[64,640]{1,0:T(8,128)S(1)}, f32[8,512]{1,0:T(8,128)S(1)}, bf16[640,256]{1,0:T...) custom-call(f32[64,640]{1,0:T(8,128)} %refs_0_.1, ...), custom_call_target="tpu_custom_call" | custom-call | flops 83886080 | bytes 770048 | tf_op jit(solution)/shard_map/pallas_call | solution.py:412
  6.6 1.6 %collective-permute-start.2 = (f32[72,128]{1,0:T(8,128)S(1)}, f32[72,128]{1,0:T(8,128)S(1)}, u32[]{:S(2)}, u32[]{:S(2)}) collective-permute-start(f32[72,128]{1,0:T(8,128)S(1)} %get-tuple-element.99), channel_id=1, source_target_pairs={{0,8},{1,2},{2,1},{3,4},{4,3},{5,6},{6,5},{7,15},{8,0},{9,10},{10,... | collective-permute-start | bytes 110600 | tf_op jit(solution)/shard_map/ppermute | solution.py:468
  8.5 0.6 %collective-permute-start.3 = (f32[72,128]{1,0:T(8,128)S(1)}, f32[72,128]{1,0:T(8,128)S(1)}, u32[]{:S(2)}, u32[]{:S(2)}) collective-permute-start(f32[72,128]{1,0:T(8,128)S(1)} %get-tuple-element.103.send1_ref), channel_id=1, source_target_pairs={{0,1},{1,0},{2,3},{3,2},{4,5},{5,4},{6,7},{7,6},{8,9},{9,8},{10,11... | collective-permute-start | bytes 110600 | tf_op jit(solution)/shard_map/ppermute | solution.py:465
  9.1 0.5 %shard_map.153 = (f32[64,512]{1,0:T(8,128)S(1)}, f32[64,512]{1,0:T(8,128)S(1)}, f32[64,640]{1,0:T(8,128)S(1)}, f32[64,640]{1,0:T(8,128)S(1)}) custom-call(f32[64,640]{1,0:T(8,128)S(1)} %get-tuple-element.104.flow_ref, f32[64,640]{1,0:T(8,128)S(1)} %get-tuple-element.105.delta_ref, f32[64,512]{1,0:T(8,128)S(1)} %get-tuple-element.106.x_ref, ...), custom_call_target="tpu_custom_call" | custom-call | flops 83886080 | bytes 1130496 | tf_op jit(solution)/shard_map/pallas_call | solution.py:412
  9.6 1.0 %collective-permute-done.2 = f32[72,128]{1,0:T(8,128)S(1)} collective-permute-done((f32[72,128]{1,0:T(8,128)S(1)}, f32[72,128]{1,0:T(8,128)S(1)}, u32[]{:S(2)}, u32[]{:S(2)}) %collective-permute-start.2) | collective-permute-done | bytes 36896 | tf_op jit(solution)/shard_map/ppermute | solution.py:468
  10.6 1.6 %collective-permute-start.4 = (f32[64,128]{1,0:T(8,128)S(1)}, f32[64,128]{1,0:T(8,128)S(1)}, u32[]{:S(2)}, u32[]{:S(2)}) collective-permute-start(f32[64,128]{1,0:T(8,128)S(1)} %get-tuple-element.111), channel_id=1, source_target_pairs={{0,8},{1,2},{2,1},{3,4},{4,3},{5,6},{6,5},{7,15},{8,0},{9,10},{10,... | collective-permute-start | bytes 98312 | tf_op jit(solution)/shard_map/ppermute | solution.py:468
  12.9 0.5 %shard_map.156 = (f32[64,512]{1,0:T(8,128)S(1)}, f32[64,512]{1,0:T(8,128)S(1)}, f32[64,640]{1,0:T(8,128)S(1)}, f32[64,640]{1,0:T(8,128)S(1)}) custom-call(f32[64,640]{1,0:T(8,128)S(1)} %get-tuple-element.117.flow_ref, f32[64,640]{1,0:T(8,128)S(1)} %get-tuple-element.118.delta_ref, f32[64,512]{1,0:T(8,128)S(1)} %get-tuple-element.119.x_ref, ...), custom_call_target="tpu_custom_call" | custom-call | flops 83886080 | bytes 1130496 | tf_op jit(solution)/shard_map/pallas_call | solution.py:412
  13.5 1.1 %collective-permute-done.4 = f32[64,128]{1,0:T(8,128)S(1)} collective-permute-done((f32[64,128]{1,0:T(8,128)S(1)}, f32[64,128]{1,0:T(8,128)S(1)}, u32[]{:S(2)}, u32[]{:S(2)}) %collective-permute-start.4) | collective-permute-done | bytes 32800 | tf_op jit(solution)/shard_map/ppermute | solution.py:468
  14.7 1.6 %collective-permute-start.6 = (f32[64,128]{1,0:T(8,128)S(1)}, f32[64,128]{1,0:T(8,128)S(1)}, u32[]{:S(2)}, u32[]{:S(2)}) collective-permute-start(f32[64,128]{1,0:T(8,128)S(1)} %get-tuple-element.122), channel_id=1, source_target_pairs={{0,8},{1,2},{2,1},{3,4},{4,3},{5,6},{6,5},{7,15},{8,0},{9,10},{10,... | collective-permute-start | bytes 98312 | tf_op jit(solution)/shard_map/ppermute | solution.py:468
  16.2 0.4 %shard_map.158 = (f32[64,640]{1,0:T(8,128)S(1)}, f32[64,640]{1,0:T(8,128)S(1)}, f32[64,128]{1,0:T(8,128)S(1)}) custom-call(f32[64,256]{1,0:T(8,128)S(1)} %get-tuple-element.123.refs_0_.z_ref, bf16[640,256]{1,0:T(8,128)(2,1)S(1)} %get-tuple-element.93.edge_ref.refs_1_, bf16[256,640]{1,0:T(8,128)(2,1)S(1)} %get-tuple-element.94.turned_ref.refs_2_, ...), custom_call_target="tpu_custom_call" | custom-call | flops 83886080 | bytes 1540096 | tf_op jit(solution)/shard_map/pallas_call | solution.py:412
  16.7 0.5 %shard_map.159 = (f32[64,512]{1,0:T(8,128)S(1)}, f32[64,512]{1,0:T(8,128)S(1)}, f32[64,640]{1,0:T(8,128)S(1)}, f32[64,640]{1,0:T(8,128)S(1)}) custom-call(f32[64,640]{1,0:T(8,128)S(1)} %get-tuple-element.127.flow_ref, f32[64,640]{1,0:T(8,128)S(1)} %get-tuple-element.128.delta_ref, f32[64,512]{1,0:T(8,128)S(1)} %get-tuple-element.129.x_ref, ...), custom_call_target="tpu_custom_call" | custom-call | flops 83886080 | bytes 1130496 | tf_op jit(solution)/shard_map/pallas_call | solution.py:412
  17.3 1.4 %collective-permute-done.6 = f32[64,128]{1,0:T(8,128)S(1)} collective-permute-done((f32[64,128]{1,0:T(8,128)S(1)}, f32[64,128]{1,0:T(8,128)S(1)}, u32[]{:S(2)}, u32[]{:S(2)}) %collective-permute-start.6) | collective-permute-done | bytes 32800 | tf_op jit(solution)/shard_map/ppermute | solution.py:468
  18.7 1.6 %collective-permute-start.8 = (f32[64,128]{1,0:T(8,128)S(1)}, f32[64,128]{1,0:T(8,128)S(1)}, u32[]{:S(2)}, u32[]{:S(2)}) collective-permute-start(f32[64,128]{1,0:T(8,128)S(1)} %get-tuple-element.132), channel_id=1, source_target_pairs={{0,8},{1,2},{2,1},{3,4},{4,3},{5,6},{6,5},{7,15},{8,0},{9,10},{10,... | collective-permute-start | bytes 98312 | tf_op jit(solution)/shard_map/ppermute | solution.py:468
  20.7 0.5 %shard_map.162 = (f32[64,512]{1,0:T(8,128)S(1)}, f32[64,512]{1,0:T(8,128)S(1)}, f32[64,512]{1,0:T(8,128)S(1)}, f32[4,512]{1,0:T(4,128)S(1)}) custom-call(f32[64,640]{1,0:T(8,128)S(1)} %get-tuple-element.138.flow_ref, f32[64,512]{1,0:T(8,128)S(1)} %get-tuple-element.139.x_ref, f32[8,512]{1,0:T(8,128)S(1)} %get-tuple-element.107.count_ref, ...), custom_call_target="tpu_custom_call" | custom-call | flops 83886080 | bytes 1966080 | tf_op jit(solution)/shard_map/pallas_call | solution.py:412
  21.2 1.5 %collective-permute-done.8 = f32[64,128]{1,0:T(8,128)S(1)} collective-permute-done((f32[64,128]{1,0:T(8,128)S(1)}, f32[64,128]{1,0:T(8,128)S(1)}, u32[]{:S(2)}, u32[]{:S(2)}) %collective-permute-start.8) | collective-permute-done | bytes 32800 | tf_op jit(solution)/shard_map/ppermute | solution.py:468
  22.8 1.5 %collective-permute-start.12 = (f32[4,512]{1,0:T(4,128)S(1)}, f32[4,512]{1,0:T(4,128)S(1)}, u32[]{:S(2)}, u32[]{:S(2)}) collective-permute-start(f32[4,512]{1,0:T(4,128)S(1)} %get-tuple-element.153.refs_0_), channel_id=1, source_target_pairs={{0,8},{8,16},{16,24},{24,0},{1,9},{9,17},{17,25},{25,1},{2,10},{10... | collective-permute-start | bytes 24584 | tf_op jit(solution)/shard_map/ppermute | solution.py:632
  24.3 1.5 %collective-permute-start.11 = (f32[4,512]{1,0:T(4,128)S(1)}, f32[4,512]{1,0:T(4,128)S(1)}, u32[]{:S(2)}, u32[]{:S(2)}) collective-permute-start(f32[4,512]{1,0:T(4,128)S(1)} %get-tuple-element.153.refs_0_), channel_id=1, source_target_pairs={{0,16},{8,24},{16,0},{24,8},{1,17},{9,25},{17,1},{25,9},{2,18},{10... | collective-permute-start | bytes 24584 | tf_op jit(solution)/shard_map/ppermute | solution.py:632
  25.9 1.4 %collective-permute-start.10 = (f32[4,512]{1,0:T(4,128)S(1)}, f32[4,512]{1,0:T(4,128)S(1)}, u32[]{:S(2)}, u32[]{:S(2)}) collective-permute-start(f32[4,512]{1,0:T(4,128)S(1)} %get-tuple-element.153.refs_0_), channel_id=1, source_target_pairs={{0,24},{8,0},{16,8},{24,16},{1,25},{9,1},{17,9},{25,17},{2,26},{10... | collective-permute-start | bytes 24584 | tf_op jit(solution)/shard_map/ppermute | solution.py:632
  27.3 0.9 %shard_map.164 = (f32[64,512]{1,0:T(8,128)}, f32[64,512]{1,0:T(8,128)S(1)}) custom-call(f32[64,256]{1,0:T(8,128)S(1)} %get-tuple-element.148.both_ref, f32[64,256]{1,0:T(8,128)S(1)} %get-tuple-element.133.refs_0_.z_ref, f32[8,256]{1,0:T(8,128)S(1)} %get-tuple-element.116.degree_ref, bf16[256,512]{1,0:T(8,128)(2,1)S(1)} %get-tuple-element.136.own_ref, ...), custom_call_target="tpu_custom_call" | custom-call | flops 83886080 | bytes 811008 | tf_op jit(solution)/shard_map/pallas_call | solution.py:412
  28.2 1.3 %collective-permute-done.10.refs_1_ = f32[4,512]{1,0:T(4,128)S(1)} collective-permute-done((f32[4,512]{1,0:T(4,128)S(1)}, f32[4,512]{1,0:T(4,128)S(1)}, u32[]{:S(2)}, u32[]{:S(2)}) %collective-permute-start.10) | collective-permute-done | bytes 8224 | tf_op jit(solution)/shard_map/ppermute | solution.py:632
  29.5 0.7 %shard_map.165 = (f32[64,512]{1,0:T(8,128)}, f32[1,512]{1,0:T(1,128)}) custom-call(f32[4,512]{1,0:T(4,128)S(1)} %get-tuple-element.153.refs_0_, f32[4,512]{1,0:T(4,128)S(1)} %collective-permute-done.10.refs_1_, f32[4,512]{1,0:T(4,128)S(1)} %collective-permute-done.11.refs_2_, f32[4,512]{1,0:T(4,128)S(1)} %collective-permute-done.12.refs_3_, ...), custom_call_target="tpu_custom_call" | custom-call | flops 83886080 | bytes 180224 | tf_op jit(solution)/shard_map/pallas_call | solution.py:412
  (28 shorter events, 2.1 us)
Async XLA Ops:
  0.7 5.8 %collective-permute-start = (f32[64,128]{1,0:T(8,128)S(1)}, f32[64,128]{1,0:T(8,128)S(1)}, u32[]{:S(2)}, u32[]{:S(2)}) collective-permute-start(f32[64,128]{1,0:T(8,128)S(1)} %get-tuple-element.80), channel_id=1, source_target_pairs={{0,8},{1,2},{2,1},{3,4},{4,3},{5,6},{6,5},{7,15},{8,0},{9,10},{10,... | collective-permute-start | bytes 98312 | tf_op jit(solution)/shard_map/ppermute | solution.py:468
  4.7 1.8 %collective-permute-start.1 = (f32[64,128]{1,0:T(8,128)S(1)}, f32[64,128]{1,0:T(8,128)S(1)}, u32[]{:S(2)}, u32[]{:S(2)}) collective-permute-start(f32[64,128]{1,0:T(8,128)S(1)} %get-tuple-element.87.pick1_ref), channel_id=1, source_target_pairs={{0,1},{1,0},{2,3},{3,2},{4,5},{5,4},{6,7},{7,6},{8,9},{9,8},{10,11... | collective-permute-start | bytes 98312 | tf_op jit(solution)/shard_map/ppermute | solution.py:465
  6.6 4.0 %collective-permute-start.2 = (f32[72,128]{1,0:T(8,128)S(1)}, f32[72,128]{1,0:T(8,128)S(1)}, u32[]{:S(2)}, u32[]{:S(2)}) collective-permute-start(f32[72,128]{1,0:T(8,128)S(1)} %get-tuple-element.99), channel_id=1, source_target_pairs={{0,8},{1,2},{2,1},{3,4},{4,3},{5,6},{6,5},{7,15},{8,0},{9,10},{10,... | collective-permute-start | bytes 110600 | tf_op jit(solution)/shard_map/ppermute | solution.py:468
  8.5 2.1 %collective-permute-start.3 = (f32[72,128]{1,0:T(8,128)S(1)}, f32[72,128]{1,0:T(8,128)S(1)}, u32[]{:S(2)}, u32[]{:S(2)}) collective-permute-start(f32[72,128]{1,0:T(8,128)S(1)} %get-tuple-element.103.send1_ref), channel_id=1, source_target_pairs={{0,1},{1,0},{2,3},{3,2},{4,5},{5,4},{6,7},{7,6},{8,9},{9,8},{10,11... | collective-permute-start | bytes 110600 | tf_op jit(solution)/shard_map/ppermute | solution.py:465
  10.6 4.0 %collective-permute-start.4 = (f32[64,128]{1,0:T(8,128)S(1)}, f32[64,128]{1,0:T(8,128)S(1)}, u32[]{:S(2)}, u32[]{:S(2)}) collective-permute-start(f32[64,128]{1,0:T(8,128)S(1)} %get-tuple-element.111), channel_id=1, source_target_pairs={{0,8},{1,2},{2,1},{3,4},{4,3},{5,6},{6,5},{7,15},{8,0},{9,10},{10,... | collective-permute-start | bytes 98312 | tf_op jit(solution)/shard_map/ppermute | solution.py:468
  12.6 2.1 %collective-permute-start.5 = (f32[64,128]{1,0:T(8,128)S(1)}, f32[64,128]{1,0:T(8,128)S(1)}, u32[]{:S(2)}, u32[]{:S(2)}) collective-permute-start(f32[64,128]{1,0:T(8,128)S(1)} %get-tuple-element.115.send1_ref), channel_id=1, source_target_pairs={{0,1},{1,0},{2,3},{3,2},{4,5},{5,4},{6,7},{7,6},{8,9},{9,8},{10,11... | collective-permute-start | bytes 98312 | tf_op jit(solution)/shard_map/ppermute | solution.py:465
  14.7 4.0 %collective-permute-start.6 = (f32[64,128]{1,0:T(8,128)S(1)}, f32[64,128]{1,0:T(8,128)S(1)}, u32[]{:S(2)}, u32[]{:S(2)}) collective-permute-start(f32[64,128]{1,0:T(8,128)S(1)} %get-tuple-element.122), channel_id=1, source_target_pairs={{0,8},{1,2},{2,1},{3,4},{4,3},{5,6},{6,5},{7,15},{8,0},{9,10},{10,... | collective-permute-start | bytes 98312 | tf_op jit(solution)/shard_map/ppermute | solution.py:468
  16.6 2.1 %collective-permute-start.7 = (f32[64,128]{1,0:T(8,128)S(1)}, f32[64,128]{1,0:T(8,128)S(1)}, u32[]{:S(2)}, u32[]{:S(2)}) collective-permute-start(f32[64,128]{1,0:T(8,128)S(1)} %get-tuple-element.126.send1_ref), channel_id=1, source_target_pairs={{0,1},{1,0},{2,3},{3,2},{4,5},{5,4},{6,7},{7,6},{8,9},{9,8},{10,11... | collective-permute-start | bytes 98312 | tf_op jit(solution)/shard_map/ppermute | solution.py:465
  18.7 4.0 %collective-permute-start.8 = (f32[64,128]{1,0:T(8,128)S(1)}, f32[64,128]{1,0:T(8,128)S(1)}, u32[]{:S(2)}, u32[]{:S(2)}) collective-permute-start(f32[64,128]{1,0:T(8,128)S(1)} %get-tuple-element.132), channel_id=1, source_target_pairs={{0,8},{1,2},{2,1},{3,4},{4,3},{5,6},{6,5},{7,15},{8,0},{9,10},{10,... | collective-permute-start | bytes 98312 | tf_op jit(solution)/shard_map/ppermute | solution.py:468
  20.6 2.1 %collective-permute-start.9 = (f32[64,128]{1,0:T(8,128)S(1)}, f32[64,128]{1,0:T(8,128)S(1)}, u32[]{:S(2)}, u32[]{:S(2)}) collective-permute-start(f32[64,128]{1,0:T(8,128)S(1)} %get-tuple-element.135.send1_ref), channel_id=1, source_target_pairs={{0,1},{1,0},{2,3},{3,2},{4,5},{5,4},{6,7},{7,6},{8,9},{9,8},{10,11... | collective-permute-start | bytes 98312 | tf_op jit(solution)/shard_map/ppermute | solution.py:465
  22.8 5.3 %collective-permute-start.12 = (f32[4,512]{1,0:T(4,128)S(1)}, f32[4,512]{1,0:T(4,128)S(1)}, u32[]{:S(2)}, u32[]{:S(2)}) collective-permute-start(f32[4,512]{1,0:T(4,128)S(1)} %get-tuple-element.153.refs_0_), channel_id=1, source_target_pairs={{0,8},{8,16},{16,24},{24,0},{1,9},{9,17},{17,25},{25,1},{2,10},{10... | collective-permute-start | bytes 24584 | tf_op jit(solution)/shard_map/ppermute | solution.py:632
  24.3 3.9 %collective-permute-start.11 = (f32[4,512]{1,0:T(4,128)S(1)}, f32[4,512]{1,0:T(4,128)S(1)}, u32[]{:S(2)}, u32[]{:S(2)}) collective-permute-start(f32[4,512]{1,0:T(4,128)S(1)} %get-tuple-element.153.refs_0_), channel_id=1, source_target_pairs={{0,16},{8,24},{16,0},{24,8},{1,17},{9,25},{17,1},{25,9},{2,18},{10... | collective-permute-start | bytes 24584 | tf_op jit(solution)/shard_map/ppermute | solution.py:632
  25.9 3.7 %collective-permute-start.10 = (f32[4,512]{1,0:T(4,128)S(1)}, f32[4,512]{1,0:T(4,128)S(1)}, u32[]{:S(2)}, u32[]{:S(2)}) collective-permute-start(f32[4,512]{1,0:T(4,128)S(1)} %get-tuple-element.153.refs_0_), channel_id=1, source_target_pairs={{0,24},{8,0},{16,8},{24,16},{1,25},{9,1},{17,9},{25,17},{2,26},{10... | collective-permute-start | bytes 24584 | tf_op jit(solution)/shard_map/ppermute | solution.py:632
